TPU v7x, 256 devices: a whole 4x4x8 slice. The times are simulated.
256 devices in a mesh: leaf: 64 (over z, x, core), vec: 4 (over y).
Axes of the slice: x: 4, y: 4, z: 8, core: 2. Of those that a mesh axis runs over, the one named last changes fastest.
Arguments:
- vectors: bfloat16 [64, 524288], P('vec', 'leaf'), may hold values from -6 to 6
- points: float32 [3, 524288], P(None, ('leaf', 'vec')), may hold values from 0 to 1
- leaf_basis: bfloat16 [4096, 64, 128], P('leaf'), may hold values from -0.5 to 0.5
- local_transfer: bfloat16 [8192, 64, 64], P('leaf'), may hold values from -0.625 to 0.625
- local_coupling: bfloat16 [8192, 64, 64], P('leaf'), may hold values from -0.75 to 0.75
- upper_transfer: bfloat16 [64, 64, 64], replicated, may hold values from -0.625 to 0.625
- upper_coupling: bfloat16 [64, 64, 64], replicated, may hold values from -0.75 to 0.75
- far_anchor: int32 [16384, 1], P('leaf'), may hold values from 0 to 63; in each aligned block of 256 rows (0 to 255, 256 to 511, ...) at most 8 rows name the same one
- far_leaves: int32 [16384, 2], P('leaf'), may hold values from 0 to 63
- far_block: bfloat16 [16384, 64, 64], P('leaf'), may hold values from -0.5 to 0.5
- near_cols: int32 [4096, 8], P('leaf'), may hold values from 0 to 4095, as said below
Outputs:
- product: float32 [64, 524288], P('vec', 'leaf')
Inputs may be any that keep to these rules, and one draw needn't show every extreme that they name: near_cols[t, 0] = t, and every entry lies within 8 leaves of t. `far_anchor`: among the 256 rows of one index of leaf, no value is named more than 8 times, and in every draw some value is named exactly 8 times.
All inputs are finite; a program needn't handle non-finite values.
Results may differ from a plain program's by a relative error of at most 0.0075.
Values may be sent and summed in bfloat16 or wider, within the bound.
No kernel may reach another device: no remote copies, remote signals or barrier semaphores. Data moves between devices by JAX's collectives and lax.ppermute only.
A program may use at most 128 MiB of HBM per device.

v0:
```python
import jax
import jax.numpy as jnp
from jax import lax
from jax.sharding import PartitionSpec as P

REACH = 8


kernel_scale = 1.0 / 64.0
delta_sq = 0.0025


def swapped(block, axis, distance):
    count = lax.axis_size(axis)
    route = []
    for low in range(count):
        high = low | 1 << distance
        if high != low and high < count:
            route += [(low, high), (high, low)]
    return lax.ppermute(block, axis, route)


def with_halo(cells, sides, width):
    for axis, dim in sides:
        count = lax.axis_size(axis)
        ends = count - 1
        head = lax.slice_in_dim(cells, 0, width, axis=dim)
        tail = lax.slice_in_dim(cells, cells.shape[dim] - width, cells.shape[dim], axis=dim)
        cells = jnp.concatenate(
            [
                lax.ppermute(tail, axis, [(i, (i + 1) % count) for i in range(ends)]),
                cells,
                lax.ppermute(head, axis, [((i + 1) % count, i) for i in range(ends)]),
            ],
            axis=dim,
        )
    return cells


def pick_node(table, node):
    return lax.dynamic_index_in_dim(table, node, 0, keepdims=False)


def per_device(
    vectors,
    points,
    leaf_basis,
    local_transfer,
    local_coupling,
    upper_transfer,
    upper_coupling,
    far_anchor,
    far_leaves,
    far_block,
    near_cols,
):
    highest = lax.Precision.HIGHEST
    vec_cols, point_count = vectors.shape
    leaf_dev, basis_rank, leaf_size = leaf_basis.shape
    n_leaf = lax.axis_size("leaf")
    top_depth = n_leaf.bit_length() - 1
    local_depth = leaf_dev.bit_length() - 1
    device = lax.axis_index("leaf")
    coords = lax.all_gather(points, "vec", axis=1, tiled=True)
    x_leaf = vectors.reshape(vec_cols, leaf_dev, leaf_size)
    coeff = jnp.einsum("vtp,tkp->tvk", x_leaf, leaf_basis, preferred_element_type=jnp.float32)
    transfer = local_transfer.astype(jnp.float32)
    coupling = local_coupling.astype(jnp.float32)
    upper_t = upper_transfer.astype(jnp.float32)
    upper_c = upper_coupling.astype(jnp.float32)
    levels = {local_depth: coeff}
    current = coeff
    for sub_depth in range(local_depth, 0, -1):
        node_count = 2**sub_depth
        product = jnp.einsum(
            "nvk,nkl->nvl", current, transfer[node_count : 2 * node_count], precision=highest
        )
        current = product.reshape(node_count // 2, 2, vec_cols, basis_rank).sum(1)
        levels[sub_depth - 1] = current
    root_coeff = current[0]
    root_share = jnp.dot(root_coeff, transfer[1], precision=highest)
    siblings = []
    carried = jnp.stack([root_coeff, root_share])
    for bit_pos in range(top_depth):
        partner = swapped(carried, "leaf", bit_pos)
        siblings.append(partner[0])
        if bit_pos + 1 < top_depth:
            node = jnp.right_shift(n_leaf + device, bit_pos + 1)
            parent = carried[1] + partner[1]
            carried = jnp.stack(
                [parent, jnp.dot(parent, pick_node(upper_t, node), precision=highest)]
            )
    downward = None
    for tree_depth in range(1, top_depth + 1):
        bit_pos = top_depth - tree_depth
        if bit_pos == 0:
            move_mat = transfer[1]
            pair_mat = coupling[1]
        else:
            node = jnp.right_shift(n_leaf + device, bit_pos)
            move_mat = pick_node(upper_t, node)
            pair_mat = pick_node(upper_c, node)
        coupled = jnp.dot(siblings[bit_pos], pair_mat, precision=highest)
        if downward is None:
            downward = coupled
        else:
            downward = jnp.dot(downward, move_mat.T, precision=highest) + coupled
    downward = downward[None]
    for sub_depth in range(1, local_depth + 1):
        node_count = 2**sub_depth
        coeffs = levels[sub_depth]
        sibling = coeffs.reshape(node_count // 2, 2, vec_cols, basis_rank)[:, ::-1].reshape(
            node_count, vec_cols, basis_rank
        )
        parent = jnp.repeat(downward, 2, axis=0)
        moved = jnp.einsum(
            "nvl,nkl->nvk", parent, transfer[node_count : 2 * node_count], precision=highest
        )
        downward = moved + jnp.einsum(
            "nvk,nkl->nvl", sibling, coupling[node_count : 2 * node_count], precision=highest
        )
    sent = coeff.astype(jnp.bfloat16)
    anchor = far_anchor[:, 0]
    source_local = far_leaves[:, 0]
    target_local = far_leaves[:, 1]
    everything = lax.all_gather(sent, "leaf", axis=0, tiled=True)
    fetched = jnp.take(everything, anchor * leaf_dev + source_local, axis=0)
    contrib = jnp.einsum("pvk,pkl->pvl", fetched, far_block, preferred_element_type=jnp.float32)
    onehot = (target_local[:, None] == jnp.arange(leaf_dev, dtype=jnp.int32)[None, :]).astype(
        jnp.float32
    )
    far_sum = jnp.einsum("pt,pvl->tvl", onehot, contrib, precision=highest)
    leaf_local = (downward + far_sum).astype(jnp.bfloat16)
    far_part = jnp.einsum(
        "tvk,tkp->vtp", leaf_local, leaf_basis, preferred_element_type=jnp.float32
    )
    padded_pts = with_halo(coords.astype(jnp.bfloat16), (("leaf", 1),), REACH * leaf_size).astype(
        coords.dtype
    )
    padded_vec = with_halo(vectors, (("leaf", 1),), REACH * leaf_size)
    block_count = leaf_dev + 2 * REACH
    pts_rows = jnp.transpose(padded_pts.reshape(3, block_count, leaf_size), (1, 0, 2))
    vec_rows = jnp.transpose(padded_vec.reshape(vec_cols, block_count, leaf_size), (1, 0, 2))
    own_rows = jnp.transpose(coords.reshape(3, leaf_dev, leaf_size), (1, 0, 2))
    local_cols = near_cols - device * leaf_dev + REACH
    group_size = min(8, leaf_dev)
    groups = leaf_dev // group_size

    def near_group(group, totals):
        first = group * group_size
        col_ids = lax.dynamic_slice_in_dim(local_cols, first, group_size, 0)
        targets = lax.dynamic_slice_in_dim(own_rows, first, group_size, 0)
        source = jnp.take(pts_rows, col_ids, axis=0)
        delta_x = targets[:, None, 0, :, None] - source[:, :, 0, None, :]
        delta_y = targets[:, None, 1, :, None] - source[:, :, 1, None, :]
        delta_z = targets[:, None, 2, :, None] - source[:, :, 2, None, :]
        dist_sq = delta_x * delta_x + delta_y * delta_y + delta_z * delta_z
        kernel = (kernel_scale * lax.rsqrt(dist_sq + delta_sq)).astype(jnp.bfloat16)
        values = jnp.take(vec_rows, col_ids, axis=0)
        block_sum = jnp.einsum("gkpq,gkvq->vgp", kernel, values, preferred_element_type=jnp.float32)
        return lax.dynamic_update_slice_in_dim(totals, block_sum, first, 1)

    near_sum = lax.fori_loop(
        0, groups, near_group, jnp.zeros((vec_cols, leaf_dev, leaf_size), jnp.float32)
    )
    return (near_sum + far_part).reshape(vec_cols, point_count)


def solution(mesh):
    return jax.shard_map(
        per_device,
        mesh=mesh,
        in_specs=(
            P("vec", "leaf"),
            P(None, ("leaf", "vec")),
            P("leaf", None, None),
            P("leaf", None, None),
            P("leaf", None, None),
            P(),
            P(),
            P("leaf", None),
            P("leaf", None),
            P("leaf", None, None),
            P("leaf", None),
        ),
        out_specs=P("vec", "leaf"),
        check_vma=False,
    )
```

profile of v0, /device:TPU:4, one launch (start us, length us, event | category | flops | bytes accessed | tf_op | source)
XLA Modules:
  0.0 243.2 jit_solution(12452155980335670206)
XLA Ops:
  6.5 2.8 %slice.146 = bf16[64,64,64]{0,2,1:T(8,128)(2,1)} slice(bf16[128,64,64]{0,2,1:T(8,128)(2,1)} %param.16), slice={[64:128], [0:64], [0:64]} | slice | bytes 1048576 | tf_op jit(solution)/shard_map/slice | solution.py:76
  9.3 2.6 %slice.147 = bf16[32,64,64]{0,2,1:T(8,128)(2,1)} slice(bf16[128,64,64]{0,2,1:T(8,128)(2,1)} %param.16), slice={[32:64], [0:64], [0:64]} | slice | bytes 524288 | tf_op jit(solution)/shard_map/slice | solution.py:76
  12.3 1.4 slice.149
  13.7 1.4 slice.150
  15.1 1.4 slice.151
  17.9 2.6 %copy.89 = bf16[64,64,64]{2,1,0:T(8,128)(2,1)S(1)} copy(bf16[64,64,64]{0,2,1:T(8,128)(2,1)} %slice.146) | data formatting | bytes 1048576
  20.5 2.8 %copy.90 = bf16[32,64,64]{2,1,0:T(8,128)(2,1)} copy(bf16[32,64,64]{0,2,1:T(8,128)(2,1)} %slice.147) | data formatting | bytes 524288
  24.6 2.3 copy.92
  26.8 2.4 copy.93
  29.2 2.3 copy.94
  31.5 1.8 copy.95
  40.1 12.7 %all_gather.6 = f32[3,8192]{1,0:T(4,128)S(1)} all-gather(f32[3,2048]{1,0:T(4,128)} %param.14), channel_id=1, replica_groups=mesh['leaf'=64,'vec'=4] {'vec'}, dimensions={1}, use_global_device_ids=true | all-gather | bytes 122880 | tf_op jit(solution)/shard_map/all_gather | solution.py:64
  54.7 1.9 collective-permute-start.2
  56.6 3.6 %collective-permute-start.3 = (bf16[3,1024]{1,0:T(4,128)(2,1)}, bf16[3,1024]{1,0:T(4,128)(2,1)}, u32[]{:S(2)}, u32[]{:S(2)}) collective-permute-start(bf16[3,1024]{1,0:T(4,128)(2,1)} %get-tuple-element.156), channel_id=1, source_target_pairs={{4,0},{8,4},{12,8},{16,12},{20,16},{24,20},{28,24},{32,28},{36,32}... | collective-permute-start | bytes 18440 | tf_op jit(solution)/shard_map/ppermute | solution.py:33
  60.3 1.4 fusion.101
  61.7 1.9 collective-permute-start
  63.6 3.6 %collective-permute-start.1 = (bf16[16,1024]{1,0:T(8,128)(2,1)}, bf16[16,1024]{1,0:T(8,128)(2,1)}, u32[]{:S(2)}, u32[]{:S(2)}) collective-permute-start(bf16[16,1024]{1,0:T(8,128)(2,1)} %get-tuple-element.154), channel_id=1, source_target_pairs={{4,0},{8,4},{12,8},{16,12},{20,16},{24,20},{28,24},{32,28},{36,32}... | collective-permute-start | bytes 98312 | tf_op jit(solution)/shard_map/ppermute | solution.py:33
  72.6 1.8 and_reduce_fusion
  82.1 1.4 slice.165
  83.5 1.4 slice.166
  84.9 1.4 slice.167
  87.7 1.4 slice.169
  89.1 1.4 slice.170
  90.5 2.4 copy.96
  92.8 2.3 copy.97
  96.5 2.4 copy.98
  98.9 1.5 rev.17
  100.3 2.3 copy.99
  105.3 2.8 %copy.101 = bf16[32,64,64]{2,1,0:T(8,128)(2,1)} copy(bf16[32,64,64]{0,2,1:T(8,128)(2,1)} %slice.169) | data formatting | bytes 524288
  108.1 7.5 %copy.83 = bf16[256,64,64]{2,1,0:T(8,128)(2,1)} copy(bf16[256,64,64]{0,2,1:T(8,128)(2,1)} %param.22) | data formatting | bytes 4194304 | tf_op args[9]
  116.4 3.3 %copy.102 = bf16[64,64,64]{2,1,0:T(8,128)(2,1)} copy(bf16[64,64,64]{0,2,1:T(8,128)(2,1)} %slice.170) | data formatting | bytes 1048576
  122.0 6.8 %collective-permute-start.7 = (f32[2,16,64]{2,1,0:T(8,128)S(1)}, f32[2,16,64]{2,1,0:T(8,128)S(1)}, u32[]{:S(2)}, u32[]{:S(2)}) collective-permute-start(f32[2,16,64]{2,1,0:T(8,128)S(1)} %pad_maximum_fusion.3), channel_id=1, source_target_pairs={{0,32},{32,0},{4,36},{36,4},{8,40},{40,8},{12,44},{44,12},{16,48},... | collective-permute-start | bytes 24584 | tf_op jit(solution)/shard_map/ppermute | solution.py:20
  131.7 3.6 %collective-permute-start.8 = (f32[2,16,64]{2,1,0:T(8,128)S(1)}, f32[2,16,64]{2,1,0:T(8,128)S(1)}, u32[]{:S(2)}, u32[]{:S(2)}) collective-permute-start(f32[2,16,64]{2,1,0:T(8,128)S(1)} %pad_maximum_fusion.4), channel_id=1, source_target_pairs={{0,64},{64,0},{4,68},{68,4},{8,72},{72,8},{12,76},{76,12},{16,80},... | collective-permute-start | bytes 24584 | tf_op jit(solution)/shard_map/ppermute | solution.py:20
  138.8 9.0 %collective-permute-start.9 = (f32[2,16,64]{2,1,0:T(8,128)}, f32[2,16,64]{2,1,0:T(8,128)}, u32[]{:S(2)}, u32[]{:S(2)}) collective-permute-start(f32[2,16,64]{2,1,0:T(8,128)} %pad_maximum_fusion.5), channel_id=1, source_target_pairs={{0,128},{128,0},{4,132},{132,4},{8,136},{136,8},{12,140},{140,12},... | collective-permute-start | bytes 24584 | tf_op jit(solution)/shard_map/ppermute | solution.py:20
  148.6 51.6 %while.13 = (s32[]{:T(128)}, f32[16,64,128]{2,0,1:T(8,128)}, s32[64,8]{0,1:T(8,128)S(1)}, bf16[80,16,128]{2,1,0:T(8,128)(2,1)S(1)}, f32[64,3,128]{2,0,1:T(8,128)...) while((s32[]{:T(128)}, f32[16,64,128]{2,0,1:T(8,128)}, ...), condition=%wide.region_1.0_spmd, body=%wide.region_0.0_spmd.sunk | while | flops 45246024 | bytes 1584527 | solution.py:163
  151.7 3.4 %fusion.160 = f32[16,64,128]{2,0,1:T(8,128)} fusion(f32[16,64,128]{2,0,1:T(8,128)} %get-tuple-element.221, s32[]{:T(128)S(6)} %select_n.98, f32[8,8,128]{2,1,0:T(8,128)} %bitcast.277, f32[8,128]{1,0:T(8,128)S(1)} %get-tuple-element.203, f32[8,8,128]{2,1,0:T(8,128)} %bitcast.278, f32[8,128]{1,0:T(8,128)S(1)} %get-tuple-element.205, ...), kind=kOutput, calls=%fused_computation.6.clone.1 | convolution fusion | flops 45219840 | bytes 438340 | tf_op jit(solution)/shard_map/while/body/eval_jaxpr/gkpq,gkvq->vgp/dot_general | solution.py:160
  158.1 3.4 %fusion.160 = f32[16,64,128]{2,0,1:T(8,128)} fusion(f32[16,64,128]{2,0,1:T(8,128)} %get-tuple-element.221, s32[]{:T(128)S(6)} %select_n.98, f32[8,8,128]{2,1,0:T(8,128)} %bitcast.277, f32[8,128]{1,0:T(8,128)S(1)} %get-tuple-element.203, f32[8,8,128]{2,1,0:T(8,128)} %bitcast.278, f32[8,128]{1,0:T(8,128)S(1)} %get-tuple-element.205, ...), kind=kOutput, calls=%fused_computation.6.clone.1 | convolution fusion | flops 45219840 | bytes 438340 | tf_op jit(solution)/shard_map/while/body/eval_jaxpr/gkpq,gkvq->vgp/dot_general | solution.py:160
  164.6 3.4 %fusion.160 = f32[16,64,128]{2,0,1:T(8,128)} fusion(f32[16,64,128]{2,0,1:T(8,128)} %get-tuple-element.221, s32[]{:T(128)S(6)} %select_n.98, f32[8,8,128]{2,1,0:T(8,128)} %bitcast.277, f32[8,128]{1,0:T(8,128)S(1)} %get-tuple-element.203, f32[8,8,128]{2,1,0:T(8,128)} %bitcast.278, f32[8,128]{1,0:T(8,128)S(1)} %get-tuple-element.205, ...), kind=kOutput, calls=%fused_computation.6.clone.1 | convolution fusion | flops 45219840 | bytes 438340 | tf_op jit(solution)/shard_map/while/body/eval_jaxpr/gkpq,gkvq->vgp/dot_general | solution.py:160
  171.0 3.4 %fusion.160 = f32[16,64,128]{2,0,1:T(8,128)} fusion(f32[16,64,128]{2,0,1:T(8,128)} %get-tuple-element.221, s32[]{:T(128)S(6)} %select_n.98, f32[8,8,128]{2,1,0:T(8,128)} %bitcast.277, f32[8,128]{1,0:T(8,128)S(1)} %get-tuple-element.203, f32[8,8,128]{2,1,0:T(8,128)} %bitcast.278, f32[8,128]{1,0:T(8,128)S(1)} %get-tuple-element.205, ...), kind=kOutput, calls=%fused_computation.6.clone.1 | convolution fusion | flops 45219840 | bytes 438340 | tf_op jit(solution)/shard_map/while/body/eval_jaxpr/gkpq,gkvq->vgp/dot_general | solution.py:160
  177.5 3.4 %fusion.160 = f32[16,64,128]{2,0,1:T(8,128)} fusion(f32[16,64,128]{2,0,1:T(8,128)} %get-tuple-element.221, s32[]{:T(128)S(6)} %select_n.98, f32[8,8,128]{2,1,0:T(8,128)} %bitcast.277, f32[8,128]{1,0:T(8,128)S(1)} %get-tuple-element.203, f32[8,8,128]{2,1,0:T(8,128)} %bitcast.278, f32[8,128]{1,0:T(8,128)S(1)} %get-tuple-element.205, ...), kind=kOutput, calls=%fused_computation.6.clone.1 | convolution fusion | flops 45219840 | bytes 438340 | tf_op jit(solution)/shard_map/while/body/eval_jaxpr/gkpq,gkvq->vgp/dot_general | solution.py:160
  184.0 3.4 %fusion.160 = f32[16,64,128]{2,0,1:T(8,128)} fusion(f32[16,64,128]{2,0,1:T(8,128)} %get-tuple-element.221, s32[]{:T(128)S(6)} %select_n.98, f32[8,8,128]{2,1,0:T(8,128)} %bitcast.277, f32[8,128]{1,0:T(8,128)S(1)} %get-tuple-element.203, f32[8,8,128]{2,1,0:T(8,128)} %bitcast.278, f32[8,128]{1,0:T(8,128)S(1)} %get-tuple-element.205, ...), kind=kOutput, calls=%fused_computation.6.clone.1 | convolution fusion | flops 45219840 | bytes 438340 | tf_op jit(solution)/shard_map/while/body/eval_jaxpr/gkpq,gkvq->vgp/dot_general | solution.py:160
  190.4 3.4 %fusion.160 = f32[16,64,128]{2,0,1:T(8,128)} fusion(f32[16,64,128]{2,0,1:T(8,128)} %get-tuple-element.221, s32[]{:T(128)S(6)} %select_n.98, f32[8,8,128]{2,1,0:T(8,128)} %bitcast.277, f32[8,128]{1,0:T(8,128)S(1)} %get-tuple-element.203, f32[8,8,128]{2,1,0:T(8,128)} %bitcast.278, f32[8,128]{1,0:T(8,128)S(1)} %get-tuple-element.205, ...), kind=kOutput, calls=%fused_computation.6.clone.1 | convolution fusion | flops 45219840 | bytes 438340 | tf_op jit(solution)/shard_map/while/body/eval_jaxpr/gkpq,gkvq->vgp/dot_general | solution.py:160
  196.8 3.4 %fusion.160 = f32[16,64,128]{2,0,1:T(8,128)} fusion(f32[16,64,128]{2,0,1:T(8,128)} %get-tuple-element.221, s32[]{:T(128)S(6)} %select_n.98, f32[8,8,128]{2,1,0:T(8,128)} %bitcast.277, f32[8,128]{1,0:T(8,128)S(1)} %get-tuple-element.203, f32[8,8,128]{2,1,0:T(8,128)} %bitcast.278, f32[8,128]{1,0:T(8,128)S(1)} %get-tuple-element.205, ...), kind=kOutput, calls=%fused_computation.6.clone.1 | convolution fusion | flops 45219840 | bytes 438340 | tf_op jit(solution)/shard_map/while/body/eval_jaxpr/gkpq,gkvq->vgp/dot_general | solution.py:160
  215.3 1.5 fusion.107
  219.7 2.5 %fusion.109 = f32[64,16,64]{2,1,0:T(8,128)} fusion(f32[64,16,64]{2,1,0:T(8,128)S(1)} %bitcast.270, bf16[64,64,64]{2,1,0:T(8,128)(2,1)S(1)} %copy.89), kind=kOutput, calls=%fused_computation.160 | convolution fusion | flops 50331648 | bytes 1048576 | tf_op jit(solution)/shard_map/nvl,nkl->nvk/dot_general | solution.py:116
  222.2 6.8 %gather_fusion.2 = bf16[256,16,64]{2,1,0:T(8,128)(2,1)S(1)} fusion(bf16[4096,16,64]{2,1,0:T(8,128)(2,1)} %all-gather.2.cloned.1.call-done, s32[1024]{0:T(1024)} %pad_clamp_fusion.1), kind=kCustom, calls=%fused_computation.2 | custom fusion | bytes 1049600 | tf_op jit(solution)/shard_map/jit(_take)/gather | solution.py:127
  229.0 3.6 %fusion.15 = f32[256,16,64]{2,1,0:T(8,128)S(1)} fusion(bf16[256,64,64]{2,1,0:T(8,128)(2,1)} %copy.83, bf16[256,16,64]{2,1,0:T(8,128)(2,1)S(1)} %gather_fusion.2, pred[256]{0:T(512)(128)(4,1)S(1)} %copy-done.36), kind=kOutput, calls=%fused_computation.40 | convolution fusion | flops 33816576 | bytes 3670272 | tf_op jit(solution)/shard_map/pvk,pkl->pvl/dot_general | solution.py:128
  232.6 1.5 fusion.9
  (252 shorter events, 85.2 us)
Async XLA Ops:
  6.5 26.8 %copy-start = (bf16[64,64,128]{2,1,0:T(8,128)(2,1)S(1)}, bf16[64,64,128]{2,1,0:T(8,128)(2,1)}, u32[]{:S(2)}) copy-start(bf16[64,64,128]{2,1,0:T(8,128)(2,1)} %param.15) | copy-start | bytes 3145732
  6.5 5.4 %copy-start.1 = (bf16[128,64,64]{0,2,1:T(8,128)(2,1)S(1)}, bf16[128,64,64]{0,2,1:T(8,128)(2,1)}, u32[]{:S(2)}) copy-start(bf16[128,64,64]{0,2,1:T(8,128)(2,1)} %param.16) | copy-start | bytes 3145732
  6.5 215.6 %all-gather.2.cloned.1.call-start = ((), (), s32[]{:S(2)}) async-start(), calls=%async_computation | async-start | bytes 17039360 | tf_op jit(solution)/shard_map/all_gather | solution.py:126
  17.9 15.5 %copy-start.13 = (bf16[16,8192]{1,0:T(8,128)(2,1)S(1)}, bf16[16,8192]{1,0:T(8,128)(2,1)}, u32[]{:S(2)}) copy-start(bf16[16,8192]{1,0:T(8,128)(2,1)} %param.13) | copy-start | bytes 786436
  31.5 49.2 %copy-start.2 = (bf16[128,64,64]{0,2,1:T(8,128)(2,1)S(1)}, bf16[128,64,64]{0,2,1:T(8,128)(2,1)}, u32[]{:S(2)}) copy-start(bf16[128,64,64]{0,2,1:T(8,128)(2,1)} %param.17) | copy-start | bytes 3145732
  33.3 48.8 %copy-start.26 = (bf16[1,64,64]{2,1,0:T(8,128)(2,1)}, bf16[1,64,64]{2,1,0:T(8,128)(2,1)S(1)}, u32[]{:S(2)}) copy-start(bf16[1,64,64]{2,1,0:T(8,128)(2,1)S(1)} %copy.95) | copy-start | bytes 24580
  33.3 2.3 copy-start.3
  33.3 4.1 %copy-start.15 = (bf16[8,64,64]{2,1,0:T(8,128)(2,1)S(1)}, bf16[8,64,64]{2,1,0:T(8,128)(2,1)}, u32[]{:S(2)}) copy-start(bf16[8,64,64]{2,1,0:T(8,128)(2,1)} %copy.92) | copy-start | bytes 196612
  33.3 4.8 %copy-start.21 = (bf16[4,64,64]{2,1,0:T(8,128)(2,1)S(1)}, bf16[4,64,64]{2,1,0:T(8,128)(2,1)}, u32[]{:S(2)}) copy-start(bf16[4,64,64]{2,1,0:T(8,128)(2,1)} %copy.93) | copy-start | bytes 98308
  33.3 4.9 %copy-start.24 = (bf16[2,64,64]{2,1,0:T(8,128)(2,1)S(1)}, bf16[2,64,64]{2,1,0:T(8,128)(2,1)}, u32[]{:S(2)}) copy-start(bf16[2,64,64]{2,1,0:T(8,128)(2,1)} %copy.94) | copy-start | bytes 49156
  34.7 1.5 copy-start.5
  37.5 0.6 copy-start.20
  38.1 0.6 copy-start.25
  38.3 0.6 copy-start.27
  38.9 0.6 copy-start.31
  40.1 28.5 %collective-permute-start.4 = (f32[2,16,64]{2,1,0:T(8,128)}, f32[2,16,64]{2,1,0:T(8,128)}, u32[]{:S(2)}, u32[]{:S(2)}) collective-permute-start(f32[2,16,64]{2,1,0:T(8,128)} %pad_maximum_fusion), channel_id=1, source_target_pairs={{0,4},{4,0},{8,12},{12,8},{16,20},{20,16},{24,28},{28,24},{32,36},... | collective-permute-start | bytes 24584 | tf_op jit(solution)/shard_map/ppermute | solution.py:20
  52.8 0.6 copy-start.17
  53.5 0.6 copy-start.22
  54.7 74.0 %collective-permute-start.2 = (bf16[3,1024]{1,0:T(4,128)(2,1)}, bf16[3,1024]{1,0:T(4,128)(2,1)}, u32[]{:S(2)}, u32[]{:S(2)}) collective-permute-start(bf16[3,1024]{1,0:T(4,128)(2,1)} %get-tuple-element.155), channel_id=1, source_target_pairs={{0,4},{4,8},{8,12},{12,16},{16,20},{20,24},{24,28},{28,32},{32,36}... | collective-permute-start | bytes 18440 | tf_op jit(solution)/shard_map/ppermute | solution.py:31
  56.6 72.1 %collective-permute-start.3 = (bf16[3,1024]{1,0:T(4,128)(2,1)}, bf16[3,1024]{1,0:T(4,128)(2,1)}, u32[]{:S(2)}, u32[]{:S(2)}) collective-permute-start(bf16[3,1024]{1,0:T(4,128)(2,1)} %get-tuple-element.156), channel_id=1, source_target_pairs={{4,0},{8,4},{12,8},{16,12},{20,16},{24,20},{28,24},{32,28},{36,32}... | collective-permute-start | bytes 18440 | tf_op jit(solution)/shard_map/ppermute | solution.py:33
  61.7 73.6 %collective-permute-start = (bf16[16,1024]{1,0:T(8,128)(2,1)}, bf16[16,1024]{1,0:T(8,128)(2,1)}, u32[]{:S(2)}, u32[]{:S(2)}) collective-permute-start(bf16[16,1024]{1,0:T(8,128)(2,1)} %get-tuple-element.153), channel_id=1, source_target_pairs={{0,4},{4,8},{8,12},{12,16},{16,20},{20,24},{24,28},{28,32},{32,36}... | collective-permute-start | bytes 98312 | tf_op jit(solution)/shard_map/ppermute | solution.py:31
  63.6 71.6 %collective-permute-start.1 = (bf16[16,1024]{1,0:T(8,128)(2,1)}, bf16[16,1024]{1,0:T(8,128)(2,1)}, u32[]{:S(2)}, u32[]{:S(2)}) collective-permute-start(bf16[16,1024]{1,0:T(8,128)(2,1)} %get-tuple-element.154), channel_id=1, source_target_pairs={{4,0},{8,4},{12,8},{16,12},{20,16},{24,20},{28,24},{32,28},{36,32}... | collective-permute-start | bytes 98312 | tf_op jit(solution)/shard_map/ppermute | solution.py:33
  70.1 0.6 copy-start.32
  71.4 4.1 %collective-permute-start.5 = (f32[2,16,64]{2,1,0:T(8,128)}, f32[2,16,64]{2,1,0:T(8,128)}, u32[]{:S(2)}, u32[]{:S(2)}) collective-permute-start(f32[2,16,64]{2,1,0:T(8,128)} %pad_maximum_fusion.1), channel_id=1, source_target_pairs={{0,8},{8,0},{4,12},{12,4},{16,24},{24,16},{20,28},{28,20},{32,40},... | collective-permute-start | bytes 24584 | tf_op jit(solution)/shard_map/ppermute | solution.py:20
  77.0 0.6 copy-start.29
  78.2 42.2 %collective-permute-start.6 = (f32[2,16,64]{2,1,0:T(8,128)}, f32[2,16,64]{2,1,0:T(8,128)}, u32[]{:S(2)}, u32[]{:S(2)}) collective-permute-start(f32[2,16,64]{2,1,0:T(8,128)} %pad_maximum_fusion.2), channel_id=1, source_target_pairs={{0,16},{16,0},{4,20},{20,4},{8,24},{24,8},{12,28},{28,12},{32,48},... | collective-permute-start | bytes 24584 | tf_op jit(solution)/shard_map/ppermute | solution.py:20
  83.5 5.5 %copy-start.35 = (s32[256,2]{0,1:T(2,128)S(1)}, s32[256,2]{0,1:T(2,128)}, u32[]{:S(2)}) copy-start(s32[256,2]{0,1:T(2,128)} %param.21) | copy-start | bytes 6148
  90.5 12.8 %copy-start.7 = (bf16[16,64,64]{0,2,1:T(8,128)(2,1)S(1)}, bf16[16,64,64]{0,2,1:T(8,128)(2,1)}, u32[]{:S(2)}) copy-start(bf16[16,64,64]{0,2,1:T(8,128)(2,1)} %slice.168) | copy-start | bytes 393220
  104.5 11.1 %copy-start.6 = (f32[64,16,64]{2,1,0:T(8,128)S(1)}, f32[64,16,64]{2,1,0:T(8,128)}, u32[]{:S(2)}) copy-start(f32[64,16,64]{2,1,0:T(8,128)} %copy-done.5) | copy-start | bytes 786436
  108.1 11.7 %copy-start.18 = (f32[3,8192]{1,0:T(4,128)S(1)}, f32[3,8192]{1,0:T(4,128)}, u32[]{:S(2)}) copy-start(f32[3,8192]{1,0:T(4,128)} %copy-done.17) | copy-start | bytes 294916
  108.1 12.3 %copy-start.30 = (f32[16,64]{1,0:T(8,128)S(1)}, f32[16,64]{1,0:T(8,128)}, u32[]{:S(2)}) copy-start(f32[16,64]{1,0:T(8,128)} %copy-done.29) | copy-start | bytes 12292
  108.1 20.7 %copy-start.23 = (bf16[3,8192]{1,0:T(4,128)(2,1)S(1)}, bf16[3,8192]{1,0:T(4,128)(2,1)}, u32[]{:S(2)}) copy-start(bf16[3,8192]{1,0:T(4,128)(2,1)} %copy-done.22) | copy-start | bytes 147460
  108.1 27.2 %copy-start.14 = (bf16[16,8192]{1,0:T(8,128)(2,1)S(1)}, bf16[16,8192]{1,0:T(8,128)(2,1)}, u32[]{:S(2)}) copy-start(bf16[16,8192]{1,0:T(8,128)(2,1)} %param.13) | copy-start | bytes 786436
  115.6 33.0 %copy-start.28 = (s32[64,8]{0,1:T(8,128)S(1)}, s32[64,8]{0,1:T(8,128)}, u32[]{:S(2)}) copy-start(s32[64,8]{0,1:T(8,128)} %subtract_add_fusion) | copy-start | bytes 6148
  122.0 8.8 %collective-permute-start.7 = (f32[2,16,64]{2,1,0:T(8,128)S(1)}, f32[2,16,64]{2,1,0:T(8,128)S(1)}, u32[]{:S(2)}, u32[]{:S(2)}) collective-permute-start(f32[2,16,64]{2,1,0:T(8,128)S(1)} %pad_maximum_fusion.3), channel_id=1, source_target_pairs={{0,32},{32,0},{4,36},{36,4},{8,40},{40,8},{12,44},{44,12},{16,48},... | collective-permute-start | bytes 24584 | tf_op jit(solution)/shard_map/ppermute | solution.py:20
  130.8 4.5 %copy-start.33 = (f32[2,16,64]{2,1,0:T(8,128)}, f32[2,16,64]{2,1,0:T(8,128)S(1)}, u32[]{:S(2)}) copy-start(f32[2,16,64]{2,1,0:T(8,128)S(1)} %collective-permute-done.7) | copy-start | bytes 24580
  131.7 5.6 %collective-permute-start.8 = (f32[2,16,64]{2,1,0:T(8,128)S(1)}, f32[2,16,64]{2,1,0:T(8,128)S(1)}, u32[]{:S(2)}, u32[]{:S(2)}) collective-permute-start(f32[2,16,64]{2,1,0:T(8,128)S(1)} %pad_maximum_fusion.4), channel_id=1, source_target_pairs={{0,64},{64,0},{4,68},{68,4},{8,72},{72,8},{12,76},{76,12},{16,80},... | collective-permute-start | bytes 24584 | tf_op jit(solution)/shard_map/ppermute | solution.py:20
  137.3 11.3 %copy-start.34 = (f32[2,16,64]{2,1,0:T(8,128)}, f32[2,16,64]{2,1,0:T(8,128)S(1)}, u32[]{:S(2)}) copy-start(f32[2,16,64]{2,1,0:T(8,128)S(1)} %collective-permute-done.8) | copy-start | bytes 24580
  138.8 61.4 %collective-permute-start.9 = (f32[2,16,64]{2,1,0:T(8,128)}, f32[2,16,64]{2,1,0:T(8,128)}, u32[]{:S(2)}, u32[]{:S(2)}) collective-permute-start(f32[2,16,64]{2,1,0:T(8,128)} %pad_maximum_fusion.5), channel_id=1, source_target_pairs={{0,128},{128,0},{4,132},{132,4},{8,136},{136,8},{12,140},{140,12},... | collective-permute-start | bytes 24584 | tf_op jit(solution)/shard_map/ppermute | solution.py:20
  148.6 65.2 %copy-start.16 = (bf16[8,64,64]{2,1,0:T(8,128)(2,1)S(1)}, bf16[8,64,64]{2,1,0:T(8,128)(2,1)}, u32[]{:S(2)}) copy-start(bf16[8,64,64]{2,1,0:T(8,128)(2,1)} %copy.92) | copy-start | bytes 196612
  148.6 69.6 %copy-start.4 = (bf16[32,64,64]{2,1,0:T(8,128)(2,1)S(1)}, bf16[32,64,64]{2,1,0:T(8,128)(2,1)}, u32[]{:S(2)}) copy-start(bf16[32,64,64]{2,1,0:T(8,128)(2,1)} %copy.90) | copy-start | bytes 786436
  200.2 18.9 %copy-start.9 = (bf16[32,64,64]{2,1,0:T(8,128)(2,1)S(1)}, bf16[32,64,64]{2,1,0:T(8,128)(2,1)}, u32[]{:S(2)}) copy-start(bf16[32,64,64]{2,1,0:T(8,128)(2,1)} %copy.101) | copy-start | bytes 786436
  200.2 18.9 %copy-start.19 = (f32[16,2,16,64]{3,2,1,0:T(8,128)S(1)}, f32[16,2,16,64]{3,2,1,0:T(8,128)}, u32[]{:S(2)}) copy-start(f32[16,2,16,64]{3,2,1,0:T(8,128)} %rev.19) | copy-start | bytes 393220
  216.8 12.2 %copy-start.36 = (pred[256]{0:T(512)(128)(4,1)S(1)}, pred[256]{0:T(512)(128)(4,1)}, u32[]{:S(2)}) copy-start(pred[256]{0:T(512)(128)(4,1)} %get-tuple-element.145) | copy-start | bytes 772
  228.9 5.1 %copy-start.8 = (bf16[64,64,64]{2,1,0:T(8,128)(2,1)S(1)}, bf16[64,64,64]{2,1,0:T(8,128)(2,1)}, u32[]{:S(2)}) copy-start(bf16[64,64,64]{2,1,0:T(8,128)(2,1)} %copy.102) | copy-start | bytes 1572868
  229.0 5.1 %copy-start.10 = (f32[32,2,16,64]{3,2,1,0:T(8,128)S(1)}, f32[32,2,16,64]{3,2,1,0:T(8,128)}, u32[]{:S(2)}) copy-start(f32[32,2,16,64]{3,2,1,0:T(8,128)} %rev.20) | copy-start | bytes 786436
  229.0 5.1 %copy-start.12 = (f32[64,16,64]{2,1,0:T(8,128)S(1)}, f32[64,16,64]{2,1,0:T(8,128)}, u32[]{:S(2)}) copy-start(f32[64,16,64]{2,1,0:T(8,128)} %fusion.109) | copy-start | bytes 786436
  232.6 2.6 %copy-start.11 = (f32[16,64,128]{2,0,1:T(8,128)S(1)}, f32[16,64,128]{2,0,1:T(8,128)}, u32[]{:S(2)}) copy-start(f32[16,64,128]{2,0,1:T(8,128)} %get-tuple-element.114) | copy-start | bytes 1572868
Sparse Core Ops, SparseCore 0:
  40.2 101.2 all-gather.1
where the time goes:
time: 247 us; the launch traced here: 243 us
  local copies, waits for them, and re-layouts  106 us (43%)
  matrix products  64.2 us (26%)
  starting transfers between devices  31.6 us (13%)
  between operations  13.8 us (6%)
  blocking collectives  12.7 us (5%)
  other arithmetic  11.6 us (5%)
  waiting for transfers between devices  3.48 us (1%)
    unnamed x91, local copies, waits for them, and re-layouts  44.2 us
    dot_general x8, matrix products, near_group(): jnp.einsum('gkpq,gkvq->vgp', kernel, values, preferred_element_type=jnp.f...  26.8 us
    ppermute x6, starting transfers between devices, swapped(): return lax.ppermute(block, axis, route)  20.5 us
    all_gather x1, blocking collectives, per_device(): coords = lax.all_gather(points, 'vec', axis=1, tiled=True)  12.7 us
    slice x6, local copies, waits for them, and re-layouts, per_device(): transfer[node_count:2 * node_count]  9.92 us
    slice x6, local copies, waits for them, and re-layouts, per_device(): coupling[node_count:2 * node_count]  8.36 us
    ppermute x2, starting transfers between devices, with_halo(): lax.ppermute(head, axis, [((i + 1) % count, i) for i in range(ends)])  7.29 us
    dot_general x6, matrix products, per_device(): jnp.einsum('nvl,nkl->nvk', parent, transfer[node_count:2 * node_count], p...  7.15 us
  transfers between devices with their start and end apart: 11, of which 3 were waited for; matrix products, arithmetic and copies ran while one was open for 54% of the time, Pallas kernels for 0%

commit v1 on v0

v1 whole, which is shorter than its diff:
```python
import functools

import jax
import jax.numpy as jnp
from jax import lax
from jax.experimental import pallas as pl
from jax.experimental.pallas import tpu as pltpu
from jax.sharding import PartitionSpec as P

F32 = jnp.float32
BF16 = jnp.bfloat16
REACH = 8
KERNEL_SCALE = 1.0 / 64.0
DELTA_SQ = 0.0025

GROUP = 8
GROUP_BITS = 3


def _spec(space=pltpu.VMEM):
    return pl.BlockSpec(memory_space=space)


def _call(body, outs, n_in, smem=(), scratch=(), flops=0, name=None):
    return pl.pallas_call(
        body,
        out_shape=outs,
        in_specs=[_spec(pltpu.SMEM) if i in smem else _spec() for i in range(n_in)],
        out_specs=jax.tree.map(lambda _: _spec(), outs),
        scratch_shapes=list(scratch),
        compiler_params=pltpu.CompilerParams(vmem_limit_bytes=40 * 1024 * 1024),
        cost_estimate=pl.CostEstimate(flops=flops, bytes_accessed=1 << 20, transcendentals=0),
        name=name,
    )


def _shape(shape, dtype):
    return jax.ShapeDtypeStruct(shape, dtype)


def _dot(a, b):
    return jnp.dot(a, b, preferred_element_type=F32)


def _dot_t(a, b):
    return lax.dot_general(a, b, (((1,), (1,)), ((), ())), preferred_element_type=F32)


def _leading(c):
    p = c * 65537.0
    return p - (p - c)


def _two(c):
    high = _leading(c)
    return jnp.concatenate([high, c - high], axis=0).astype(BF16)


def _mul(c, w):
    rows = c.shape[0]
    both = _dot(_two(c), w)
    return both[:rows] + both[rows:]


def _mul_t(c, w):
    rows = c.shape[0]
    both = _dot_t(_two(c), w)
    return both[:rows] + both[rows:]


def _swap_halves(x):
    half = x.shape[-1] // 2
    return jnp.concatenate([x[:, half:], x[:, :half]], axis=1)


def _request_kernel(anchor_ref, leaves_ref, table_ref, plan_ref):
    me = lax.axis_index("leaf")
    pairs = anchor_ref.shape[1]
    tiles = leaves_ref.shape[0]
    del tiles
    anchor = anchor_ref[...]
    source = leaves_ref[0:1, :]
    my_z = me // GROUP
    my_k = me % GROUP
    core = anchor & 1
    dz = ((anchor >> GROUP_BITS) - my_z) & 7
    near_side = (dz & 3) == 0
    server = jnp.where(near_side, core, jnp.where(dz > 4, 0, 1))
    step = jnp.where(dz > 4, 8 - dz, dz)
    base = jnp.where(
        dz == 0,
        0,
        jnp.where(dz == 4, 224, 32 + (step - 1) * 64 + (core ^ server) * 32),
    )
    tile = base + (source >> 1)
    group = (((anchor & 6) | server) ^ my_k)
    sub8 = lax.broadcasted_iota(jnp.int32, (8, pairs), 0)
    picked = (sub8 == group).astype(F32)
    row = lax.broadcasted_iota(jnp.int32, (pairs, pairs), 0)
    col = lax.broadcasted_iota(jnp.int32, (pairs, pairs), 1)
    upto = (row <= col).astype(F32).astype(BF16)
    count = _dot(picked.astype(BF16), upto)
    slot = (jnp.sum(picked * count, axis=0, keepdims=True) - 1.0).astype(jnp.int32)
    flip = (source ^ slot) & 1
    sub128 = lax.broadcasted_iota(jnp.int32, (128, pairs), 0)
    placed = (sub128 == slot).astype(F32).astype(BF16)
    table = _dot_t((picked * tile.astype(F32)).astype(BF16), placed)
    flips = _dot_t((picked * flip.astype(F32)).astype(BF16), placed)
    table_ref[...] = table + 256.0 * flips
    place = group * 64 + slot
    number = lax.broadcasted_iota(jnp.int32, (1, pairs), 1)
    plan_ref[0:1, :] = (place >> 1) + 256 * ((place ^ number) & 1)
    plan_ref[1:2, :] = leaves_ref[1:2, :]


def _coeff_kernel(vec_ref, basis_ref, sent_ref, coeff_ref):
    leaves = basis_ref.shape[0]
    lane = lax.broadcasted_iota(jnp.int32, (16, 128), 1)
    for i in range(leaves // 2):
        x0 = vec_ref[:, 256 * i : 256 * i + 128]
        x1 = vec_ref[:, 256 * i + 128 : 256 * i + 256]
        w = basis_ref[2 * i : 2 * i + 2].reshape(128, 128)
        r = _dot_t(jnp.concatenate([x0, x1], axis=0), w)
        c = jnp.where(lane < 64, r[:16], r[16:])
        coeff_ref[i] = c
        sent_ref[i] = c.astype(BF16)


def _up_kernel(coeff_ref, move_ref, table_ref, levels_ref, out_ref):
    def parent(tile, node):
        return _mul(tile, move_ref[node : node + 2].reshape(128, 64))

    size = 32
    current = [coeff_ref[i] for i in range(size)]
    node = 64
    while True:
        parents = [parent(current[i], node + 2 * i) for i in range(size)]
        if size == 1:
            root = parents[0]
            break
        size //= 2
        node //= 2
        current = [
            jnp.concatenate([parents[2 * i], parents[2 * i + 1]], axis=1) for i in range(size)
        ]
        for i in range(size):
            levels_ref[size + i] = current[i]
    levels_ref[0] = jnp.concatenate([root, root], axis=1)
    out_ref[0:8, :] = table_ref[...]
    out_ref[8:24, :] = jnp.concatenate([root, _mul(root, move_ref[1])], axis=1)


def _pair(a, b):
    return jnp.concatenate([a, b], axis=1)


def _group_kernel(group_ref, upper_ref, sib_ref, top_ref):
    me = lax.axis_index("leaf")
    my_k = me % GROUP
    my_z = me // GROUP
    shares = [group_ref[a ^ my_k, 8:24, 64:128] for a in range(GROUP)]
    sib_ref[0] = group_ref[1, 8:24, 0:64]
    nodes = [shares[2 * i] + shares[2 * i + 1] for i in range(GROUP // 2)]
    depth = 1
    while len(nodes) > 1:
        want = (my_k >> depth) ^ 1
        sib = nodes[0]
        for i in range(1, len(nodes)):
            sib = jnp.where(want == i, nodes[i], sib)
        sib_ref[depth] = sib
        depth += 1
        first = (GROUP + my_z) * len(nodes)
        nodes = [
            _mul(
                _pair(nodes[2 * i], nodes[2 * i + 1]),
                upper_ref[pl.ds(first + 2 * i, 2)].reshape(128, 64),
            )
            for i in range(len(nodes) // 2)
        ]
    top_ref[...] = nodes[0]


def _tree_kernel(
    coeff_ref, levels_ref, sib_ref, planes_ref, move_ref, pair_ref, upper_t_ref, upper_c_ref, out_ref
):
    me = lax.axis_index("leaf")
    my_z = me // GROUP
    sibs = [sib_ref[0], sib_ref[1], sib_ref[2], planes_ref[1]]
    nodes = [planes_ref[a ^ my_z] for a in range(8)]
    two = [
        _mul(
            _pair(nodes[2 * i], nodes[2 * i + 1]),
            upper_t_ref[8 + 2 * i : 10 + 2 * i].reshape(128, 64),
        )
        for i in range(4)
    ]
    want = (my_z >> 1) ^ 1
    sib = jnp.zeros((16, 64), F32)
    for i in range(4):
        sib = jnp.where(want == i, two[i], sib)
    sibs.append(sib)
    one = [
        _mul(_pair(two[2 * i], two[2 * i + 1]), upper_t_ref[4 + 2 * i : 6 + 2 * i].reshape(128, 64))
        for i in range(2)
    ]
    sibs.append(jnp.where((my_z >> 2) == 0, one[1], one[0]))
    node = 64 + me
    local = None
    for depth in range(1, 7):
        bit = 6 - depth
        if bit == 0:
            move, pair = move_ref[1], pair_ref[1]
        else:
            move, pair = upper_t_ref[node >> bit], upper_c_ref[node >> bit]
        coupled = _mul(sibs[bit], pair)
        local = coupled if local is None else _mul_t(local, move) + coupled
    lane = lax.broadcasted_iota(jnp.int32, (16, 128), 1)
    parents = [local]
    size = 1
    while True:
        children = []
        for i in range(size):
            node = 2 * size + 2 * i
            tile = coeff_ref[i] if size == 32 else levels_ref[size + i]
            moved = _mul_t(parents[i], move_ref[node : node + 2].reshape(128, 64))
            w = pair_ref[node : node + 2].reshape(128, 64)
            other = _swap_halves(tile)
            both = _mul(
                jnp.concatenate(
                    [jnp.where(lane < 64, other, 0.0), jnp.where(lane < 64, 0.0, other)], axis=0
                ),
                w,
            )
            children.append(moved + _pair(both[:16], both[16:]))
        if size == 32:
            break
        parents = []
        for c in children:
            parents += [c[:, :64], c[:, 64:]]
        size *= 2
    for i in range(32):
        out_ref[i] = children[i]


def _both_ways(scratch, blocks):
    at = 0
    for ref in blocks:
        count = ref.shape[0]
        x = ref[...]
        scratch[at : at + count] = x
        y = _swap_halves(x.reshape(count * 16, 128)).reshape(count, 16, 128)
        scratch[256 + at : 256 + at + count] = y
        at += count


def _gather_kernel(table_ref, b0, b1, b2, b3, b4, *rest):
    outs, scratch = rest[:GROUP], rest[GROUP]
    _both_ways(scratch, [b0, b1, b2, b3, b4])
    lane = lax.broadcasted_iota(jnp.int32, (16, 128), 1)
    for k in range(GROUP):
        for s in range(32):
            a = scratch[table_ref[k, 2 * s]]
            b = scratch[table_ref[k, 2 * s + 1]]
            outs[k][s] = jnp.where(lane < 64, a, b)


def _points_kernel(p0, p1, p2, p3, vec_ref, source_ref, target_ref, first_ref, last_ref):
    mine = lax.axis_index("vec")
    width = p0.shape[1]
    for shift, ref in enumerate((p0, p1, p2, p3)):
        spot = pl.multiple_of(((mine + shift) & 3) * width, width)
        c = ref[...] - 0.5
        high = _leading(c)
        mid = _leading(c - high)
        rounded = high + mid
        square = rounded * rounded
        norm = square[0:1] + square[1:2] + square[2:3]

        def thirds(n):
            n1 = _leading(n)
            n2 = _leading(n - n1)
            return [n1, n2, n - n1 - n2]

        one = jnp.ones((3, width), F32)
        zero = jnp.zeros((2, width), F32)
        own = jnp.concatenate([high, mid, zero], axis=0)
        source = jnp.concatenate([own, jnp.concatenate(thirds(norm + DELTA_SQ) + [one, zero], axis=0)], axis=0)
        target = jnp.concatenate(
            [
                -2.0 * jnp.concatenate([high, high, zero], axis=0),
                -2.0 * jnp.concatenate([mid, mid, zero], axis=0),
                jnp.concatenate([one] + thirds(norm) + [zero], axis=0),
                jnp.zeros((8, width), F32),
            ],
            axis=0,
        )
        source_ref[:, pl.ds(spot, width)] = source.astype(BF16)
        target_ref[:, pl.ds(spot, width)] = target.astype(BF16)
    halo = first_ref.shape[1]
    total = vec_ref.shape[1]
    first_ref[0:16, :] = source_ref[:, 0:halo]
    first_ref[16:32, :] = vec_ref[:, 0:halo]
    last_ref[0:16, :] = source_ref[:, total - halo : total]
    last_ref[16:32, :] = vec_ref[:, total - halo : total]


def _near_kernel(cols_ref, source_ref, target_ref, vec_ref, left_ref, right_ref, out_ref, rows, values):
    me = lax.axis_index("leaf")
    leaves = cols_ref.shape[1]
    first = REACH - me * leaves
    zero = jnp.zeros((8, 128), F32)

    def place(index, feature, value):
        f = feature.astype(F32)
        f = jnp.concatenate([f[0:8], f[0:8], f[8:16], zero], axis=0)
        rows[index] = jnp.transpose(f).astype(BF16)
        values[index] = value

    for i in range(REACH):
        lanes = slice(128 * i, 128 * i + 128)
        place(i, left_ref[0:16, lanes], left_ref[16:32, lanes])
        place(REACH + leaves + i, right_ref[0:16, lanes], right_ref[16:32, lanes])
    for i in range(leaves):
        lanes = slice(128 * i, 128 * i + 128)
        place(REACH + i, source_ref[:, lanes], vec_ref[:, lanes])

    def leaf(t, carry):
        lanes = pl.ds(pl.multiple_of(t * 128, 128), 128)
        target = target_ref[:, lanes]
        kernel, value = [], []
        for k in range(cols_ref.shape[0]):
            index = cols_ref[k, t] + first
            dist = _dot(rows[index], target)
            kernel.append(lax.rsqrt(dist).astype(BF16))
            value.append(values[index])
        total = _dot(jnp.concatenate(value, axis=1), jnp.concatenate(kernel, axis=0))
        out_ref[:, lanes] = total * KERNEL_SCALE
        return carry

    lax.fori_loop(0, leaves, leaf, 0, unroll=2)


def _final_kernel(plan_ref, r0, r1, r2, r3, r4, r5, r6, r7, block_ref, local_ref, basis_ref, near_ref, out_ref, scratch, far):
    _both_ways(scratch, [r0, r1, r2, r3, r4, r5, r6, r7])
    far[...] = jnp.zeros_like(far)
    lane = lax.broadcasted_iota(jnp.int32, (16, 128), 1)
    pairs = block_ref.shape[0]

    def add(i, carry):
        w = block_ref[pl.ds(2 * i, 2)].reshape(128, 64)
        a = scratch[plan_ref[0, 2 * i]]
        b = scratch[plan_ref[0, 2 * i + 1]]
        zero = jnp.zeros_like(a)
        x = jnp.concatenate([jnp.where(lane < 64, a, zero), jnp.where(lane < 64, zero, b)], axis=0)
        r = _dot(x, w)
        far[plan_ref[1, 2 * i]] += r[:16]
        far[plan_ref[1, 2 * i + 1]] += r[16:]
        return carry

    lax.fori_loop(0, pairs // 2, add, 0, unroll=4)
    for i in range(basis_ref.shape[0] // 2):
        total = (local_ref[i] + _pair(far[2 * i], far[2 * i + 1])).astype(BF16)
        zero = jnp.zeros_like(total)
        x = jnp.concatenate([jnp.where(lane < 64, total, zero), jnp.where(lane < 64, zero, total)], axis=0)
        r = _dot(x, basis_ref[2 * i : 2 * i + 2].reshape(128, 128))
        at = 256 * i
        out_ref[:, at : at + 128] = near_ref[:, at : at + 128] + r[:16]
        out_ref[:, at + 128 : at + 256] = near_ref[:, at + 128 : at + 256] + r[16:]


def per_device(
    vectors,
    points,
    leaf_basis,
    local_transfer,
    local_coupling,
    upper_transfer,
    upper_coupling,
    far_anchor,
    far_leaves,
    far_block,
    near_cols,
):
    n_leaf = lax.axis_size("leaf")
    n_vec = lax.axis_size("vec")
    everyone = range(n_leaf)

    def permute(x, to):
        return lax.ppermute(x, "leaf", [(i, to(i)) for i in everyone])

    tile = (32, 16, 128)

    table, plan = _call(
        _request_kernel,
        [_shape((8, 128), F32), _shape((2, 256), jnp.int32)],
        2,
        flops=1 << 20,
        name="request",
    )(far_anchor.reshape(1, -1), far_leaves.T)

    sent, coeff = _call(
        _coeff_kernel, [_shape(tile, BF16), _shape(tile, F32)], 2, flops=1 << 24, name="coeff"
    )(vectors, leaf_basis)

    def onward(i):
        z, rest = i // GROUP, i % GROUP
        return (z + 1 if i % 2 == 0 else z - 1) % (n_leaf // GROUP) * GROUP + rest

    mate = permute(sent, lambda i: i ^ 1)
    ring1 = permute(jnp.concatenate([sent, mate], axis=0), onward)
    ring2 = permute(ring1, onward)
    ring3 = permute(ring2, onward)
    ring4 = permute(ring3[:32], onward)

    levels, carried = _call(
        _up_kernel, [_shape(tile, F32), _shape((24, 128), F32)], 3, flops=1 << 24, name="up"
    )(coeff, local_transfer, table)
    group = carried[None]
    for bit in range(GROUP_BITS):
        group = jnp.concatenate([group, permute(group, lambda i: i ^ (1 << bit))], axis=0)
    siblings, top = _call(
        _group_kernel, [_shape((3, 16, 64), F32), _shape((16, 64), F32)], 2, flops=1 << 20, name="group"
    )(group, upper_transfer)
    planes = top[None]
    for bit in range(GROUP_BITS):
        planes = jnp.concatenate([planes, permute(planes, lambda i: i ^ (GROUP << bit))], axis=0)

    wanted = jnp.stack([group[k, k] for k in range(GROUP)]).astype(jnp.int32)
    rows = _call(
        _gather_kernel,
        [_shape(tile, BF16)] * GROUP,
        6,
        smem=(0,),
        scratch=[pltpu.VMEM((512, 16, 128), BF16)],
        flops=1 << 22,
        name="gather",
    )(wanted, sent, ring1, ring2, ring3, ring4)
    got = [rows[0]] + [permute(rows[k], lambda i, k=k: i ^ k) for k in range(1, GROUP)]

    turns = [points] + [
        lax.ppermute(points, "vec", [((i + s) % n_vec, i) for i in range(n_vec)]) for s in range(1, n_vec)
    ]
    halo = REACH * leaf_basis.shape[2]
    width = vectors.shape[1]
    source, target, first, last = _call(
        _points_kernel,
        [
            _shape((16, width), BF16),
            _shape((32, width), BF16),
            _shape((32, halo), BF16),
            _shape((32, halo), BF16),
        ],
        5,
        flops=1 << 22,
        name="points",
    )(*turns, vectors)
    left = lax.ppermute(last, "leaf", [(i, i + 1) for i in range(n_leaf - 1)])
    right = lax.ppermute(first, "leaf", [(i + 1, i) for i in range(n_leaf - 1)])
    blocks = leaf_basis.shape[0] + 2 * REACH
    near = _call(
        _near_kernel,
        _shape(vectors.shape, F32),
        6,
        smem=(0,),
        scratch=[pltpu.VMEM((blocks, 128, 32), BF16), pltpu.VMEM((blocks, 16, 128), BF16)],
        flops=1 << 30,
        name="near",
    )(near_cols.T, source, target, vectors, left, right)

    local = _call(_tree_kernel, _shape(tile, F32), 8, flops=1 << 26, name="tree")(
        coeff, levels, siblings, planes, local_transfer, local_coupling, upper_transfer, upper_coupling
    )
    return _call(
        _final_kernel,
        _shape(vectors.shape, F32),
        13,
        smem=(0,),
        scratch=[pltpu.VMEM((512, 16, 128), BF16), pltpu.VMEM((64, 16, 64), F32)],
        flops=1 << 27,
        name="final",
    )(plan, *got, far_block, local, leaf_basis, near)


def solution(mesh):
    return jax.shard_map(
        per_device,
        mesh=mesh,
        in_specs=(
            P("vec", "leaf"),
            P(None, ("leaf", "vec")),
            P("leaf", None, None),
            P("leaf", None, None),
            P("leaf", None, None),
            P(),
            P(),
            P("leaf", None),
            P("leaf", None),
            P("leaf", None, None),
            P("leaf", None),
        ),
        out_specs=P("vec", "leaf"),
        check_vma=False,
    )
```

time: 247 us -> 131 us (0.53)
  the two profiles are of different devices: /device:TPU:4 before, /device:TPU:1 now
where the time goes in v1:
time: 131 us; the launch traced here: 130 us
  starting transfers between devices  50 us (38%)
  Pallas kernels  37.1 us (28%)
  local copies, waits for them, and re-layouts  34.4 us (26%)
  waiting for transfers between devices  5.01 us (4%)
  other arithmetic  3.69 us (3%)
    ppermute x18, starting transfers between devices, permute(): return lax.ppermute(x, 'leaf', [(i, to(i)) for i in everyone])  43 us
    unnamed x75, local copies, waits for them, and re-layouts  30.7 us
    pallas_call x1, Pallas kernels, per_device(): _call(_near_kernel, _shape(vectors.shape, F32), 6, smem=(0,), scratch=[pl...  19 us
    pallas_call x1, Pallas kernels, per_device(): _call(_final_kernel, _shape(vectors.shape, F32), 13, smem=(0,), scratch=[...  7.7 us
    ppermute x18, waiting for transfers between devices, permute(): return lax.ppermute(x, 'leaf', [(i, to(i)) for i in everyone])  5 us
    pallas_call x1, Pallas kernels, per_device(): _call(_tree_kernel, _shape(tile, F32), 8, flops=1 << 26, name='tree')  3.24 us
    another operation x5, local copies, waits for them, and re-layouts, per_device(): wanted = jnp.stack([group[k, k] for k in range(GROUP)]).astype(jnp.int32)  3.05 us
    ppermute x1, starting transfers between devices, per_device(): right = lax.ppermute(first, 'leaf', [(i + 1, i) for i in range(n_leaf - 1)])  3.01 us
  transfers between devices with their start and end apart: 23, of which 4 were waited for; matrix products, arithmetic and copies ran while one was open for 18% of the time, Pallas kernels for 22%

profile of v1, /device:TPU:1, one launch (start us, length us, event | category | flops | bytes accessed | tf_op | source)
XLA Modules:
  0.0 130.5 jit_solution(16584703916740789764)
XLA Ops:
  0.0 1.2 copy-done.2
  1.2 0.9 copy-done.5
  2.8 3.3 %collective-permute-start.3 = (bf16[32,16,128]{2,1,0:T(8,128)(2,1)S(1)}, bf16[32,16,128]{2,1,0:T(8,128)(2,1)}, u32[]{:S(2)}, u32[]{:S(2)}) collective-permute-start(bf16[32,16,128]{2,1,0:T(8,128)(2,1)S(1)} %get-tuple-element.29.b0), channel_id=1, source_target_pairs={{0,4},{4,0},{8,12},{12,8},{16,20},{20,16},{24,28},{28,24},{32,36},... | collective-permute-start | bytes 393224 | tf_op jit(solution)/shard_map/ppermute | solution.py:389
  6.1 3.9 %copy.12.move_ref = bf16[128,64,64]{2,1,0:T(8,128)(2,1)S(1)} copy(bf16[128,64,64]{0,2,1:T(8,128)(2,1)} %param.14) | data formatting | bytes 2097152 | tf_op args[3]
  10.4 1.5 %up.1 = (f32[32,16,128]{2,1,0:T(8,128)S(1)}, f32[24,128]{1,0:T(8,128)S(1)}) custom-call(f32[32,16,128]{2,1,0:T(8,128)S(1)} %get-tuple-element.26.coeff_ref, bf16[128,64,64]{2,1,0:T(8,128)(2,1)S(1)} %copy.12.move_ref, f32[8,128]{1,0:T(8,128)S(1)} %get-tuple-element.27.table_ref), custom_call_target="tpu_custom_call" | custom-call | flops 16777216 | bytes 1048576 | tf_op jit(solution)/shard_map/up/pallas_call | solution.py:415
  12.0 1.1 collective-permute-start.18
  13.4 0.7 collective-permute-start.20
  14.1 1.2 collective-permute-start.1
  15.3 0.9 pad_maximum_fusion
  16.2 5.6 %collective-permute-start.4 = (bf16[64,16,128]{2,1,0:T(8,128)(2,1)S(1)}, bf16[64,16,128]{2,1,0:T(8,128)(2,1)S(1)}, u32[]{:S(2)}, u32[]{:S(2)}) collective-permute-start(bf16[64,16,128]{2,1,0:T(8,128)(2,1)S(1)} %pad_maximum_fusion), channel_id=1, source_target_pairs={{0,32},{4,228},{8,40},{12,236},{16,48},{20,244},{24,56},{28,252},{... | collective-permute-start | bytes 786440 | tf_op jit(solution)/shard_map/ppermute | solution.py:389
  22.5 2.5 %collective-permute-start.2 = (f32[4,24,128]{2,1,0:T(8,128)S(1)}, f32[4,24,128]{2,1,0:T(8,128)S(1)}, u32[]{:S(2)}, u32[]{:S(2)}) collective-permute-start(f32[4,24,128]{2,1,0:T(8,128)S(1)} %pad_maximum_fusion.3), channel_id=1, source_target_pairs={{0,16},{4,20},{8,24},{12,28},{16,0},{20,4},{24,8},{28,12},{32,48},... | collective-permute-start | bytes 147464 | tf_op jit(solution)/shard_map/ppermute | solution.py:389
  25.2 3.1 %collective-permute-start.5 = (bf16[64,16,128]{2,1,0:T(8,128)(2,1)S(1)}, bf16[64,16,128]{2,1,0:T(8,128)(2,1)S(1)}, u32[]{:S(2)}, u32[]{:S(2)}) collective-permute-start(bf16[64,16,128]{2,1,0:T(8,128)(2,1)S(1)} %collective-permute-done.4.b1), channel_id=1, source_target_pairs={{0,32},{4,228},{8,40},{12,236},{16,48},{20,244},{24,56},{28,252},{... | collective-permute-start | bytes 786440 | tf_op jit(solution)/shard_map/ppermute | solution.py:389
  29.9 1.7 %collective-permute-done.5.b2 = bf16[64,16,128]{2,1,0:T(8,128)(2,1)S(1)} collective-permute-done((bf16[64,16,128]{2,1,0:T(8,128)(2,1)S(1)}, bf16[64,16,128]{2,1,0:T(8,128)(2,1)S(1)}, u32[]{:S(2)}, u32[]{:S(2)}) %collective-permute-start.5) | collective-permute-done | bytes 262176 | tf_op jit(solution)/shard_map/ppermute | solution.py:389
  31.6 3.1 %collective-permute-start.6 = (bf16[64,16,128]{2,1,0:T(8,128)(2,1)S(1)}, bf16[64,16,128]{2,1,0:T(8,128)(2,1)S(1)}, u32[]{:S(2)}, u32[]{:S(2)}) collective-permute-start(bf16[64,16,128]{2,1,0:T(8,128)(2,1)S(1)} %collective-permute-done.5.b2), channel_id=1, source_target_pairs={{0,32},{4,228},{8,40},{12,236},{16,48},{20,244},{24,56},{28,252},{... | collective-permute-start | bytes 786440 | tf_op jit(solution)/shard_map/ppermute | solution.py:389
  36.0 2.1 %collective-permute-done.6.b3 = bf16[64,16,128]{2,1,0:T(8,128)(2,1)S(1)} collective-permute-done((bf16[64,16,128]{2,1,0:T(8,128)(2,1)S(1)}, bf16[64,16,128]{2,1,0:T(8,128)(2,1)S(1)}, u32[]{:S(2)}, u32[]{:S(2)}) %collective-permute-start.6) | collective-permute-done | bytes 262176 | tf_op jit(solution)/shard_map/ppermute | solution.py:389
  38.1 0.7 slice.44
  38.7 0.7 copy-done.9
  39.4 3.1 %collective-permute-start.7 = (bf16[32,16,128]{2,1,0:T(8,128)(2,1)}, bf16[32,16,128]{2,1,0:T(8,128)(2,1)}, u32[]{:S(2)}, u32[]{:S(2)}) collective-permute-start(bf16[32,16,128]{2,1,0:T(8,128)(2,1)} %slice.44), channel_id=1, source_target_pairs={{0,32},{4,228},{8,40},{12,236},{16,48},{20,244},{24,56},{28,252},{... | collective-permute-start | bytes 393224 | tf_op jit(solution)/shard_map/ppermute | solution.py:389
  43.2 0.7 stack.3
  43.9 0.9 collective-permute-done.7.b4
  44.8 0.9 copy-done.10
  45.8 0.9 copy-done.14
  46.7 0.9 copy-done.16
  47.7 2.5 %gather.1 = (bf16[32,16,128]{2,1,0:T(8,128)(2,1)S(1)}, bf16[32,16,128]{2,1,0:T(8,128)(2,1)S(1)}, bf16[32,16,128]{2,1,0:T(8,128)(2,1)S(1)}, bf16[32,16,128]{2,1,0...) custom-call(s32[8,128]{1,0:T(8,128)S(1)} %convert_element_type.3.tab, ...), custom_call_target="tpu_custom_call" | custom-call | flops 4194304 | bytes 1048576 | tf_op jit(solution)/shard_map/gather/pallas_call | solution.py:429
  50.8 0.7 copy-done.29
  52.2 6.4 %collective-permute-start.10 = (bf16[32,16,128]{2,1,0:T(8,128)(2,1)}, bf16[32,16,128]{2,1,0:T(8,128)(2,1)S(1)}, u32[]{:S(2)}, u32[]{:S(2)}) collective-permute-start(bf16[32,16,128]{2,1,0:T(8,128)(2,1)} %get-tuple-element.33), channel_id=1, source_target_pairs={{0,12},{4,8},{8,4},{12,0},{16,28},{20,24},{24,20},{28,16},{32,44},... | collective-permute-start | bytes 393224 | tf_op jit(solution)/shard_map/ppermute | solution.py:389
  58.6 2.7 %collective-permute-start.11 = (bf16[32,16,128]{2,1,0:T(8,128)(2,1)}, bf16[32,16,128]{2,1,0:T(8,128)(2,1)}, u32[]{:S(2)}, u32[]{:S(2)}) collective-permute-start(bf16[32,16,128]{2,1,0:T(8,128)(2,1)} %get-tuple-element.34), channel_id=1, source_target_pairs={{0,16},{4,20},{8,24},{12,28},{16,0},{20,4},{24,8},{28,12},{32,48},... | collective-permute-start | bytes 393224 | tf_op jit(solution)/shard_map/ppermute | solution.py:389
  61.3 0.9 copy-done.6
  62.3 0.8 copy-done.19
  63.0 1.8 %points.1 = (bf16[16,8192]{1,0:T(8,128)(2,1)S(1)}, bf16[32,8192]{1,0:T(8,128)(2,1)S(1)}, bf16[32,1024]{1,0:T(8,128)(2,1)}, bf16[32,1024]{1,0:T(8,128)(2,1)}) custom-call(f32[3,2048]{1,0:T(4,128)S(1)} %copy-done.19, f32[3,2048]{1,0:T(4,128)} %collective-permute-done.18.p1, f32[3,2048]{1,0:T(4,128)} %collective-permute-done.19.p2, ...), custom_call_target="tpu_custom_call" | custom-call | flops 4194304 | bytes 1048576 | tf_op jit(solution)/shard_map/points/pallas_call | solution.py:445
  64.9 0.8 copy-done.22
  65.7 0.7 copy-done.24
  66.4 1.9 %collective-permute-start.21 = (bf16[32,1024]{1,0:T(8,128)(2,1)}, bf16[32,1024]{1,0:T(8,128)(2,1)}, u32[]{:S(2)}, u32[]{:S(2)}) collective-permute-start(bf16[32,1024]{1,0:T(8,128)(2,1)} %get-tuple-element.43), channel_id=1, source_target_pairs={{0,4},{4,8},{8,12},{12,16},{16,20},{20,24},{24,28},{28,32},{32,36}... | collective-permute-start | bytes 196616 | tf_op jit(solution)/shard_map/ppermute | solution.py:457
  68.3 3.0 %collective-permute-start.22 = (bf16[32,1024]{1,0:T(8,128)(2,1)}, bf16[32,1024]{1,0:T(8,128)(2,1)}, u32[]{:S(2)}, u32[]{:S(2)}) collective-permute-start(bf16[32,1024]{1,0:T(8,128)(2,1)} %get-tuple-element.44), channel_id=1, source_target_pairs={{4,0},{8,4},{12,8},{16,12},{20,16},{24,20},{28,24},{32,28},{36,32}... | collective-permute-start | bytes 196616 | tf_op jit(solution)/shard_map/ppermute | solution.py:458
  71.3 1.3 %pad_maximum_fusion.4 = f32[4,16,64]{2,1,0:T(8,128)} fusion(f32[2,16,64]{2,1,0:T(8,128)} %collective-permute-done.16, f32[1,16,64]{2,1,0:T(8,128)} %copy-done.34, f32[1,16,64]{2,1,0:T(8,128)S(1)} %bitcast.28), kind=kLoop, calls=%fused_computation.4 | loop fusion | flops 8192 | bytes 32768 | tf_op jit(solution)/shard_map/concatenate | solution.py:426
  72.7 3.7 %collective-permute-start.17 = (f32[4,16,64]{2,1,0:T(8,128)}, f32[4,16,64]{2,1,0:T(8,128)}, u32[]{:S(2)}, u32[]{:S(2)}) collective-permute-start(f32[4,16,64]{2,1,0:T(8,128)} %pad_maximum_fusion.4), channel_id=1, source_target_pairs={{0,128},{4,132},{8,136},{12,140},{16,144},{20,148},{24,152},{28,15... | collective-permute-start | bytes 49160 | tf_op jit(solution)/shard_map/ppermute | solution.py:389
  76.4 4.8 %copy.14.pair_ref = bf16[128,64,64]{2,1,0:T(8,128)(2,1)} copy(bf16[128,64,64]{0,2,1:T(8,128)(2,1)} %param.15) | data formatting | bytes 2097152 | tf_op args[4]
  81.1 7.4 %copy.15.block_ref = bf16[256,64,64]{2,1,0:T(8,128)(2,1)} copy(bf16[256,64,64]{0,2,1:T(8,128)(2,1)} %param.20) | data formatting | bytes 4194304 | tf_op args[9]
  88.6 2.2 %collective-permute-start.12 = (bf16[32,16,128]{2,1,0:T(8,128)(2,1)}, bf16[32,16,128]{2,1,0:T(8,128)(2,1)S(1)}, u32[]{:S(2)}, u32[]{:S(2)}) collective-permute-start(bf16[32,16,128]{2,1,0:T(8,128)(2,1)} %copy-done.30), channel_id=1, source_target_pairs={{0,20},{4,16},{8,28},{12,24},{16,4},{20,0},{24,12},{28,8},{32,52},... | collective-permute-start | bytes 393224 | tf_op jit(solution)/shard_map/ppermute | solution.py:389
  90.7 1.8 %collective-permute-start.13 = (bf16[32,16,128]{2,1,0:T(8,128)(2,1)}, bf16[32,16,128]{2,1,0:T(8,128)(2,1)S(1)}, u32[]{:S(2)}, u32[]{:S(2)}) collective-permute-start(bf16[32,16,128]{2,1,0:T(8,128)(2,1)} %copy-done.29), channel_id=1, source_target_pairs={{0,24},{4,28},{8,16},{12,20},{16,8},{20,12},{24,0},{28,4},{32,56},... | collective-permute-start | bytes 393224 | tf_op jit(solution)/shard_map/ppermute | solution.py:389
  92.5 3.8 %collective-permute-start.14 = (bf16[32,16,128]{2,1,0:T(8,128)(2,1)}, bf16[32,16,128]{2,1,0:T(8,128)(2,1)S(1)}, u32[]{:S(2)}, u32[]{:S(2)}) collective-permute-start(bf16[32,16,128]{2,1,0:T(8,128)(2,1)} %copy-done.28), channel_id=1, source_target_pairs={{0,28},{4,24},{8,20},{12,16},{16,12},{20,8},{24,4},{28,0},{32,60},... | collective-permute-start | bytes 393224 | tf_op jit(solution)/shard_map/ppermute | solution.py:389
  96.7 0.9 copy-done.7
  97.6 1.0 copy-done.23
  98.7 0.9 copy-done.25
  99.6 19.0 %near.1.near_ref = f32[16,8192]{1,0:T(8,128)S(1)} custom-call(s32[8,64]{1,0:T(8,128)S(1)} %bitcast.30, bf16[16,8192]{1,0:T(8,128)(2,1)S(1)} %copy-done.25, bf16[32,8192]{1,0:T(8,128)(2,1)S(1)} %copy-done.23, bf16[16,8192]{1,0:T(8,128)(2,1)S(1)} %copy-done.7, bf16[32,1024]{1,0:T(8,128)(2,1)} %collective-permute-done.21.left_ref, ...), custom_call_target="tpu_custom_call" | custom-call | flops 1073741824 | bytes 1048576 | tf_op jit(solution)/shard_map/near/pallas_call | solution.py:460
  118.6 0.8 pad_maximum_fusion.2.planes_ref
  119.5 3.2 %tree.1.local_ref = f32[32,16,128]{2,1,0:T(8,128)S(1)} custom-call(f32[32,16,128]{2,1,0:T(8,128)S(1)} %get-tuple-element.26.coeff_ref, f32[32,16,128]{2,1,0:T(8,128)S(1)} %copy-done.12, f32[3,16,64]{2,1,0:T(8,128)S(1)} %copy-done.21, f32[8,16,64]{2,1,0:T(8,128)S(1)} %pad_maximum_fusion.2.planes_ref, bf16[128,64,64]{2,1,0:T(8,128)(2,1)S(1)} %copy.12.move_ref, ...), custom_call_target="tpu_custom_call" | custom-call | flops 67108864 | bytes 1048576 | tf_op jit(solution)/shard_map/tree/pallas_call | solution.py:470
  122.8 7.7 %final.1 = f32[16,8192]{1,0:T(8,128)} custom-call(s32[2,256]{1,0:T(2,128)S(1)} %get-tuple-element.25.plan_ref, bf16[32,16,128]{2,1,0:T(8,128)(2,1)S(1)} %copy-done.18, bf16[32,16,128]{2,1,0:T(8,128)(2,1)S(1)} %collective-permute-done.8.r1, bf16[32,16,128]{2,1,0:T(8,128)(2,1)S(1)} %collective-permute-done.9.r2, ...), custom_call_target="tpu_custom_call" | custom-call | flops 134217728 | bytes 1048576 | tf_op jit(solution)/shard_map/final/pallas_call | solution.py:473
  (96 shorter events, 7.3 us)
Async XLA Ops:
  0.0 1.2 copy-start.2
  1.2 0.9 copy-start.5
  2.2 7.9 %copy-start.32 = (s32[256,2]{0,1:T(2,128)S(1)}, s32[256,2]{0,1:T(2,128)}, u32[]{:S(2)}) copy-start(s32[256,2]{0,1:T(2,128)} %param.19) | copy-start | bytes 6148
  2.2 7.9 %copy-start.33 = (s32[256,1]{0,1:T(1,128)S(1)}, s32[256,1]{0,1:T(1,128)}, u32[]{:S(2)}) copy-start(s32[256,1]{0,1:T(1,128)} %param.18) | copy-start | bytes 3076
  2.8 12.5 %collective-permute-start.3 = (bf16[32,16,128]{2,1,0:T(8,128)(2,1)S(1)}, bf16[32,16,128]{2,1,0:T(8,128)(2,1)}, u32[]{:S(2)}, u32[]{:S(2)}) collective-permute-start(bf16[32,16,128]{2,1,0:T(8,128)(2,1)S(1)} %get-tuple-element.29.b0), channel_id=1, source_target_pairs={{0,4},{4,0},{8,12},{12,8},{16,20},{20,16},{24,28},{28,24},{32,36},... | collective-permute-start | bytes 393224 | tf_op jit(solution)/shard_map/ppermute | solution.py:389
  10.1 18.8 %copy-start.4 = (bf16[64,64,64]{2,1,0:T(8,128)(2,1)S(1)}, bf16[64,64,64]{2,1,0:T(8,128)(2,1)}, u32[]{:S(2)}) copy-start(bf16[64,64,64]{2,1,0:T(8,128)(2,1)} %upper_t_ref.1) | copy-start | bytes 1572868
  11.9 17.0 %copy-start.11 = (f32[32,16,128]{2,1,0:T(8,128)}, f32[32,16,128]{2,1,0:T(8,128)S(1)}, u32[]{:S(2)}) copy-start(f32[32,16,128]{2,1,0:T(8,128)S(1)} %get-tuple-element.38.levels_ref) | copy-start | bytes 786436
  11.9 2.1 %collective-permute-start = (f32[1,24,128]{2,1,0:T(8,128)S(1)}, f32[1,24,128]{2,1,0:T(8,128)S(1)}, u32[]{:S(2)}, u32[]{:S(2)}) collective-permute-start(f32[1,24,128]{2,1,0:T(8,128)S(1)} %bitcast.21), channel_id=1, source_target_pairs={{0,4},{4,0},{8,12},{12,8},{16,20},{20,16},{24,28},{28,24},{32,36},... | collective-permute-start | bytes 36872 | tf_op jit(solution)/shard_map/ppermute | solution.py:389
  12.0 46.6 %collective-permute-start.18 = (f32[3,2048]{1,0:T(4,128)}, f32[3,2048]{1,0:T(4,128)}, u32[]{:S(2)}, u32[]{:S(2)}) collective-permute-start(f32[3,2048]{1,0:T(4,128)} %p0.1), channel_id=1, source_target_pairs={{1,0},{2,1},{3,2},{0,3},{5,4},{6,5},{7,6},{4,7},{9,8},{10,9},{11,1... | collective-permute-start | bytes 73736 | tf_op jit(solution)/shard_map/ppermute | solution.py:441
  13.0 48.3 %collective-permute-start.19 = (f32[3,2048]{1,0:T(4,128)}, f32[3,2048]{1,0:T(4,128)}, u32[]{:S(2)}, u32[]{:S(2)}) collective-permute-start(f32[3,2048]{1,0:T(4,128)} %p0.1), channel_id=1, source_target_pairs={{2,0},{3,1},{0,2},{1,3},{6,4},{7,5},{4,6},{5,7},{10,8},{11,9},{8,1... | collective-permute-start | bytes 73736 | tf_op jit(solution)/shard_map/ppermute | solution.py:441
  13.4 48.0 %collective-permute-start.20 = (f32[3,2048]{1,0:T(4,128)}, f32[3,2048]{1,0:T(4,128)}, u32[]{:S(2)}, u32[]{:S(2)}) collective-permute-start(f32[3,2048]{1,0:T(4,128)} %p0.1), channel_id=1, source_target_pairs={{3,0},{0,1},{1,2},{2,3},{7,4},{4,5},{5,6},{6,7},{11,8},{8,9},{9,10... | collective-permute-start | bytes 73736 | tf_op jit(solution)/shard_map/ppermute | solution.py:441
  14.1 8.4 %collective-permute-start.1 = (f32[2,24,128]{2,1,0:T(8,128)S(1)}, f32[2,24,128]{2,1,0:T(8,128)S(1)}, u32[]{:S(2)}, u32[]{:S(2)}) collective-permute-start(f32[2,24,128]{2,1,0:T(8,128)S(1)} %pad_maximum_fusion.5), channel_id=1, source_target_pairs={{0,8},{4,12},{8,0},{12,4},{16,24},{20,28},{24,16},{28,20},{32,40},... | collective-permute-start | bytes 73736 | tf_op jit(solution)/shard_map/ppermute | solution.py:389
  16.2 9.0 %collective-permute-start.4 = (bf16[64,16,128]{2,1,0:T(8,128)(2,1)S(1)}, bf16[64,16,128]{2,1,0:T(8,128)(2,1)S(1)}, u32[]{:S(2)}, u32[]{:S(2)}) collective-permute-start(bf16[64,16,128]{2,1,0:T(8,128)(2,1)S(1)} %pad_maximum_fusion), channel_id=1, source_target_pairs={{0,32},{4,228},{8,40},{12,236},{16,48},{20,244},{24,56},{28,252},{... | collective-permute-start | bytes 786440 | tf_op jit(solution)/shard_map/ppermute | solution.py:389
  22.5 6.4 %collective-permute-start.2 = (f32[4,24,128]{2,1,0:T(8,128)S(1)}, f32[4,24,128]{2,1,0:T(8,128)S(1)}, u32[]{:S(2)}, u32[]{:S(2)}) collective-permute-start(f32[4,24,128]{2,1,0:T(8,128)S(1)} %pad_maximum_fusion.3), channel_id=1, source_target_pairs={{0,16},{4,20},{8,24},{12,28},{16,0},{20,4},{24,8},{28,12},{32,48},... | collective-permute-start | bytes 147464 | tf_op jit(solution)/shard_map/ppermute | solution.py:389
  25.2 13.5 %copy-start.13 = (bf16[64,16,128]{2,1,0:T(8,128)(2,1)}, bf16[64,16,128]{2,1,0:T(8,128)(2,1)S(1)}, u32[]{:S(2)}) copy-start(bf16[64,16,128]{2,1,0:T(8,128)(2,1)S(1)} %collective-permute-done.4.b1) | copy-start | bytes 786436
  25.2 6.4 %collective-permute-start.5 = (bf16[64,16,128]{2,1,0:T(8,128)(2,1)S(1)}, bf16[64,16,128]{2,1,0:T(8,128)(2,1)S(1)}, u32[]{:S(2)}, u32[]{:S(2)}) collective-permute-start(bf16[64,16,128]{2,1,0:T(8,128)(2,1)S(1)} %collective-permute-done.4.b1), channel_id=1, source_target_pairs={{0,32},{4,228},{8,40},{12,236},{16,48},{20,244},{24,56},{28,252},{... | collective-permute-start | bytes 786440 | tf_op jit(solution)/shard_map/ppermute | solution.py:389
  29.9 5.4 %collective-permute-start.15 = (f32[1,16,64]{2,1,0:T(8,128)S(1)}, f32[1,16,64]{2,1,0:T(8,128)S(1)}, u32[]{:S(2)}, u32[]{:S(2)}) collective-permute-start(f32[1,16,64]{2,1,0:T(8,128)S(1)} %bitcast.26), channel_id=1, source_target_pairs={{0,32},{4,36},{8,40},{12,44},{16,48},{20,52},{24,56},{28,60},{32,0... | collective-permute-start | bytes 12296 | tf_op jit(solution)/shard_map/ppermute | solution.py:389
  31.6 10.9 %copy-start.15 = (bf16[64,16,128]{2,1,0:T(8,128)(2,1)}, bf16[64,16,128]{2,1,0:T(8,128)(2,1)S(1)}, u32[]{:S(2)}) copy-start(bf16[64,16,128]{2,1,0:T(8,128)(2,1)S(1)} %collective-permute-done.5.b2) | copy-start | bytes 786436
  31.6 6.4 %collective-permute-start.6 = (bf16[64,16,128]{2,1,0:T(8,128)(2,1)S(1)}, bf16[64,16,128]{2,1,0:T(8,128)(2,1)S(1)}, u32[]{:S(2)}, u32[]{:S(2)}) collective-permute-start(bf16[64,16,128]{2,1,0:T(8,128)(2,1)S(1)} %collective-permute-done.5.b2), channel_id=1, source_target_pairs={{0,32},{4,228},{8,40},{12,236},{16,48},{20,244},{24,56},{28,252},{... | collective-permute-start | bytes 786440 | tf_op jit(solution)/shard_map/ppermute | solution.py:389
  35.3 7.8 %copy-start.34 = (f32[1,16,64]{2,1,0:T(8,128)}, f32[1,16,64]{2,1,0:T(8,128)S(1)}, u32[]{:S(2)}) copy-start(f32[1,16,64]{2,1,0:T(8,128)S(1)} %collective-permute-done.15) | copy-start | bytes 12292
  36.0 35.4 %collective-permute-start.16 = (f32[2,16,64]{2,1,0:T(8,128)}, f32[2,16,64]{2,1,0:T(8,128)}, u32[]{:S(2)}, u32[]{:S(2)}) collective-permute-start(f32[2,16,64]{2,1,0:T(8,128)} %pad_maximum_fusion.6), channel_id=1, source_target_pairs={{0,64},{4,68},{8,72},{12,76},{16,80},{20,84},{24,88},{28,92},{32,9... | collective-permute-start | bytes 24584 | tf_op jit(solution)/shard_map/ppermute | solution.py:389
  39.4 5.4 %collective-permute-start.7 = (bf16[32,16,128]{2,1,0:T(8,128)(2,1)}, bf16[32,16,128]{2,1,0:T(8,128)(2,1)}, u32[]{:S(2)}, u32[]{:S(2)}) collective-permute-start(bf16[32,16,128]{2,1,0:T(8,128)(2,1)} %slice.44), channel_id=1, source_target_pairs={{0,32},{4,228},{8,40},{12,236},{16,48},{20,244},{24,56},{28,252},{... | collective-permute-start | bytes 393224 | tf_op jit(solution)/shard_map/ppermute | solution.py:389
  44.8 0.9 copy-start.10
  52.1 12.7 %copy-start.26 = (bf16[32,16,128]{2,1,0:T(8,128)(2,1)}, bf16[32,16,128]{2,1,0:T(8,128)(2,1)S(1)}, u32[]{:S(2)}) copy-start(bf16[32,16,128]{2,1,0:T(8,128)(2,1)S(1)} %get-tuple-element.32) | copy-start | bytes 393220
  52.1 14.2 %copy-start.27 = (bf16[32,16,128]{2,1,0:T(8,128)(2,1)}, bf16[32,16,128]{2,1,0:T(8,128)(2,1)S(1)}, u32[]{:S(2)}) copy-start(bf16[32,16,128]{2,1,0:T(8,128)(2,1)S(1)} %get-tuple-element.31) | copy-start | bytes 393220
  52.2 16.1 %copy-start.28 = (bf16[32,16,128]{2,1,0:T(8,128)(2,1)}, bf16[32,16,128]{2,1,0:T(8,128)(2,1)S(1)}, u32[]{:S(2)}) copy-start(bf16[32,16,128]{2,1,0:T(8,128)(2,1)S(1)} %get-tuple-element.37) | copy-start | bytes 393220
  52.2 44.2 %collective-permute-start.10 = (bf16[32,16,128]{2,1,0:T(8,128)(2,1)}, bf16[32,16,128]{2,1,0:T(8,128)(2,1)S(1)}, u32[]{:S(2)}, u32[]{:S(2)}) collective-permute-start(bf16[32,16,128]{2,1,0:T(8,128)(2,1)} %get-tuple-element.33), channel_id=1, source_target_pairs={{0,12},{4,8},{8,4},{12,0},{16,28},{20,24},{24,20},{28,16},{32,44},... | collective-permute-start | bytes 393224 | tf_op jit(solution)/shard_map/ppermute | solution.py:389
  58.6 37.7 %collective-permute-start.11 = (bf16[32,16,128]{2,1,0:T(8,128)(2,1)}, bf16[32,16,128]{2,1,0:T(8,128)(2,1)}, u32[]{:S(2)}, u32[]{:S(2)}) collective-permute-start(bf16[32,16,128]{2,1,0:T(8,128)(2,1)} %get-tuple-element.34), channel_id=1, source_target_pairs={{0,16},{4,20},{8,24},{12,28},{16,0},{20,4},{24,8},{28,12},{32,48},... | collective-permute-start | bytes 393224 | tf_op jit(solution)/shard_map/ppermute | solution.py:389
  61.3 1.0 copy-start.6
  66.4 22.2 %collective-permute-start.21 = (bf16[32,1024]{1,0:T(8,128)(2,1)}, bf16[32,1024]{1,0:T(8,128)(2,1)}, u32[]{:S(2)}, u32[]{:S(2)}) collective-permute-start(bf16[32,1024]{1,0:T(8,128)(2,1)} %get-tuple-element.43), channel_id=1, source_target_pairs={{0,4},{4,8},{8,12},{12,16},{16,20},{20,24},{24,28},{28,32},{32,36}... | collective-permute-start | bytes 196616 | tf_op jit(solution)/shard_map/ppermute | solution.py:457
  68.3 22.4 %collective-permute-start.22 = (bf16[32,1024]{1,0:T(8,128)(2,1)}, bf16[32,1024]{1,0:T(8,128)(2,1)}, u32[]{:S(2)}, u32[]{:S(2)}) collective-permute-start(bf16[32,1024]{1,0:T(8,128)(2,1)} %get-tuple-element.44), channel_id=1, source_target_pairs={{4,0},{8,4},{12,8},{16,12},{20,16},{24,20},{28,24},{32,28},{36,32}... | collective-permute-start | bytes 196616 | tf_op jit(solution)/shard_map/ppermute | solution.py:458
  72.7 19.8 %collective-permute-start.17 = (f32[4,16,64]{2,1,0:T(8,128)}, f32[4,16,64]{2,1,0:T(8,128)}, u32[]{:S(2)}, u32[]{:S(2)}) collective-permute-start(f32[4,16,64]{2,1,0:T(8,128)} %pad_maximum_fusion.4), channel_id=1, source_target_pairs={{0,128},{4,132},{8,136},{12,140},{16,144},{20,148},{24,152},{28,15... | collective-permute-start | bytes 49160 | tf_op jit(solution)/shard_map/ppermute | solution.py:389
  81.1 15.5 %copy-start.31 = (s32[64,8]{0,1:T(8,128)S(1)}, s32[64,8]{0,1:T(8,128)}, u32[]{:S(2)}) copy-start(s32[64,8]{0,1:T(8,128)} %param.21) | copy-start | bytes 6148
  88.6 30.8 %copy-start.1 = (bf16[128,64,64]{2,1,0:T(8,128)(2,1)S(1)}, bf16[128,64,64]{2,1,0:T(8,128)(2,1)}, u32[]{:S(2)}) copy-start(bf16[128,64,64]{2,1,0:T(8,128)(2,1)} %copy.14.pair_ref) | copy-start | bytes 3145732
  88.6 34.1 %collective-permute-start.12 = (bf16[32,16,128]{2,1,0:T(8,128)(2,1)}, bf16[32,16,128]{2,1,0:T(8,128)(2,1)S(1)}, u32[]{:S(2)}, u32[]{:S(2)}) collective-permute-start(bf16[32,16,128]{2,1,0:T(8,128)(2,1)} %copy-done.30), channel_id=1, source_target_pairs={{0,20},{4,16},{8,28},{12,24},{16,4},{20,0},{24,12},{28,8},{32,52},... | collective-permute-start | bytes 393224 | tf_op jit(solution)/shard_map/ppermute | solution.py:389
  90.7 32.0 %collective-permute-start.13 = (bf16[32,16,128]{2,1,0:T(8,128)(2,1)}, bf16[32,16,128]{2,1,0:T(8,128)(2,1)S(1)}, u32[]{:S(2)}, u32[]{:S(2)}) collective-permute-start(bf16[32,16,128]{2,1,0:T(8,128)(2,1)} %copy-done.29), channel_id=1, source_target_pairs={{0,24},{4,28},{8,16},{12,20},{16,8},{20,12},{24,0},{28,4},{32,56},... | collective-permute-start | bytes 393224 | tf_op jit(solution)/shard_map/ppermute | solution.py:389
  92.5 30.2 %collective-permute-start.14 = (bf16[32,16,128]{2,1,0:T(8,128)(2,1)}, bf16[32,16,128]{2,1,0:T(8,128)(2,1)S(1)}, u32[]{:S(2)}, u32[]{:S(2)}) collective-permute-start(bf16[32,16,128]{2,1,0:T(8,128)(2,1)} %copy-done.28), channel_id=1, source_target_pairs={{0,28},{4,24},{8,20},{12,16},{16,12},{20,8},{24,4},{28,0},{32,60},... | collective-permute-start | bytes 393224 | tf_op jit(solution)/shard_map/ppermute | solution.py:389
  96.3 26.4 %collective-permute-start.8 = (bf16[32,16,128]{2,1,0:T(8,128)(2,1)}, bf16[32,16,128]{2,1,0:T(8,128)(2,1)S(1)}, u32[]{:S(2)}, u32[]{:S(2)}) collective-permute-start(bf16[32,16,128]{2,1,0:T(8,128)(2,1)} %copy-done.27), channel_id=1, source_target_pairs={{0,4},{4,0},{8,12},{12,8},{16,20},{20,16},{24,28},{28,24},{32,36},... | collective-permute-start | bytes 393224 | tf_op jit(solution)/shard_map/ppermute | solution.py:389
  96.3 26.4 %collective-permute-start.9 = (bf16[32,16,128]{2,1,0:T(8,128)(2,1)}, bf16[32,16,128]{2,1,0:T(8,128)(2,1)S(1)}, u32[]{:S(2)}, u32[]{:S(2)}) collective-permute-start(bf16[32,16,128]{2,1,0:T(8,128)(2,1)} %copy-done.26), channel_id=1, source_target_pairs={{0,8},{4,12},{8,0},{12,4},{16,24},{20,28},{24,16},{28,20},{32,40},... | collective-permute-start | bytes 393224 | tf_op jit(solution)/shard_map/ppermute | solution.py:389
  96.7 1.0 copy-start.7
  97.6 1.0 copy-start.23
  99.6 19.0 %copy-start.35 = (f32[1,16,64]{2,1,0:T(8,128)S(1)}, f32[1,16,64]{2,1,0:T(8,128)}, u32[]{:S(2)}) copy-start(f32[1,16,64]{2,1,0:T(8,128)} %copy-done.34) | copy-start | bytes 12292
  99.6 19.8 %copy-start.8 = (bf16[64,64,64]{2,1,0:T(8,128)(2,1)S(1)}, bf16[64,64,64]{2,1,0:T(8,128)(2,1)}, u32[]{:S(2)}) copy-start(bf16[64,64,64]{2,1,0:T(8,128)(2,1)} %upper_c_ref.1) | copy-start | bytes 1572868
  99.6 19.8 %copy-start.12 = (f32[32,16,128]{2,1,0:T(8,128)S(1)}, f32[32,16,128]{2,1,0:T(8,128)}, u32[]{:S(2)}) copy-start(f32[32,16,128]{2,1,0:T(8,128)} %copy-done.11) | copy-start | bytes 786436
  99.6 19.8 %copy-start.21 = (f32[3,16,64]{2,1,0:T(8,128)S(1)}, f32[3,16,64]{2,1,0:T(8,128)}, u32[]{:S(2)}) copy-start(f32[3,16,64]{2,1,0:T(8,128)} %copy-done.20) | copy-start | bytes 36868
  119.4 3.3 %copy-start = (bf16[256,64,64]{2,1,0:T(8,128)(2,1)S(1)}, bf16[256,64,64]{2,1,0:T(8,128)(2,1)}, u32[]{:S(2)}) copy-start(bf16[256,64,64]{2,1,0:T(8,128)(2,1)} %copy.15.block_ref) | copy-start | bytes 6291460
  119.4 3.3 %copy-start.3 = (bf16[64,64,128]{2,1,0:T(8,128)(2,1)S(1)}, bf16[64,64,128]{2,1,0:T(8,128)(2,1)}, u32[]{:S(2)}) copy-start(bf16[64,64,128]{2,1,0:T(8,128)(2,1)} %basis_ref.3) | copy-start | bytes 3145732
  119.5 3.3 %copy-start.18 = (bf16[32,16,128]{2,1,0:T(8,128)(2,1)S(1)}, bf16[32,16,128]{2,1,0:T(8,128)(2,1)}, u32[]{:S(2)}) copy-start(bf16[32,16,128]{2,1,0:T(8,128)(2,1)} %copy-done.17) | copy-start | bytes 393220
  (11 other events, 8.4 us)

commit v2 on v1

v2 whole, which is shorter than its diff:
```python
import functools

import jax
import jax.numpy as jnp
from jax import lax
from jax.experimental import pallas as pl
from jax.experimental.layout import Layout, with_layout_constraint
from jax.experimental.pallas import tpu as pltpu
from jax.sharding import PartitionSpec as P

F32 = jnp.float32
BF16 = jnp.bfloat16
REACH = 8
KERNEL_SCALE = 1.0 / 64.0
DELTA_SQ = 0.0025

GROUP = 8
GROUP_BITS = 3

NEAR_PARTS = 2


def _spec(space=pltpu.VMEM):
    return pl.BlockSpec(memory_space=space)


def _call(body, outs, n_in, smem=(), scratch=(), flops=0, name=None, mib=8, hbm=()):
    return pl.pallas_call(
        body,
        out_shape=outs,
        in_specs=[
            _spec(pltpu.SMEM if i in smem else pltpu.HBM if i in hbm else pltpu.VMEM) for i in range(n_in)
        ],
        out_specs=jax.tree.map(lambda _: _spec(), outs),
        scratch_shapes=list(scratch),
        compiler_params=pltpu.CompilerParams(vmem_limit_bytes=mib * 1024 * 1024),
        cost_estimate=pl.CostEstimate(flops=flops, bytes_accessed=1 << 20, transcendentals=0),
        name=name,
    )


def _shape(shape, dtype):
    return jax.ShapeDtypeStruct(shape, dtype)


def _dot(a, b):
    return jnp.dot(a, b, preferred_element_type=F32)


def _dot_t(a, b):
    return lax.dot_general(a, b, (((1,), (1,)), ((), ())), preferred_element_type=F32)


def _leading(c):
    p = c * 65537.0
    return p - (p - c)


def _two(c):
    high = _leading(c)
    return jnp.concatenate([high, c - high], axis=0).astype(BF16)


def _mul(c, w):
    rows = c.shape[0]
    both = _dot(_two(c), w)
    return both[:rows] + both[rows:]


def _mul_t(c, w):
    rows = c.shape[0]
    both = _dot_t(_two(c), w)
    return both[:rows] + both[rows:]


def _swap_halves(x):
    half = x.shape[-1] // 2
    return jnp.concatenate([x[:, half:], x[:, :half]], axis=1)


def _pair(a, b):
    return jnp.concatenate([a, b], axis=1)


def _request(anchor_ref, leaves_ref, plan_ref):
    me = lax.axis_index("leaf")
    pairs = anchor_ref.shape[1]
    anchor = anchor_ref[...]
    source = leaves_ref[0:1, :]
    my_z = me // GROUP
    my_k = me % GROUP
    core = anchor & 1
    dz = ((anchor >> GROUP_BITS) - my_z) & 7
    near_side = (dz & 3) == 0
    server = jnp.where(near_side, core, jnp.where(dz > 4, 0, 1))
    step = jnp.where(dz > 4, 8 - dz, dz)
    base = jnp.where(
        dz == 0,
        0,
        jnp.where(dz == 4, 224, 32 + (step - 1) * 64 + (core ^ server) * 32),
    )
    tile = base + (source >> 1)
    group = (((anchor & 6) | server) ^ my_k)
    sub8 = lax.broadcasted_iota(jnp.int32, (8, pairs), 0)
    picked = (sub8 == group).astype(F32)
    row = lax.broadcasted_iota(jnp.int32, (pairs, pairs), 0)
    col = lax.broadcasted_iota(jnp.int32, (pairs, pairs), 1)
    upto = (row <= col).astype(F32).astype(BF16)
    count = _dot(picked.astype(BF16), upto)
    slot = (jnp.sum(picked * count, axis=0, keepdims=True) - 1.0).astype(jnp.int32)
    flip = (source ^ slot) & 1
    sub128 = lax.broadcasted_iota(jnp.int32, (128, pairs), 0)
    placed = (sub128 == slot).astype(F32).astype(BF16)
    table = _dot_t((picked * tile.astype(F32)).astype(BF16), placed)
    flips = _dot_t((picked * flip.astype(F32)).astype(BF16), placed)
    halves = jnp.floor((count[:, pairs - 1 : pairs] + 1.0) * 0.5)
    before = jnp.sum(jnp.where(sub8 < group, halves, 0.0), axis=0, keepdims=True)
    position = before.astype(jnp.int32) + (slot >> 1)
    even = (slot & 1) == 0
    number = lax.broadcasted_iota(jnp.int32, (1, pairs), 1)
    wanted = leaves_ref[1:2, :]

    def only(which, value):
        return jnp.where(which, value, 0).astype(F32)

    odd = jnp.logical_not(even)
    facts = jnp.concatenate(
        [
            only(even, group * 32 + (slot >> 1)),
            only(even, number),
            only(odd, number),
            only(even, wanted),
            only(odd, wanted),
            only(even, jnp.ones_like(slot)),
            only(odd, jnp.ones_like(slot)),
            jnp.zeros((1, pairs), F32),
        ],
        axis=0,
    )
    listed = (row == position).astype(F32).astype(BF16)
    plan = _dot_t(facts.astype(BF16), listed)
    plan_ref[0:3, :] = plan[0:3].astype(jnp.int32)
    plan_ref[3:4, :] = (plan[3:4] + 64.0 * (1.0 - plan[5:6])).astype(jnp.int32)
    plan_ref[4:5, :] = (plan[4:5] + 64.0 * (1.0 - plan[6:7])).astype(jnp.int32)
    total = jnp.sum(halves, axis=0, keepdims=True)
    plan_ref[5:8, :] = jnp.broadcast_to(total, (3, pairs)).astype(jnp.int32)
    return jnp.concatenate([table, flips], axis=0).astype(BF16)


LEAF_TILES = 32
OWN_TILES = LEAF_TILES + 1
TABLE_AT = OWN_TILES
EDGE_AT = TABLE_AT + 1
MATE_TILES = EDGE_AT + 2 * REACH


def _split_points(coords):
    c = coords - 0.5
    high = _leading(c)
    return high, _leading(c - high)


def _prepare_kernel(
    anchor_ref, leaves_ref, vec_ref, basis_ref, move_ref, p0, p1, p2, p3,
    own_ref, give_ref, edge_ref, coeff_ref, levels_ref, plan_ref,
):
    me = lax.axis_index("leaf")
    mine = lax.axis_index("vec")
    core = me & 1
    leaves = basis_ref.shape[0]
    lane = lax.broadcasted_iota(jnp.int32, (16, 128), 1)

    current = []
    for i in range(leaves // 2):
        x0 = vec_ref[:, 256 * i : 256 * i + 128]
        x1 = vec_ref[:, 256 * i + 128 : 256 * i + 256]
        w = basis_ref[2 * i : 2 * i + 2].reshape(128, 128)
        r = _dot_t(jnp.concatenate([x0, x1], axis=0), w)
        c = jnp.where(lane < 64, r[:16], r[16:])
        coeff_ref[i] = c
        own_ref[i] = c.astype(BF16)
        give_ref[i] = c.astype(BF16)
        current.append(c)

    size, node = leaves // 2, leaves
    while True:
        parents = [
            _mul(current[i], move_ref[node + 2 * i : node + 2 * i + 2].reshape(128, 64))
            for i in range(size)
        ]
        if size == 1:
            root = parents[0]
            break
        size //= 2
        node //= 2
        current = [_pair(parents[2 * i], parents[2 * i + 1]) for i in range(size)]
        for i in range(size):
            levels_ref[size + i] = current[i]
    levels_ref[0] = jnp.zeros((16, 128), F32)
    passed = _pair(_mul(root, move_ref[1]), root).astype(BF16)
    own_ref[LEAF_TILES] = passed
    give_ref[LEAF_TILES] = passed

    give_ref[TABLE_AT] = _request(anchor_ref, leaves_ref, plan_ref)

    width = p0.shape[1]
    halo = REACH * 128

    def end(last):
        block, lanes = (3, slice(width - halo, width)) if last else (0, slice(0, halo))
        chosen = p0[:, lanes]
        for turn, ref in ((1, p1), (2, p2), (3, p3)):
            chosen = jnp.where(((mine + turn) & 3) == block, ref[:, lanes], chosen)
        return chosen

    def place(ref, at, coords, first):
        high, mid = _split_points(coords)
        both = jnp.concatenate([high, mid, jnp.zeros((10, halo), F32)], axis=0).astype(BF16)
        for j in range(REACH):
            lanes = pl.ds(pl.multiple_of((first + j) * 128, 128), 128)
            ref[at + j] = vec_ref[:, lanes]
            ref[at + REACH + j] = both[:, 128 * j : 128 * j + 128]

    low, high = end(False), end(True)
    place(give_ref, EDGE_AT, jnp.where(core == 0, high, low), jnp.where(core == 0, leaves - REACH, 0))
    place(edge_ref, 0, jnp.where(core == 0, low, high), jnp.where(core == 0, 0, leaves - REACH))


def _inner_kernel(coeff_ref, levels_ref, move_ref, pair_ref, out_ref, couple_ref):
    lane = lax.broadcasted_iota(jnp.int32, (16, 128), 1)
    couple_ref[...] = pair_ref[1]
    parents = None
    size = 1
    while True:
        children = []
        for i in range(size):
            node = 2 * size + 2 * i
            tile = coeff_ref[i] if size == LEAF_TILES else levels_ref[size + i]
            other = _swap_halves(tile)
            both = _mul(
                jnp.concatenate(
                    [jnp.where(lane < 64, other, 0.0), jnp.where(lane < 64, 0.0, other)], axis=0
                ),
                pair_ref[node : node + 2].reshape(128, 64),
            )
            child = _pair(both[:16], both[16:])
            if parents is not None:
                child = child + _mul_t(parents[i], move_ref[node : node + 2].reshape(128, 64))
            children.append(child)
        if size == LEAF_TILES:
            break
        parents = []
        for c in children:
            parents += [c[:, :64], c[:, 64:]]
        size *= 2
    for i in range(LEAF_TILES):
        out_ref[i] = children[i]


def _from_root(root_local, move_ref):
    parents = [root_local]
    size = 1
    while True:
        children = [
            _mul_t(parents[i], move_ref[2 * size + 2 * i : 2 * size + 2 * i + 2].reshape(128, 64))
            for i in range(size)
        ]
        if size == LEAF_TILES:
            return children
        parents = []
        for c in children:
            parents += [c[:, :64], c[:, 64:]]
        size *= 2


def _root_local(mate_passed, got, move_ref, couple_ref, upper_t_ref, upper_c_ref, c5, c4, c3, c2, c1):
    me = lax.axis_index("leaf")
    my_k = me % GROUP
    my_z = me // GROUP
    my_x = my_k >> 1

    def chip(x, c, tile):
        return got[(2 * x + c) ^ my_k, tile].astype(F32)

    for x in range(4):
        c5[my_z * 4 + x] = chip(x, 0, 0)[:, 0:64]
        for c, sign in ((0, -1), (1, 1)):
            one, two = chip(x, c, 0), chip(x, c, 1)
            steps = [one[:, 64:128], two[:, 0:64], two[:, 64:128]]
            for i in range(3):
                c5[((my_z + sign * (i + 1)) & 7) * 4 + x] = steps[i]
        c5[((my_z + 4) & 7) * 4 + x] = chip(x, 0, 2)[:, 0:64] + chip(x, 1, 2)[:, 0:64]
    count = 32
    for below, above in ((c5, c4), (c4, c3), (c3, c2), (c2, c1)):
        for i in range(count // 2):
            node = count + 2 * i
            above[i] = _mul(
                _pair(below[2 * i], below[2 * i + 1]), upper_t_ref[node : node + 2].reshape(128, 64)
            )
        count //= 2
    place = my_z * 4 + my_x
    sibs = [
        mate_passed[:, 64:128].astype(F32),
        c5[place ^ 1],
        c4[(place >> 1) ^ 1],
        c3[(place >> 2) ^ 1],
        c2[(place >> 3) ^ 1],
        c1[(place >> 4) ^ 1],
    ]
    node = 64 + me
    coupled = [_mul(sibs[bit], upper_c_ref[node >> bit] if bit else couple_ref[...]) for bit in range(6)]
    local = coupled[5]
    for bit in range(4, -1, -1):
        local = _mul_t(local, upper_t_ref[node >> bit] if bit else move_ref[1]) + coupled[bit]
    return local


def _tree_kernel(
    pair_in, g0, g1, g2, g3, g4, g5, g6, g7, inner_ref, move_ref, couple_ref, upper_t_ref, upper_c_ref,
    out_ref, got, c5, c4, c3, c2, c1,
):
    for k, ref in enumerate((g0, g1, g2, g3, g4, g5, g6, g7)):
        got[k] = ref[LEAF_TILES : LEAF_TILES + 3]
    root_local = _root_local(
        pair_in[OWN_TILES + LEAF_TILES], got, move_ref, couple_ref, upper_t_ref, upper_c_ref, c5, c4, c3, c2, c1
    )
    down = _from_root(root_local, move_ref)
    for i in range(LEAF_TILES):
        out_ref[i] = inner_ref[i] + down[i]


def _both_ways(scratch, blocks):
    at = 0
    for ref, first in blocks:
        x = ref[first : first + LEAF_TILES]
        scratch[at : at + LEAF_TILES] = x
        y = _swap_halves(x.reshape(LEAF_TILES * 16, 128)).reshape(LEAF_TILES, 16, 128)
        scratch[256 + at : 256 + at + LEAF_TILES] = y
        at += LEAF_TILES


def _gather_kernel(table_ref, pair, r1, r2, r3, r4, *rest):
    outs, scratch = rest[:GROUP], rest[GROUP]
    blocks = [(pair, 0)]
    for ref in (r1, r2, r3):
        blocks += [(ref, 0), (ref, OWN_TILES)]
    _both_ways(scratch, blocks + [(r4, 0)])
    lane = lax.broadcasted_iota(jnp.int32, (16, 128), 1)

    def chip(ref):
        return (ref[LEAF_TILES].astype(F32) + ref[OWN_TILES + LEAF_TILES].astype(F32))[:, :64]

    passed = [
        _pair(chip(pair), chip(r1)).astype(BF16),
        _pair(chip(r2), chip(r3)).astype(BF16),
        r4[LEAF_TILES],
    ]
    for k in range(GROUP):
        for s in range(LEAF_TILES):
            a = scratch[table_ref[k, 2 * s]]
            b = scratch[table_ref[k, 2 * s + 1]]
            outs[k][s] = jnp.where(lane < 64, a, b)
        for i in range(3):
            outs[k][LEAF_TILES + i] = passed[i]


def _features(high, mid):
    width = high.shape[1]
    rounded = high + mid
    square = rounded * rounded
    norm = square[0:1] + square[1:2] + square[2:3]

    def thirds(n):
        n1 = _leading(n)
        n2 = _leading(n - n1)
        return [n1, n2, n - n1 - n2]

    one = jnp.ones((3, width), F32)
    zero = jnp.zeros((2, width), F32)
    pad = jnp.zeros((8, width), F32)
    own = [high, mid, zero]
    source = jnp.concatenate(own + own + thirds(norm + DELTA_SQ) + [one, zero, pad], axis=0)
    target = jnp.concatenate(
        [-2.0 * high, -2.0 * high, zero, -2.0 * mid, -2.0 * mid, zero, one] + thirds(norm) + [zero, pad],
        axis=0,
    )
    return source, target


TOGETHER = 8


def _near_kernel(
    part, parts, cols_ref, p0, p1, p2, p3, vec_ref, mate_ref, edge_ref, out_ref, rows, values, targets, kernel
):
    me = lax.axis_index("leaf")
    mine = lax.axis_index("vec")
    core = me & 1
    leaves = cols_ref.shape[1]
    near, count = cols_ref.shape[0], leaves // parts
    begin = part * count
    per = p0.shape[1] // 128

    beyond = jnp.where(core == 0, REACH + leaves, 0)
    for ref, first, at in ((mate_ref, EDGE_AT, beyond), (edge_ref, 0, REACH + leaves - beyond)):
        for j in range(REACH):
            both = ref[first + REACH + j].astype(F32)
            features = _features(both[0:3], both[3:6])[0]
            rows[at + j] = jnp.transpose(features).astype(BF16)
            values[at + j] = ref[first + j]
    for turn, ref in enumerate((p0, p1, p2, p3)):
        block = (mine + turn) & 3
        features, target = _features(*_split_points(ref[...]))
        for j in range(per):
            at = block * per + j
            rows[REACH + at] = jnp.transpose(features[:, 128 * j : 128 * j + 128]).astype(BF16)
            targets[at] = target[:, 128 * j : 128 * j + 128].astype(BF16)
    for i in range(leaves):
        values[REACH + i] = vec_ref[:, 128 * i : 128 * i + 128]

    shift = REACH - me * leaves

    def group(step, carry):
        for g in range(TOGETHER):
            t = begin + step * TOGETHER + g
            target = targets[t]
            for k in range(near):
                dist = _dot(rows[cols_ref[k, t] + shift], target)
                kernel[g, 128 * k : 128 * k + 128] = lax.rsqrt(dist).astype(BF16)
        for g in range(TOGETHER):
            t = begin + step * TOGETHER + g
            value = jnp.concatenate([values[cols_ref[k, t] + shift] for k in range(near)], axis=1)
            lanes = pl.ds(pl.multiple_of((step * TOGETHER + g) * 128, 128), 128)
            out_ref[:, lanes] = _dot(value, kernel[g]) * KERNEL_SCALE
        return carry

    lax.fori_loop(0, count // TOGETHER, group, 0)


BATCH = 8


def _final_kernel(plan_ref, r0, r1, r2, r3, r4, r5, r6, r7, block_ref, local_ref, basis_ref, *rest):
    nears, (out_ref, got, far) = rest[:NEAR_PARTS], rest[NEAR_PARTS:]
    for k, ref in enumerate((r0, r1, r2, r3, r4, r5, r6, r7)):
        got[32 * k : 32 * k + 32] = ref[0:LEAF_TILES]
    far[...] = jnp.zeros_like(far)
    lane = lax.broadcasted_iota(jnp.int32, (16, 128), 1)

    def split(x):
        zero = jnp.zeros_like(x)
        return jnp.concatenate([jnp.where(lane < 64, x, zero), jnp.where(lane < 64, zero, x)], axis=0)

    def add(step, carry):
        sums = []
        for i in range(BATCH):
            j = step * BATCH + i
            w = jnp.concatenate([block_ref[plan_ref[1, j]], block_ref[plan_ref[2, j]]], axis=0)
            sums.append(_dot(split(got[plan_ref[0, j]]), w))
        for i in range(BATCH):
            j = step * BATCH + i
            far[plan_ref[3, j]] += sums[i][:16]
            far[plan_ref[4, j]] += sums[i][16:]
        return carry

    lax.fori_loop(0, (plan_ref[5, 0] + BATCH - 1) // BATCH, add, 0)
    for i in range(basis_ref.shape[0] // 2):
        total = (local_ref[i] + _pair(far[2 * i], far[2 * i + 1])).astype(BF16)
        r = _dot(split(total), basis_ref[2 * i : 2 * i + 2].reshape(128, 128))
        at = 256 * i
        near_ref, off = nears[at // nears[0].shape[1]], at % nears[0].shape[1]
        out_ref[:, at : at + 128] = near_ref[:, off : off + 128] + r[:16]
        out_ref[:, at + 128 : at + 256] = near_ref[:, off + 128 : off + 256] + r[16:]


def per_device(
    vectors,
    points,
    leaf_basis,
    local_transfer,
    local_coupling,
    upper_transfer,
    upper_coupling,
    far_anchor,
    far_leaves,
    far_block,
    near_cols,
):
    n_leaf = lax.axis_size("leaf")
    n_vec = lax.axis_size("vec")
    everyone = range(n_leaf)

    def permute(x, to):
        return lax.ppermute(x, "leaf", [(i, to(i)) for i in everyone])

    def after(x, *done):
        return lax.optimization_barrier((x, done))[0]

    def tiles(count, dtype=BF16):
        return _shape((count, 16, 128), dtype)

    width = vectors.shape[1]
    leaves = leaf_basis.shape[0]

    turns = [points] + [
        lax.ppermute(points, "vec", [((i + s) % n_vec, i) for i in range(n_vec)]) for s in range(1, n_vec)
    ]

    own, give, edge, coeff, levels, plan = _call(
        _prepare_kernel,
        [
            tiles(OWN_TILES),
            tiles(MATE_TILES),
            tiles(2 * REACH),
            tiles(LEAF_TILES, F32),
            tiles(LEAF_TILES, F32),
            _shape((8, far_anchor.shape[0]), jnp.int32),
        ],
        9,
        flops=1 << 26,
        name="prepare",
    )(far_anchor.reshape(1, -1), far_leaves.T, vectors, leaf_basis, local_transfer, *turns)
    mate = permute(give, lambda i: i ^ 1)
    beyond = lax.ppermute(
        edge, "leaf", [(i, i - 1 + 2 * (i % 2)) for i in range(n_leaf) if 0 <= i - 1 + 2 * (i % 2) < n_leaf]
    )

    def onward(i):
        z, rest = i // GROUP, i % GROUP
        return (z + 1 if i % 2 == 0 else z - 1) % (n_leaf // GROUP) * GROUP + rest

    pair = jnp.concatenate([own, mate[:OWN_TILES]], axis=0)
    ring1 = permute(pair, onward)
    tables = jnp.concatenate([give[TABLE_AT : TABLE_AT + 1], mate[TABLE_AT : TABLE_AT + 1]], axis=0)
    for bit in range(1, GROUP_BITS):
        tables = jnp.concatenate([tables, permute(tables, lambda i: i ^ (1 << bit))], axis=0)
    wanted = jnp.stack([tables[k, k] + 256 * tables[k, 8 + k].astype(F32) for k in range(GROUP)])
    wanted = wanted.astype(jnp.int32)

    blocks = leaves + 2 * REACH

    def near_part(part, done):
        args = after((near_cols.T, *turns, vectors, mate, beyond), done)
        return _call(
            functools.partial(_near_kernel, part, NEAR_PARTS),
            _shape((vectors.shape[0], width // NEAR_PARTS), F32),
            8,
            smem=(0,),
            scratch=[
                pltpu.VMEM((blocks, 128, 32), BF16),
                pltpu.VMEM((blocks, 16, 128), BF16),
                pltpu.VMEM((leaves, 32, 128), BF16),
                pltpu.VMEM((TOGETHER, 1024, 128), BF16),
            ],
            flops=1 << 31,
            name="near%d" % part,
            mib=12,
        )(*args)

    def by_rows(x, done):
        return with_layout_constraint(after(x, done), Layout(major_to_minor=(0, 1, 2)))

    far_block = by_rows(far_block, pair)
    ring2 = permute(after(ring1, far_block), onward)
    local_coupling = by_rows(local_coupling, ring1)
    ring3 = permute(after(ring2, local_coupling), onward)
    near = [near_part(0, ring2)]
    ring4 = permute(after(ring3, near[0])[:OWN_TILES], onward)

    rows = _call(
        _gather_kernel,
        [tiles(LEAF_TILES + 3)] * GROUP,
        6,
        smem=(0,),
        scratch=[pltpu.VMEM((512, 16, 128), BF16)],
        flops=1 << 22,
        name="gather",
    )(wanted, pair, ring1, ring2, ring3, ring4)
    got = [rows[0]] + [permute(rows[k], lambda i, k=k: i ^ k) for k in range(1, GROUP)]

    near.append(near_part(1, rows[0]))
    inner, couple = _call(
        _inner_kernel,
        [tiles(LEAF_TILES, F32), _shape((64, 64), BF16)],
        4,
        flops=1 << 28,
        name="inner",
    )(*after((coeff, levels), rows[0]), local_transfer, local_coupling)

    local = _call(
        _tree_kernel,
        tiles(LEAF_TILES, F32),
        14,
        scratch=[pltpu.VMEM((GROUP, 3, 16, 128), BF16)] + [pltpu.VMEM((n, 16, 64), F32) for n in (32, 16, 8, 4, 2)],
        flops=1 << 26,
        name="tree",
    )(pair, *got, inner, local_transfer, couple, upper_transfer, upper_coupling)
    return _call(
        _final_kernel,
        _shape(vectors.shape, F32),
        12 + NEAR_PARTS,
        smem=(0,),
        scratch=[pltpu.VMEM((256, 16, 128), BF16), pltpu.VMEM((65, 16, 64), F32)],
        flops=1 << 27,
        name="final",
        mib=16,
    )(plan, *got, far_block, local, leaf_basis, *near)


def solution(mesh):
    return jax.shard_map(
        per_device,
        mesh=mesh,
        in_specs=(
            P("vec", "leaf"),
            P(None, ("leaf", "vec")),
            P("leaf", None, None),
            P("leaf", None, None),
            P("leaf", None, None),
            P(),
            P(),
            P("leaf", None),
            P("leaf", None),
            P("leaf", None, None),
            P("leaf", None),
        ),
        out_specs=P("vec", "leaf"),
        check_vma=False,
    )
```

time: 131 us -> 95.2 us (0.73)
  starting transfers between devices: 50 us -> 31.2 us
  Pallas kernels: 37.1 us -> 27.3 us
  local copies, waits for them, and re-layouts: 34.4 us -> 26.1 us
  other arithmetic: 3.69 us -> 6.85 us
  waiting for transfers between devices: 5.01 us -> 2.79 us
    ppermute x18 -> x14, starting transfers between devices: 43 us -> 22.3 us  [permute(): return lax.ppermute(x, 'leaf', [(i, to(i)) for i in everyone])]
    unnamed x75 -> x67, local copies, waits for them, and re-layouts: 30.7 us -> 11.8 us
    optimization_barrier x0 -> x2, local copies, waits for them, and re-layouts: none -> 12.2 us  [after(): return lax.optimization_barrier((x, done))[0]]
    pallas_call x9 -> x7, Pallas kernels: 37.1 us -> 27.3 us  [the longest x2 11.2 us: near_part(): _call(functools.partial(_near_kernel, part, NEAR_PARTS), _shape((vectors....]
    add x0 -> x4, other arithmetic: none -> 4.24 us  [per_device(): tables[k, k] + 256 * tables[k, 8 + k].astype(F32)]
    ppermute x3, starting transfers between devices: 2.09 us -> 5.89 us  [per_device(): lax.ppermute(points, 'vec', [((i + s) % n_vec, i) for i in range(n_vec)])]
    ppermute x18 -> x14, waiting for transfers between devices: 5 us -> 2.78 us  [permute(): return lax.ppermute(x, 'leaf', [(i, to(i)) for i in everyone])]
    ppermute x2 -> x1, starting transfers between devices: 4.92 us -> 3.01 us  [per_device(): lax.ppermute(edge, 'leaf', [(i, i - 1 + 2 * (i % 2)) for i in range(n_lea...]
  transfers between devices with their start and end apart: 23 -> 18, of which waited for: 4 -> 2; matrix products, arithmetic and copies ran while one was open for 18% -> 26% of each run, Pallas kernels for 22% -> 15%
where the time goes in v2:
time: 95.2 us; the launch traced here: 94.6 us
  starting transfers between devices  31.2 us (33%)
  Pallas kernels  27.3 us (29%)
  local copies, waits for them, and re-layouts  26.1 us (27%)
  other arithmetic  6.85 us (7%)
  waiting for transfers between devices  2.79 us (3%)
    ppermute x14, starting transfers between devices, permute(): return lax.ppermute(x, 'leaf', [(i, to(i)) for i in everyone])  22.3 us
    optimization_barrier x2, local copies, waits for them, and re-layouts, after(): return lax.optimization_barrier((x, done))[0]  12.2 us
    unnamed x67, local copies, waits for them, and re-layouts  11.8 us
    pallas_call x2, Pallas kernels, near_part(): _call(functools.partial(_near_kernel, part, NEAR_PARTS), _shape((vectors....  11.2 us
    ppermute x3, starting transfers between devices, per_device(): lax.ppermute(points, 'vec', [((i + s) % n_vec, i) for i in range(n_vec)])  5.89 us
    pallas_call x1, Pallas kernels, per_device(): _call(_final_kernel, _shape(vectors.shape, F32), 12 + NEAR_PARTS, smem=(0...  5.47 us
    add x4, other arithmetic, per_device(): tables[k, k] + 256 * tables[k, 8 + k].astype(F32)  4.24 us
    pallas_call x1, Pallas kernels, per_device(): _call(_tree_kernel, tiles(LEAF_TILES, F32), 14, scratch=[pltpu.VMEM((GROU...  3.23 us
  transfers between devices with their start and end apart: 18, of which 2 were waited for; matrix products, arithmetic and copies ran while one was open for 26% of the time, Pallas kernels for 15%

profile of v2, /device:TPU:1, one launch (start us, length us, event | category | flops | bytes accessed | tf_op | source)
XLA Modules:
  0.0 94.6 jit_solution(2729010818947314819)
XLA Ops:
  0.0 2.2 %collective-permute-start.2 = (f32[3,2048]{1,0:T(4,128)}, f32[3,2048]{1,0:T(4,128)S(1)}, u32[]{:S(2)}, u32[]{:S(2)}) collective-permute-start(f32[3,2048]{1,0:T(4,128)} %p0.3), channel_id=1, source_target_pairs={{3,0},{0,1},{1,2},{2,3},{7,4},{4,5},{5,6},{6,7},{11,8},{8,9},{9,10... | collective-permute-start | bytes 73736 | tf_op jit(solution)/shard_map/ppermute | solution.py:506
  2.2 2.6 %collective-permute-start.1 = (f32[3,2048]{1,0:T(4,128)}, f32[3,2048]{1,0:T(4,128)S(1)}, u32[]{:S(2)}, u32[]{:S(2)}) collective-permute-start(f32[3,2048]{1,0:T(4,128)} %p0.3), channel_id=1, source_target_pairs={{2,0},{3,1},{0,2},{1,3},{6,4},{7,5},{4,6},{5,7},{10,8},{11,9},{8,1... | collective-permute-start | bytes 73736 | tf_op jit(solution)/shard_map/ppermute | solution.py:506
  4.9 1.1 %collective-permute-start = (f32[3,2048]{1,0:T(4,128)}, f32[3,2048]{1,0:T(4,128)S(1)}, u32[]{:S(2)}, u32[]{:S(2)}) collective-permute-start(f32[3,2048]{1,0:T(4,128)} %p0.3), channel_id=1, source_target_pairs={{1,0},{2,1},{3,2},{0,3},{5,4},{6,5},{7,6},{4,7},{9,8},{10,9},{11,1... | collective-permute-start | bytes 73736 | tf_op jit(solution)/shard_map/ppermute | solution.py:506
  5.9 3.9 %copy.12.move_ref = bf16[128,64,64]{2,1,0:T(8,128)(2,1)S(1)} copy(bf16[128,64,64]{0,2,1:T(8,128)(2,1)} %param.14) | data formatting | bytes 2097152 | tf_op args[3]
  10.0 2.5 %prepare.1 = (bf16[33,16,128]{2,1,0:T(8,128)(2,1)S(1)}, bf16[50,16,128]{2,1,0:T(8,128)(2,1)S(1)}, bf16[16,16,128]{2,1,0:T(8,128)(2,1)}, f32[32,16,128]{2,1,0:T(8...) custom-call(s32[1,256]{1,0:T(1,128)S(1)} %bitcast.20, s32[2,256]{1,0:T(2,128)S(1)} %bitcast.19, ...), custom_call_target="tpu_custom_call" | custom-call | flops 67108864 | bytes 1048576 | tf_op jit(solution)/shard_map/prepare/pallas_call | solution.py:509
  12.5 0.7 copy-done.12
  13.2 1.5 %collective-permute-start.3 = (bf16[50,16,128]{2,1,0:T(8,128)(2,1)S(1)}, bf16[50,16,128]{2,1,0:T(8,128)(2,1)S(1)}, u32[]{:S(2)}, u32[]{:S(2)}) collective-permute-start(bf16[50,16,128]{2,1,0:T(8,128)(2,1)S(1)} %get-tuple-element.45), channel_id=1, source_target_pairs={{0,4},{4,0},{8,12},{12,8},{16,20},{20,16},{24,28},{28,24},{32,36},... | collective-permute-start | bytes 614408 | tf_op jit(solution)/shard_map/ppermute | solution.py:494
  14.7 3.0 %collective-permute-start.9 = (bf16[16,16,128]{2,1,0:T(8,128)(2,1)}, bf16[16,16,128]{2,1,0:T(8,128)(2,1)}, u32[]{:S(2)}, u32[]{:S(2)}) collective-permute-start(bf16[16,16,128]{2,1,0:T(8,128)(2,1)} %get-tuple-element.51), channel_id=1, source_target_pairs={{4,8},{8,4},{12,16},{16,12},{20,24},{24,20},{28,32},{32,28},{36,40... | collective-permute-start | bytes 196616 | tf_op jit(solution)/shard_map/ppermute | solution.py:524
  17.8 5.7 %collective-permute-start.6 = (bf16[66,16,128]{2,1,0:T(8,128)(2,1)S(1)}, bf16[66,16,128]{2,1,0:T(8,128)(2,1)}, u32[]{:S(2)}, u32[]{:S(2)}) collective-permute-start(bf16[66,16,128]{2,1,0:T(8,128)(2,1)S(1)} %pad_maximum_fusion.pair.pair_in), channel_id=1, source_target_pairs={{0,32},{4,228},{8,40},{12,236},{16,48},{20,244},{24,56},{28,252},{... | collective-permute-start | bytes 811016 | tf_op jit(solution)/shard_map/ppermute | solution.py:494
  23.5 0.5 add_bitcast_fusion
  24.0 0.6 pad_maximum_fusion.2
  24.6 1.2 %collective-permute-start.4 = (bf16[2,16,128]{2,1,0:T(8,128)(2,1)}, bf16[2,16,128]{2,1,0:T(8,128)(2,1)}, u32[]{:S(2)}, u32[]{:S(2)}) collective-permute-start(bf16[2,16,128]{2,1,0:T(8,128)(2,1)} %pad_maximum_fusion.2), channel_id=1, source_target_pairs={{0,8},{4,12},{8,0},{12,4},{16,24},{20,28},{24,16},{28,20},{32,40},... | collective-permute-start | bytes 24584 | tf_op jit(solution)/shard_map/ppermute | solution.py:494
  25.9 7.4 %copy.13.block_ref = bf16[256,64,64]{2,1,0:T(8,128)(2,1)} copy(bf16[256,64,64]{0,2,1:T(8,128)(2,1)} %param.20) | data formatting | bytes 4194304 | tf_op jit(solution)/shard_map/optimization_barrier | solution.py:497
  33.3 0.7 collective-permute-start.7
  34.0 1.2 %fusion.14 = f32[1,128]{1,0:T(1,128)} fusion(bf16[50,16,128]{2,1,0:T(8,128)(2,1)} %copy-done.16), kind=kLoop, calls=%fused_computation.32 | loop fusion | flops 512 | bytes 1024 | tf_op jit(solution)/shard_map/add | solution.py:537
  35.2 1.3 %pad_maximum_fusion.1 = bf16[4,16,128]{2,1,0:T(8,128)(2,1)} fusion(bf16[2,16,128]{2,1,0:T(8,128)(2,1)} %collective-permute-done.4, bf16[1,16,128]{2,1,0:T(8,128)(2,1)} %copy-done.32, bf16[1,16,128]{2,1,0:T(8,128)(2,1)S(1)} %slice.68), kind=kLoop, calls=%fused_computation.1 | loop fusion | flops 16384 | bytes 32768 | tf_op jit(solution)/shard_map/concatenate | solution.py:536
  36.5 1.9 %collective-permute-start.5 = (bf16[4,16,128]{2,1,0:T(8,128)(2,1)}, bf16[4,16,128]{2,1,0:T(8,128)(2,1)}, u32[]{:S(2)}, u32[]{:S(2)}) collective-permute-start(bf16[4,16,128]{2,1,0:T(8,128)(2,1)} %pad_maximum_fusion.1), channel_id=1, source_target_pairs={{0,16},{4,20},{8,24},{12,28},{16,0},{20,4},{24,8},{28,12},{32,48},... | collective-permute-start | bytes 49160 | tf_op jit(solution)/shard_map/ppermute | solution.py:494
  38.4 4.8 %copy.14.pair_ref = bf16[128,64,64]{2,1,0:T(8,128)(2,1)} copy(bf16[128,64,64]{0,2,1:T(8,128)(2,1)} %param.15) | data formatting | bytes 2097152 | tf_op jit(solution)/shard_map/optimization_barrier | solution.py:497
  43.2 0.7 collective-permute-start.8
  43.9 1.2 %fusion.16 = (f32[1,128]{1,0:T(1,128)}, f32[1,128]{1,0:T(1,128)}) fusion(bf16[2,16,128]{2,1,0:T(8,128)(2,1)} %collective-permute-done.4), kind=kLoop, calls=%fused_computation.34 | loop fusion | flops 1024 | bytes 2048 | tf_op jit(solution)/shard_map/add | solution.py:537
  45.2 0.9 copy-done.8
  46.1 0.9 copy-done.17
  47.0 5.6 %near0.1.rest_0_ = f32[16,4096]{1,0:T(8,128)S(1)} custom-call(s32[8,64]{1,0:T(8,128)S(1)} %bitcast.21, f32[3,2048]{1,0:T(4,128)S(1)} %copy-done.19, f32[3,2048]{1,0:T(4,128)S(1)} %collective-permute-done.p1, f32[3,2048]{1,0:T(4,128)S(1)} %collective-permute-done.1.p2, f32[3,2048]{1,0:T(4,128)S(1)} %collective-permute-done.2.p3, ...), custom_call_target="tpu_custom_call" | custom-call | flops 2147483648 | bytes 1048576 | tf_op jit(solution)/shard_map/near0/pallas_call | solution.py:544
  52.7 0.7 slice.83
  53.4 0.0 copy-done.14
  53.5 0.7 copy-done.5
  54.2 0.7 collective-permute-start.10
  54.9 1.3 %fusion.20 = (f32[1,128]{1,0:T(1,128)}, f32[1,128]{1,0:T(1,128)}, f32[1,128]{1,0:T(1,128)}, f32[1,128]{1,0:T(1,128)}) fusion(bf16[4,16,128]{2,1,0:T(8,128)(2,1)} %collective-permute-done.5), kind=kLoop, calls=%fused_computation.38 | loop fusion | flops 2048 | bytes 4096 | tf_op jit(solution)/shard_map/add | solution.py:537
  56.2 1.3 %stack.2 = f32[8,128]{1,0:T(8,128)} concatenate(f32[1,128]{1,0:T(1,128)} %add_bitcast_fusion, f32[1,128]{1,0:T(1,128)} %fusion.14, f32[1,128]{1,0:T(1,128)} %get-tuple-element.88, f32[1,128]{1,0:T(1,128)} %get-tuple-element.87, f32[1,128]{1,0:T(1,128)} %get-tuple-element.86, f32[1,128]{1,0:T(1,128)} %get-tuple-element.84, f32[1,128]{1,0:T(1,128)} %get-tuple-element.85, ...), dimensions={0} | concatenate | bytes 8192 | tf_op jit(solution)/shard_map/stack | solution.py:537
  57.5 0.7 convert_element_type.195.table_ref
  58.2 0.3 collective-permute-done.10.r4
  58.5 1.0 %copy-done.6 = bf16[66,16,128]{2,1,0:T(8,128)(2,1)S(1)} copy-done((bf16[66,16,128]{2,1,0:T(8,128)(2,1)S(1)}, bf16[66,16,128]{2,1,0:T(8,128)(2,1)}, u32[]{:S(2)}) %copy-start.6) | copy-done | bytes 270360
  59.5 2.0 %gather.1 = (bf16[35,16,128]{2,1,0:T(8,128)(2,1)S(1)}, bf16[35,16,128]{2,1,0:T(8,128)(2,1)S(1)}, bf16[35,16,128]{2,1,0:T(8,128)(2,1)S(1)}, bf16[35,16,128]{2,1,0...) custom-call(s32[8,128]{1,0:T(8,128)S(1)} %convert_element_type.195.t, ...), custom_call_target="tpu_custom_call" | custom-call | flops 4194304 | bytes 1048576 | tf_op jit(solution)/shard_map/gather/pallas_call | solution.py:570
  61.5 1.8 %collective-permute-start.11 = (bf16[35,16,128]{2,1,0:T(8,128)(2,1)S(1)}, bf16[35,16,128]{2,1,0:T(8,128)(2,1)S(1)}, u32[]{:S(2)}, u32[]{:S(2)}) collective-permute-start(bf16[35,16,128]{2,1,0:T(8,128)(2,1)S(1)} %get-tuple-element.62), channel_id=1, source_target_pairs={{0,4},{4,0},{8,12},{12,8},{16,20},{20,16},{24,28},{28,24},{32,36},... | collective-permute-start | bytes 430088 | tf_op jit(solution)/shard_map/ppermute | solution.py:494
  63.3 1.7 %collective-permute-start.13 = (bf16[35,16,128]{2,1,0:T(8,128)(2,1)S(1)}, bf16[35,16,128]{2,1,0:T(8,128)(2,1)S(1)}, u32[]{:S(2)}, u32[]{:S(2)}) collective-permute-start(bf16[35,16,128]{2,1,0:T(8,128)(2,1)S(1)} %get-tuple-element.64), channel_id=1, source_target_pairs={{0,12},{4,8},{8,4},{12,0},{16,28},{20,24},{24,20},{28,16},{32,44},... | collective-permute-start | bytes 430088 | tf_op jit(solution)/shard_map/ppermute | solution.py:494
  65.1 1.2 %collective-permute-start.14 = (bf16[35,16,128]{2,1,0:T(8,128)(2,1)S(1)}, bf16[35,16,128]{2,1,0:T(8,128)(2,1)S(1)}, u32[]{:S(2)}, u32[]{:S(2)}) collective-permute-start(bf16[35,16,128]{2,1,0:T(8,128)(2,1)S(1)} %get-tuple-element.65), channel_id=1, source_target_pairs={{0,16},{4,20},{8,24},{12,28},{16,0},{20,4},{24,8},{28,12},{32,48},... | collective-permute-start | bytes 430088 | tf_op jit(solution)/shard_map/ppermute | solution.py:494
  66.3 2.1 %collective-permute-start.15 = (bf16[35,16,128]{2,1,0:T(8,128)(2,1)S(1)}, bf16[35,16,128]{2,1,0:T(8,128)(2,1)S(1)}, u32[]{:S(2)}, u32[]{:S(2)}) collective-permute-start(bf16[35,16,128]{2,1,0:T(8,128)(2,1)S(1)} %get-tuple-element.66), channel_id=1, source_target_pairs={{0,20},{4,16},{8,28},{12,24},{16,4},{20,0},{24,12},{28,8},{32,52},... | collective-permute-start | bytes 430088 | tf_op jit(solution)/shard_map/ppermute | solution.py:494
  68.4 1.6 %copy-done.1 = bf16[128,64,64]{2,1,0:T(8,128)(2,1)S(1)} copy-done((bf16[128,64,64]{2,1,0:T(8,128)(2,1)S(1)}, bf16[128,64,64]{2,1,0:T(8,128)(2,1)}, u32[]{:S(2)}) %copy-start.1) | copy-done | bytes 1048600
  70.0 0.9 %copy-done.11 = f32[32,16,128]{2,1,0:T(8,128)S(1)} copy-done((f32[32,16,128]{2,1,0:T(8,128)S(1)}, f32[32,16,128]{2,1,0:T(8,128)}, u32[]{:S(2)}) %copy-start.11) | copy-done | bytes 262168
  70.9 0.9 %copy-done.13 = f32[32,16,128]{2,1,0:T(8,128)S(1)} copy-done((f32[32,16,128]{2,1,0:T(8,128)S(1)}, f32[32,16,128]{2,1,0:T(8,128)}, u32[]{:S(2)}) %copy-start.13) | copy-done | bytes 262168
  71.9 2.8 %inner.1 = (f32[32,16,128]{2,1,0:T(8,128)S(1)}, bf16[64,64]{1,0:T(8,128)(2,1)S(1)}) custom-call(f32[32,16,128]{2,1,0:T(8,128)S(1)} %copy-done.11, f32[32,16,128]{2,1,0:T(8,128)S(1)} %copy-done.13, bf16[128,64,64]{2,1,0:T(8,128)(2,1)S(1)} %copy.12.move_ref, bf16[128,64,64]{2,1,0:T(8,128)(2,1)S(1)} %copy-done.1), custom_call_target="tpu_custom_call" | custom-call | flops 268435456 | bytes 1048576 | tf_op jit(solution)/shard_map/inner/pallas_call | solution.py:582
  74.7 1.8 %collective-permute-start.16 = (bf16[35,16,128]{2,1,0:T(8,128)(2,1)S(1)}, bf16[35,16,128]{2,1,0:T(8,128)(2,1)S(1)}, u32[]{:S(2)}, u32[]{:S(2)}) collective-permute-start(bf16[35,16,128]{2,1,0:T(8,128)(2,1)S(1)} %get-tuple-element.67), channel_id=1, source_target_pairs={{0,24},{4,28},{8,16},{12,20},{16,8},{20,12},{24,0},{28,4},{32,56},... | collective-permute-start | bytes 430088 | tf_op jit(solution)/shard_map/ppermute | solution.py:494
  76.5 1.2 %collective-permute-start.17 = (bf16[35,16,128]{2,1,0:T(8,128)(2,1)S(1)}, bf16[35,16,128]{2,1,0:T(8,128)(2,1)S(1)}, u32[]{:S(2)}, u32[]{:S(2)}) collective-permute-start(bf16[35,16,128]{2,1,0:T(8,128)(2,1)S(1)} %get-tuple-element.68), channel_id=1, source_target_pairs={{0,28},{4,24},{8,20},{12,16},{16,12},{20,8},{24,4},{28,0},{32,60},... | collective-permute-start | bytes 430088 | tf_op jit(solution)/shard_map/ppermute | solution.py:494
  77.8 5.6 %near1.1.rest_1_ = f32[16,4096]{1,0:T(8,128)S(1)} custom-call(s32[8,64]{1,0:T(8,128)S(1)} %bitcast.22, f32[3,2048]{1,0:T(4,128)S(1)} %copy-done.20, f32[3,2048]{1,0:T(4,128)S(1)} %copy-done.26, f32[3,2048]{1,0:T(4,128)S(1)} %copy-done.24, f32[3,2048]{1,0:T(4,128)S(1)} %copy-done.22, bf16[16,8192]{1,0:T(8,128)(2,1)S(1)} %copy-done.9, ...), custom_call_target="tpu_custom_call" | custom-call | flops 2147483648 | bytes 1048576 | tf_op jit(solution)/shard_map/near1/pallas_call | solution.py:544
  83.4 2.4 %collective-permute-done.17.g7.r7 = bf16[35,16,128]{2,1,0:T(8,128)(2,1)S(1)} collective-permute-done((bf16[35,16,128]{2,1,0:T(8,128)(2,1)S(1)}, bf16[35,16,128]{2,1,0:T(8,128)(2,1)S(1)}, u32[]{:S(2)}, u32[]{:S(2)}) %collective-permute-start.17) | collective-permute-done | bytes 143392 | tf_op jit(solution)/shard_map/ppermute | solution.py:494
  85.9 3.2 %tree.1.local_ref = f32[32,16,128]{2,1,0:T(8,128)S(1)} custom-call(bf16[66,16,128]{2,1,0:T(8,128)(2,1)S(1)} %pad_maximum_fusion.pair.pair_in, bf16[35,16,128]{2,1,0:T(8,128)(2,1)S(1)} %get-tuple-element.61.g0.r0, bf16[35,16,128]{2,1,0:T(8,128)(2,1)S(1)} %collective-permute-done.11.g1.r1, bf16[35,16,128]{2,1,0:T(8,128)(2,1)S(1)} %collective-permute-done.12.g2.r2, ...), custom_call_target="tpu_custom_call" | custom-call | flops 67108864 | bytes 1048576 | tf_op jit(solution)/shard_map/tree/pallas_call | solution.py:590
  89.1 0.0 copy-done.28
  89.1 5.5 %final.1 = f32[16,8192]{1,0:T(8,128)} custom-call(s32[8,256]{1,0:T(8,128)S(1)} %copy-done.28, bf16[35,16,128]{2,1,0:T(8,128)(2,1)S(1)} %get-tuple-element.61.g0.r0, bf16[35,16,128]{2,1,0:T(8,128)(2,1)S(1)} %collective-permute-done.11.g1.r1, bf16[35,16,128]{2,1,0:T(8,128)(2,1)S(1)} %collective-permute-done.12.g2.r2, ...), custom_call_target="tpu_custom_call" | custom-call | flops 134217728 | bytes 1048576 | tf_op jit(solution)/shard_map/final/pallas_call | solution.py:598
  (77 shorter events, 0.2 us)
Async XLA Ops:
  0.0 9.9 %copy-start.19 = (f32[3,2048]{1,0:T(4,128)S(1)}, f32[3,2048]{1,0:T(4,128)}, u32[]{:S(2)}) copy-start(f32[3,2048]{1,0:T(4,128)} %p0.3) | copy-start | bytes 73732
  0.0 9.9 %copy-start.7 = (bf16[16,8192]{1,0:T(8,128)(2,1)S(1)}, bf16[16,8192]{1,0:T(8,128)(2,1)}, u32[]{:S(2)}) copy-start(bf16[16,8192]{1,0:T(8,128)(2,1)} %vec_ref.3) | copy-start | bytes 786436
  0.0 9.9 %copy-start.2 = (bf16[64,64,128]{2,1,0:T(8,128)(2,1)S(1)}, bf16[64,64,128]{2,1,0:T(8,128)(2,1)}, u32[]{:S(2)}) copy-start(bf16[64,64,128]{2,1,0:T(8,128)(2,1)} %basis_ref.3) | copy-start | bytes 3145732
  0.0 10.0 %copy-start.29 = (s32[256,2]{0,1:T(2,128)S(1)}, s32[256,2]{0,1:T(2,128)}, u32[]{:S(2)}) copy-start(s32[256,2]{0,1:T(2,128)} %param.19) | copy-start | bytes 6148
  0.0 10.0 %copy-start.30 = (s32[256,1]{0,1:T(1,128)S(1)}, s32[256,1]{0,1:T(1,128)}, u32[]{:S(2)}) copy-start(s32[256,1]{0,1:T(1,128)} %param.18) | copy-start | bytes 3076
  0.0 9.8 %collective-permute-start.2 = (f32[3,2048]{1,0:T(4,128)}, f32[3,2048]{1,0:T(4,128)S(1)}, u32[]{:S(2)}, u32[]{:S(2)}) collective-permute-start(f32[3,2048]{1,0:T(4,128)} %p0.3), channel_id=1, source_target_pairs={{3,0},{0,1},{1,2},{2,3},{7,4},{4,5},{5,6},{6,7},{11,8},{8,9},{9,10... | collective-permute-start | bytes 73736 | tf_op jit(solution)/shard_map/ppermute | solution.py:506
  2.2 7.7 %collective-permute-start.1 = (f32[3,2048]{1,0:T(4,128)}, f32[3,2048]{1,0:T(4,128)S(1)}, u32[]{:S(2)}, u32[]{:S(2)}) collective-permute-start(f32[3,2048]{1,0:T(4,128)} %p0.3), channel_id=1, source_target_pairs={{2,0},{3,1},{0,2},{1,3},{6,4},{7,5},{4,6},{5,7},{10,8},{11,9},{8,1... | collective-permute-start | bytes 73736 | tf_op jit(solution)/shard_map/ppermute | solution.py:506
  4.9 5.1 %collective-permute-start = (f32[3,2048]{1,0:T(4,128)}, f32[3,2048]{1,0:T(4,128)S(1)}, u32[]{:S(2)}, u32[]{:S(2)}) collective-permute-start(f32[3,2048]{1,0:T(4,128)} %p0.3), channel_id=1, source_target_pairs={{1,0},{2,1},{3,2},{0,3},{5,4},{6,5},{7,6},{4,7},{9,8},{10,9},{11,1... | collective-permute-start | bytes 73736 | tf_op jit(solution)/shard_map/ppermute | solution.py:506
  9.9 35.2 %copy-start.21 = (f32[3,2048]{1,0:T(4,128)}, f32[3,2048]{1,0:T(4,128)S(1)}, u32[]{:S(2)}) copy-start(f32[3,2048]{1,0:T(4,128)S(1)} %collective-permute-done.2.p3) | copy-start | bytes 73732
  9.9 35.2 %copy-start.23 = (f32[3,2048]{1,0:T(4,128)}, f32[3,2048]{1,0:T(4,128)S(1)}, u32[]{:S(2)}) copy-start(f32[3,2048]{1,0:T(4,128)S(1)} %collective-permute-done.1.p2) | copy-start | bytes 73732
  9.9 35.2 %copy-start.25 = (f32[3,2048]{1,0:T(4,128)}, f32[3,2048]{1,0:T(4,128)S(1)}, u32[]{:S(2)}) copy-start(f32[3,2048]{1,0:T(4,128)S(1)} %collective-permute-done.p1) | copy-start | bytes 73732
  13.2 4.6 %copy-start.10 = (f32[32,16,128]{2,1,0:T(8,128)}, f32[32,16,128]{2,1,0:T(8,128)S(1)}, u32[]{:S(2)}) copy-start(f32[32,16,128]{2,1,0:T(8,128)S(1)} %get-tuple-element.71.coeff_ref) | copy-start | bytes 786436
  13.2 4.6 %copy-start.27 = (s32[8,256]{1,0:T(8,128)}, s32[8,256]{1,0:T(8,128)S(1)}, u32[]{:S(2)}) copy-start(s32[8,256]{1,0:T(8,128)S(1)} %get-tuple-element.44.plan_ref) | copy-start | bytes 24580
  13.2 4.5 %collective-permute-start.3 = (bf16[50,16,128]{2,1,0:T(8,128)(2,1)S(1)}, bf16[50,16,128]{2,1,0:T(8,128)(2,1)S(1)}, u32[]{:S(2)}, u32[]{:S(2)}) collective-permute-start(bf16[50,16,128]{2,1,0:T(8,128)(2,1)S(1)} %get-tuple-element.45), channel_id=1, source_target_pairs={{0,4},{4,0},{8,12},{12,8},{16,20},{20,16},{24,28},{28,24},{32,36},... | collective-permute-start | bytes 614408 | tf_op jit(solution)/shard_map/ppermute | solution.py:494
  14.7 30.4 %collective-permute-start.9 = (bf16[16,16,128]{2,1,0:T(8,128)(2,1)}, bf16[16,16,128]{2,1,0:T(8,128)(2,1)}, u32[]{:S(2)}, u32[]{:S(2)}) collective-permute-start(bf16[16,16,128]{2,1,0:T(8,128)(2,1)} %get-tuple-element.51), channel_id=1, source_target_pairs={{4,8},{8,4},{12,16},{16,12},{20,24},{24,20},{28,32},{32,28},{36,40... | collective-permute-start | bytes 196616 | tf_op jit(solution)/shard_map/ppermute | solution.py:524
  17.8 6.3 %copy-start.16 = (bf16[50,16,128]{2,1,0:T(8,128)(2,1)}, bf16[50,16,128]{2,1,0:T(8,128)(2,1)S(1)}, u32[]{:S(2)}) copy-start(bf16[50,16,128]{2,1,0:T(8,128)(2,1)S(1)} %collective-permute-done.3.mate_ref) | copy-start | bytes 614404
  17.8 15.5 %collective-permute-start.6 = (bf16[66,16,128]{2,1,0:T(8,128)(2,1)S(1)}, bf16[66,16,128]{2,1,0:T(8,128)(2,1)}, u32[]{:S(2)}, u32[]{:S(2)}) collective-permute-start(bf16[66,16,128]{2,1,0:T(8,128)(2,1)S(1)} %pad_maximum_fusion.pair.pair_in), channel_id=1, source_target_pairs={{0,32},{4,228},{8,40},{12,236},{16,48},{20,244},{24,56},{28,252},{... | collective-permute-start | bytes 811016 | tf_op jit(solution)/shard_map/ppermute | solution.py:494
  24.0 1.8 %copy-start.32 = (bf16[1,16,128]{2,1,0:T(8,128)(2,1)}, bf16[1,16,128]{2,1,0:T(8,128)(2,1)S(1)}, u32[]{:S(2)}) copy-start(bf16[1,16,128]{2,1,0:T(8,128)(2,1)S(1)} %slice.86) | copy-start | bytes 12292
  24.6 10.6 %collective-permute-start.4 = (bf16[2,16,128]{2,1,0:T(8,128)(2,1)}, bf16[2,16,128]{2,1,0:T(8,128)(2,1)}, u32[]{:S(2)}, u32[]{:S(2)}) collective-permute-start(bf16[2,16,128]{2,1,0:T(8,128)(2,1)} %pad_maximum_fusion.2), channel_id=1, source_target_pairs={{0,8},{4,12},{8,0},{12,4},{16,24},{20,28},{24,16},{28,20},{32,40},... | collective-permute-start | bytes 24584 | tf_op jit(solution)/shard_map/ppermute | solution.py:494
  33.3 11.8 %copy-start.31 = (s32[64,8]{0,1:T(8,128)S(1)}, s32[64,8]{0,1:T(8,128)}, u32[]{:S(2)}) copy-start(s32[64,8]{0,1:T(8,128)} %param.21) | copy-start | bytes 6148
  33.3 9.9 %collective-permute-start.7 = (bf16[66,16,128]{2,1,0:T(8,128)(2,1)}, bf16[66,16,128]{2,1,0:T(8,128)(2,1)}, u32[]{:S(2)}, u32[]{:S(2)}) collective-permute-start(bf16[66,16,128]{2,1,0:T(8,128)(2,1)} %collective-permute-done.6.r1), channel_id=1, source_target_pairs={{0,32},{4,228},{8,40},{12,236},{16,48},{20,244},{24,56},{28,252},{... | collective-permute-start | bytes 811016 | tf_op jit(solution)/shard_map/ppermute | solution.py:494
  36.5 18.4 %collective-permute-start.5 = (bf16[4,16,128]{2,1,0:T(8,128)(2,1)}, bf16[4,16,128]{2,1,0:T(8,128)(2,1)}, u32[]{:S(2)}, u32[]{:S(2)}) collective-permute-start(bf16[4,16,128]{2,1,0:T(8,128)(2,1)} %pad_maximum_fusion.1), channel_id=1, source_target_pairs={{0,16},{4,20},{8,24},{12,28},{16,0},{20,4},{24,8},{28,12},{32,48},... | collective-permute-start | bytes 49160 | tf_op jit(solution)/shard_map/ppermute | solution.py:494
  43.2 9.5 %collective-permute-start.8 = (bf16[66,16,128]{2,1,0:T(8,128)(2,1)}, bf16[66,16,128]{2,1,0:T(8,128)(2,1)S(1)}, u32[]{:S(2)}, u32[]{:S(2)}) collective-permute-start(bf16[66,16,128]{2,1,0:T(8,128)(2,1)} %collective-permute-done.7.r2), channel_id=1, source_target_pairs={{0,32},{4,228},{8,40},{12,236},{16,48},{20,244},{24,56},{28,252},{... | collective-permute-start | bytes 811016 | tf_op jit(solution)/shard_map/ppermute | solution.py:494
  45.2 1.0 %copy-start.8 = (bf16[16,8192]{1,0:T(8,128)(2,1)S(1)}, bf16[16,8192]{1,0:T(8,128)(2,1)}, u32[]{:S(2)}) copy-start(bf16[16,8192]{1,0:T(8,128)(2,1)} %vec_ref.3) | copy-start | bytes 786436
  46.1 0.9 copy-start.17
  54.2 4.4 %collective-permute-start.10 = (bf16[33,16,128]{2,1,0:T(8,128)(2,1)}, bf16[33,16,128]{2,1,0:T(8,128)(2,1)S(1)}, u32[]{:S(2)}, u32[]{:S(2)}) collective-permute-start(bf16[33,16,128]{2,1,0:T(8,128)(2,1)} %slice.83), channel_id=1, source_target_pairs={{0,32},{4,228},{8,40},{12,236},{16,48},{20,244},{24,56},{28,252},{... | collective-permute-start | bytes 405512 | tf_op jit(solution)/shard_map/ppermute | solution.py:494
  58.5 1.0 %copy-start.6 = (bf16[66,16,128]{2,1,0:T(8,128)(2,1)S(1)}, bf16[66,16,128]{2,1,0:T(8,128)(2,1)}, u32[]{:S(2)}) copy-start(bf16[66,16,128]{2,1,0:T(8,128)(2,1)} %copy-done.5) | copy-start | bytes 811012
  61.5 13.2 %collective-permute-start.11 = (bf16[35,16,128]{2,1,0:T(8,128)(2,1)S(1)}, bf16[35,16,128]{2,1,0:T(8,128)(2,1)S(1)}, u32[]{:S(2)}, u32[]{:S(2)}) collective-permute-start(bf16[35,16,128]{2,1,0:T(8,128)(2,1)S(1)} %get-tuple-element.62), channel_id=1, source_target_pairs={{0,4},{4,0},{8,12},{12,8},{16,20},{20,16},{24,28},{28,24},{32,36},... | collective-permute-start | bytes 430088 | tf_op jit(solution)/shard_map/ppermute | solution.py:494
  63.3 13.2 %collective-permute-start.12 = (bf16[35,16,128]{2,1,0:T(8,128)(2,1)S(1)}, bf16[35,16,128]{2,1,0:T(8,128)(2,1)S(1)}, u32[]{:S(2)}, u32[]{:S(2)}) collective-permute-start(bf16[35,16,128]{2,1,0:T(8,128)(2,1)S(1)} %get-tuple-element.63), channel_id=1, source_target_pairs={{0,8},{4,12},{8,0},{12,4},{16,24},{20,28},{24,16},{28,20},{32,40},... | collective-permute-start | bytes 430088 | tf_op jit(solution)/shard_map/ppermute | solution.py:494
  63.3 20.1 %collective-permute-start.13 = (bf16[35,16,128]{2,1,0:T(8,128)(2,1)S(1)}, bf16[35,16,128]{2,1,0:T(8,128)(2,1)S(1)}, u32[]{:S(2)}, u32[]{:S(2)}) collective-permute-start(bf16[35,16,128]{2,1,0:T(8,128)(2,1)S(1)} %get-tuple-element.64), channel_id=1, source_target_pairs={{0,12},{4,8},{8,4},{12,0},{16,28},{20,24},{24,20},{28,16},{32,44},... | collective-permute-start | bytes 430088 | tf_op jit(solution)/shard_map/ppermute | solution.py:494
  65.1 18.3 %collective-permute-start.14 = (bf16[35,16,128]{2,1,0:T(8,128)(2,1)S(1)}, bf16[35,16,128]{2,1,0:T(8,128)(2,1)S(1)}, u32[]{:S(2)}, u32[]{:S(2)}) collective-permute-start(bf16[35,16,128]{2,1,0:T(8,128)(2,1)S(1)} %get-tuple-element.65), channel_id=1, source_target_pairs={{0,16},{4,20},{8,24},{12,28},{16,0},{20,4},{24,8},{28,12},{32,48},... | collective-permute-start | bytes 430088 | tf_op jit(solution)/shard_map/ppermute | solution.py:494
  66.3 17.1 %collective-permute-start.15 = (bf16[35,16,128]{2,1,0:T(8,128)(2,1)S(1)}, bf16[35,16,128]{2,1,0:T(8,128)(2,1)S(1)}, u32[]{:S(2)}, u32[]{:S(2)}) collective-permute-start(bf16[35,16,128]{2,1,0:T(8,128)(2,1)S(1)} %get-tuple-element.66), channel_id=1, source_target_pairs={{0,20},{4,16},{8,28},{12,24},{16,4},{20,0},{24,12},{28,8},{32,52},... | collective-permute-start | bytes 430088 | tf_op jit(solution)/shard_map/ppermute | solution.py:494
  68.4 1.6 %copy-start.1 = (bf16[128,64,64]{2,1,0:T(8,128)(2,1)S(1)}, bf16[128,64,64]{2,1,0:T(8,128)(2,1)}, u32[]{:S(2)}) copy-start(bf16[128,64,64]{2,1,0:T(8,128)(2,1)} %copy.14.pair_ref) | copy-start | bytes 3145732
  70.0 0.9 %copy-start.11 = (f32[32,16,128]{2,1,0:T(8,128)S(1)}, f32[32,16,128]{2,1,0:T(8,128)}, u32[]{:S(2)}) copy-start(f32[32,16,128]{2,1,0:T(8,128)} %copy-done.10) | copy-start | bytes 786436
  70.9 0.9 %copy-start.13 = (f32[32,16,128]{2,1,0:T(8,128)S(1)}, f32[32,16,128]{2,1,0:T(8,128)}, u32[]{:S(2)}) copy-start(f32[32,16,128]{2,1,0:T(8,128)} %copy-done.12) | copy-start | bytes 786436
  71.9 5.9 %copy-start.9 = (bf16[16,8192]{1,0:T(8,128)(2,1)S(1)}, bf16[16,8192]{1,0:T(8,128)(2,1)}, u32[]{:S(2)}) copy-start(bf16[16,8192]{1,0:T(8,128)(2,1)} %vec_ref.3) | copy-start | bytes 786436
  71.9 5.9 %copy-start.18 = (bf16[50,16,128]{2,1,0:T(8,128)(2,1)S(1)}, bf16[50,16,128]{2,1,0:T(8,128)(2,1)}, u32[]{:S(2)}) copy-start(bf16[50,16,128]{2,1,0:T(8,128)(2,1)} %copy-done.16) | copy-start | bytes 614404
  71.9 5.9 %copy-start.20 = (f32[3,2048]{1,0:T(4,128)S(1)}, f32[3,2048]{1,0:T(4,128)}, u32[]{:S(2)}) copy-start(f32[3,2048]{1,0:T(4,128)} %p0.3) | copy-start | bytes 73732
  71.9 5.9 %copy-start.22 = (f32[3,2048]{1,0:T(4,128)S(1)}, f32[3,2048]{1,0:T(4,128)}, u32[]{:S(2)}) copy-start(f32[3,2048]{1,0:T(4,128)} %copy-done.21) | copy-start | bytes 73732
  71.9 5.9 %copy-start.24 = (f32[3,2048]{1,0:T(4,128)S(1)}, f32[3,2048]{1,0:T(4,128)}, u32[]{:S(2)}) copy-start(f32[3,2048]{1,0:T(4,128)} %copy-done.23) | copy-start | bytes 73732
  71.9 5.9 %copy-start.26 = (f32[3,2048]{1,0:T(4,128)S(1)}, f32[3,2048]{1,0:T(4,128)}, u32[]{:S(2)}) copy-start(f32[3,2048]{1,0:T(4,128)} %copy-done.25) | copy-start | bytes 73732
  74.7 8.7 %collective-permute-start.16 = (bf16[35,16,128]{2,1,0:T(8,128)(2,1)S(1)}, bf16[35,16,128]{2,1,0:T(8,128)(2,1)S(1)}, u32[]{:S(2)}, u32[]{:S(2)}) collective-permute-start(bf16[35,16,128]{2,1,0:T(8,128)(2,1)S(1)} %get-tuple-element.67), channel_id=1, source_target_pairs={{0,24},{4,28},{8,16},{12,20},{16,8},{20,12},{24,0},{28,4},{32,56},... | collective-permute-start | bytes 430088 | tf_op jit(solution)/shard_map/ppermute | solution.py:494
  76.5 9.3 %copy-start.3 = (bf16[64,64,64]{2,1,0:T(8,128)(2,1)S(1)}, bf16[64,64,64]{2,1,0:T(8,128)(2,1)}, u32[]{:S(2)}) copy-start(bf16[64,64,64]{2,1,0:T(8,128)(2,1)} %upper_t_ref.1) | copy-start | bytes 1572868
  76.5 9.3 %copy-start.4 = (bf16[64,64,64]{2,1,0:T(8,128)(2,1)S(1)}, bf16[64,64,64]{2,1,0:T(8,128)(2,1)}, u32[]{:S(2)}) copy-start(bf16[64,64,64]{2,1,0:T(8,128)(2,1)} %upper_c_ref.1) | copy-start | bytes 1572868
  76.5 9.3 %collective-permute-start.17 = (bf16[35,16,128]{2,1,0:T(8,128)(2,1)S(1)}, bf16[35,16,128]{2,1,0:T(8,128)(2,1)S(1)}, u32[]{:S(2)}, u32[]{:S(2)}) collective-permute-start(bf16[35,16,128]{2,1,0:T(8,128)(2,1)S(1)} %get-tuple-element.68), channel_id=1, source_target_pairs={{0,28},{4,24},{8,20},{12,16},{16,12},{20,8},{24,4},{28,0},{32,60},... | collective-permute-start | bytes 430088 | tf_op jit(solution)/shard_map/ppermute | solution.py:494
  85.8 3.3 %copy-start = (bf16[256,64,64]{2,1,0:T(8,128)(2,1)S(1)}, bf16[256,64,64]{2,1,0:T(8,128)(2,1)}, u32[]{:S(2)}) copy-start(bf16[256,64,64]{2,1,0:T(8,128)(2,1)} %copy.13.block_ref) | copy-start | bytes 6291460
  85.8 3.3 %copy-start.15 = (f32[16,4096]{1,0:T(8,128)S(1)}, f32[16,4096]{1,0:T(8,128)}, u32[]{:S(2)}) copy-start(f32[16,4096]{1,0:T(8,128)} %copy-done.14) | copy-start | bytes 786436
  85.9 3.3 %copy-start.28 = (s32[8,256]{1,0:T(8,128)S(1)}, s32[8,256]{1,0:T(8,128)}, u32[]{:S(2)}) copy-start(s32[8,256]{1,0:T(8,128)} %copy-done.27) | copy-start | bytes 24580
  (3 other events, 2.2 us)

commit v3 on v2

--- a/solution.py
+++ b/solution.py
@@ -17,7 +17,7 @@
 GROUP = 8
 GROUP_BITS = 3
 
-NEAR_PARTS = 2
+NEAR_PARTS = 1
 
 
 def _spec(space=pltpu.VMEM):
@@ -82,7 +82,7 @@
     return jnp.concatenate([a, b], axis=1)
 
 
-def _request(anchor_ref, leaves_ref, plan_ref):
+def _request_kernel(anchor_ref, leaves_ref, table_ref, plan_ref):
     me = lax.axis_index("leaf")
     pairs = anchor_ref.shape[1]
     anchor = anchor_ref[...]
@@ -113,6 +113,7 @@
     placed = (sub128 == slot).astype(F32).astype(BF16)
     table = _dot_t((picked * tile.astype(F32)).astype(BF16), placed)
     flips = _dot_t((picked * flip.astype(F32)).astype(BF16), placed)
+    table_ref[...] = (table + 256.0 * flips).astype(jnp.int32)
     halves = jnp.floor((count[:, pairs - 1 : pairs] + 1.0) * 0.5)
     before = jnp.sum(jnp.where(sub8 < group, halves, 0.0), axis=0, keepdims=True)
     position = before.astype(jnp.int32) + (slot >> 1)
@@ -144,14 +145,10 @@
     plan_ref[4:5, :] = (plan[4:5] + 64.0 * (1.0 - plan[6:7])).astype(jnp.int32)
     total = jnp.sum(halves, axis=0, keepdims=True)
     plan_ref[5:8, :] = jnp.broadcast_to(total, (3, pairs)).astype(jnp.int32)
-    return jnp.concatenate([table, flips], axis=0).astype(BF16)
 
 
 LEAF_TILES = 32
 OWN_TILES = LEAF_TILES + 1
-TABLE_AT = OWN_TILES
-EDGE_AT = TABLE_AT + 1
-MATE_TILES = EDGE_AT + 2 * REACH
 
 
 def _split_points(coords):
@@ -161,12 +158,8 @@
 
 
 def _prepare_kernel(
-    anchor_ref, leaves_ref, vec_ref, basis_ref, move_ref, p0, p1, p2, p3,
-    own_ref, give_ref, edge_ref, coeff_ref, levels_ref, plan_ref,
+    vec_ref, basis_ref, move_ref, own_ref, coeff_ref, levels_ref
 ):
-    me = lax.axis_index("leaf")
-    mine = lax.axis_index("vec")
-    core = me & 1
     leaves = basis_ref.shape[0]
     lane = lax.broadcasted_iota(jnp.int32, (16, 128), 1)
 
@@ -179,7 +172,6 @@
         c = jnp.where(lane < 64, r[:16], r[16:])
         coeff_ref[i] = c
         own_ref[i] = c.astype(BF16)
-        give_ref[i] = c.astype(BF16)
         current.append(c)
 
     size, node = leaves // 2, leaves
@@ -199,9 +191,13 @@
     levels_ref[0] = jnp.zeros((16, 128), F32)
     passed = _pair(_mul(root, move_ref[1]), root).astype(BF16)
     own_ref[LEAF_TILES] = passed
-    give_ref[LEAF_TILES] = passed
-
-    give_ref[TABLE_AT] = _request(anchor_ref, leaves_ref, plan_ref)
+
+
+def _edges_kernel(p0, p1, p2, p3, vec_ref, give_ref, edge_ref):
+    me = lax.axis_index("leaf")
+    mine = lax.axis_index("vec")
+    core = me & 1
+    leaves = vec_ref.shape[1] // 128
 
     width = p0.shape[1]
     halo = REACH * 128
@@ -222,7 +218,7 @@
             ref[at + REACH + j] = both[:, 128 * j : 128 * j + 128]
 
     low, high = end(False), end(True)
-    place(give_ref, EDGE_AT, jnp.where(core == 0, high, low), jnp.where(core == 0, leaves - REACH, 0))
+    place(give_ref, 0, jnp.where(core == 0, high, low), jnp.where(core == 0, leaves - REACH, 0))
     place(edge_ref, 0, jnp.where(core == 0, low, high), jnp.where(core == 0, 0, leaves - REACH))
 
 
@@ -339,7 +335,8 @@
         at += LEAF_TILES
 
 
-def _gather_kernel(table_ref, pair, r1, r2, r3, r4, *rest):
+def _gather_kernel(t0, t1, t2, t3, pair, r1, r2, r3, r4, *rest):
+    tables = (t0, t1, t2, t3)
     outs, scratch = rest[:GROUP], rest[GROUP]
     blocks = [(pair, 0)]
     for ref in (r1, r2, r3):
@@ -357,8 +354,8 @@
     ]
     for k in range(GROUP):
         for s in range(LEAF_TILES):
-            a = scratch[table_ref[k, 2 * s]]
-            b = scratch[table_ref[k, 2 * s + 1]]
+            a = scratch[tables[k // 2][k % 2, k, 2 * s]]
+            b = scratch[tables[k // 2][k % 2, k, 2 * s + 1]]
             outs[k][s] = jnp.where(lane < 64, a, b)
         for i in range(3):
             outs[k][LEAF_TILES + i] = passed[i]
@@ -402,7 +399,7 @@
     per = p0.shape[1] // 128
 
     beyond = jnp.where(core == 0, REACH + leaves, 0)
-    for ref, first, at in ((mate_ref, EDGE_AT, beyond), (edge_ref, 0, REACH + leaves - beyond)):
+    for ref, first, at in ((mate_ref, 0, beyond), (edge_ref, 0, REACH + leaves - beyond)):
         for j in range(REACH):
             both = ref[first + REACH + j].astype(F32)
             features = _features(both[0:3], both[3:6])[0]
@@ -502,45 +499,81 @@
     width = vectors.shape[1]
     leaves = leaf_basis.shape[0]
 
+    own, coeff, levels = _call(
+        _prepare_kernel,
+        [tiles(OWN_TILES), tiles(LEAF_TILES, F32), tiles(LEAF_TILES, F32)],
+        3,
+        flops=1 << 26,
+        name="prepare",
+    )(vectors, leaf_basis, local_transfer)
+    mate = permute(own, lambda i: i ^ 1)
+
+    table, plan = _call(
+        _request_kernel,
+        [_shape((8, 128), jnp.int32), _shape((8, far_anchor.shape[0]), jnp.int32)],
+        2,
+        flops=1 << 22,
+        name="request",
+    )(*after((far_anchor.reshape(1, -1), far_leaves.T), own))
+    chip = jnp.stack([table, permute(table, lambda i: i ^ 1)])
+    tables = [chip] + [permute(chip, lambda i, x=x: i ^ 2 * x) for x in (1, 2, 3)]
+
+    def onward(i):
+        z, rest = i // GROUP, i % GROUP
+        return (z + 1 if i % 2 == 0 else z - 1) % (n_leaf // GROUP) * GROUP + rest
+
+    pair = jnp.concatenate([own, mate], axis=0)
+    ring1 = permute(pair, onward)
+
+    def by_rows(x, done):
+        return with_layout_constraint(after(x, done), Layout(major_to_minor=(0, 1, 2)))
+
+    far_block = by_rows(far_block, pair)
+    ring2 = permute(after(ring1, far_block), onward)
+    local_coupling = by_rows(local_coupling, ring1)
+    ring3 = permute(after(ring2, local_coupling, tables), onward)
+
+    points = after(points, ring2)
     turns = [points] + [
         lax.ppermute(points, "vec", [((i + s) % n_vec, i) for i in range(n_vec)]) for s in range(1, n_vec)
     ]
-
-    own, give, edge, coeff, levels, plan = _call(
-        _prepare_kernel,
-        [
-            tiles(OWN_TILES),
-            tiles(MATE_TILES),
-            tiles(2 * REACH),
-            tiles(LEAF_TILES, F32),
-            tiles(LEAF_TILES, F32),
-            _shape((8, far_anchor.shape[0]), jnp.int32),
-        ],
+    ring4 = permute(after(ring3, turns)[:OWN_TILES], onward)
+    give, edge = _call(
+        _edges_kernel, [tiles(2 * REACH), tiles(2 * REACH)], 5, flops=1 << 22, name="edges"
+    )(*turns, vectors)
+    sides = (
+        permute(give, lambda i: i ^ 1),
+        lax.ppermute(
+            edge,
+            "leaf",
+            [(i, i - 1 + 2 * (i % 2)) for i in range(n_leaf) if 0 <= i - 1 + 2 * (i % 2) < n_leaf],
+        ),
+    )
+    inner, couple = _call(
+        _inner_kernel,
+        [tiles(LEAF_TILES, F32), _shape((64, 64), BF16)],
+        4,
+        flops=1 << 28,
+        name="inner",
+    )(*after((coeff, levels), ring3), local_transfer, local_coupling)
+
+
+    rows = _call(
+        _gather_kernel,
+        [tiles(LEAF_TILES + 3)] * GROUP,
         9,
-        flops=1 << 26,
-        name="prepare",
-    )(far_anchor.reshape(1, -1), far_leaves.T, vectors, leaf_basis, local_transfer, *turns)
-    mate = permute(give, lambda i: i ^ 1)
-    beyond = lax.ppermute(
-        edge, "leaf", [(i, i - 1 + 2 * (i % 2)) for i in range(n_leaf) if 0 <= i - 1 + 2 * (i % 2) < n_leaf]
-    )
-
-    def onward(i):
-        z, rest = i // GROUP, i % GROUP
-        return (z + 1 if i % 2 == 0 else z - 1) % (n_leaf // GROUP) * GROUP + rest
-
-    pair = jnp.concatenate([own, mate[:OWN_TILES]], axis=0)
-    ring1 = permute(pair, onward)
-    tables = jnp.concatenate([give[TABLE_AT : TABLE_AT + 1], mate[TABLE_AT : TABLE_AT + 1]], axis=0)
-    for bit in range(1, GROUP_BITS):
-        tables = jnp.concatenate([tables, permute(tables, lambda i: i ^ (1 << bit))], axis=0)
-    wanted = jnp.stack([tables[k, k] + 256 * tables[k, 8 + k].astype(F32) for k in range(GROUP)])
-    wanted = wanted.astype(jnp.int32)
+        smem=(0, 1, 2, 3),
+        scratch=[pltpu.VMEM((512, 16, 128), BF16)],
+        flops=1 << 22,
+        name="gather",
+    )(*after(tables, inner, sides), pair, ring1, ring2, ring3, ring4)
+
+    got = [rows[0]] + [permute(rows[k], lambda i, k=k: i ^ k) for k in range(1, GROUP)]
 
     blocks = leaves + 2 * REACH
 
     def near_part(part, done):
-        args = after((near_cols.T, *turns, vectors, mate, beyond), done)
+        args = after((near_cols.T, *turns, vectors, *sides), done)
         return _call(
             functools.partial(_near_kernel, part, NEAR_PARTS),
             _shape((vectors.shape[0], width // NEAR_PARTS), F32),
@@ -557,35 +590,7 @@
             mib=12,
         )(*args)
 
-    def by_rows(x, done):
-        return with_layout_constraint(after(x, done), Layout(major_to_minor=(0, 1, 2)))
-
-    far_block = by_rows(far_block, pair)
-    ring2 = permute(after(ring1, far_block), onward)
-    local_coupling = by_rows(local_coupling, ring1)
-    ring3 = permute(after(ring2, local_coupling), onward)
-    near = [near_part(0, ring2)]
-    ring4 = permute(after(ring3, near[0])[:OWN_TILES], onward)
-
-    rows = _call(
-        _gather_kernel,
-        [tiles(LEAF_TILES + 3)] * GROUP,
-        6,
-        smem=(0,),
-        scratch=[pltpu.VMEM((512, 16, 128), BF16)],
-        flops=1 << 22,
-        name="gather",
-    )(wanted, pair, ring1, ring2, ring3, ring4)
-    got = [rows[0]] + [permute(rows[k], lambda i, k=k: i ^ k) for k in range(1, GROUP)]
-
-    near.append(near_part(1, rows[0]))
-    inner, couple = _call(
-        _inner_kernel,
-        [tiles(LEAF_TILES, F32), _shape((64, 64), BF16)],
-        4,
-        flops=1 << 28,
-        name="inner",
-    )(*after((coeff, levels), rows[0]), local_transfer, local_coupling)
+    near = [near_part(part, rows[0]) for part in range(NEAR_PARTS)]
 
     local = _call(
         _tree_kernel,

time: 95.2 us -> 88.7 us (0.932)
  other arithmetic: 6.85 us -> 0.01 us
  waiting for transfers between devices: 2.79 us -> 8.37 us
  local copies, waits for them, and re-layouts: 26.1 us -> 21.5 us
  Pallas kernels: 27.3 us -> 25.3 us
  starting transfers between devices: 31.2 us -> 32.8 us
    ppermute x14 -> x17, starting transfers between devices: 22.3 us -> 27.1 us  [permute(): return lax.ppermute(x, 'leaf', [(i, to(i)) for i in everyone])]
    add x4 -> x0, other arithmetic: 4.24 us -> none  [per_device(): tables[k, k] + 256 * tables[k, 8 + k].astype(F32)]
    ppermute x3, waiting for transfers between devices: 0.01 us -> 3.87 us  [per_device(): lax.ppermute(points, 'vec', [((i + s) % n_vec, i) for i in range(n_vec)])]
    unnamed x67 -> x34, local copies, waits for them, and re-layouts: 11.8 us -> 9.23 us
    ppermute x3, starting transfers between devices: 5.89 us -> 3.77 us  [per_device(): lax.ppermute(points, 'vec', [((i + s) % n_vec, i) for i in range(n_vec)])]
    pallas_call x2 -> x1, Pallas kernels: 11.2 us -> 9.2 us  [near_part(): _call(functools.partial(_near_kernel, part, NEAR_PARTS), _shape((vectors....]
    concatenate x3 -> x0, other arithmetic: 1.93 us -> none  [the longest x1 1.3 us: per_device(): jnp.concatenate([tables, permute(tables, lambda i: i ^ 1 << bit)], axis=0)]
    ppermute x14 -> x17, waiting for transfers between devices: 2.78 us -> 4.49 us  [permute(): return lax.ppermute(x, 'leaf', [(i, to(i)) for i in everyone])]
  transfers between devices with their start and end apart: 18 -> 21, of which waited for: 2 -> 5; matrix products, arithmetic and copies ran while one was open for 26% -> 14% of each run, Pallas kernels for 15% -> 14%
where the time goes in v3:
time: 88.7 us; the launch traced here: 88.1 us
  starting transfers between devices  32.8 us (37%)
  Pallas kernels  25.3 us (29%)
  local copies, waits for them, and re-layouts  21.5 us (24%)
  waiting for transfers between devices  8.37 us (9%)
    ppermute x17, starting transfers between devices, permute(): return lax.ppermute(x, 'leaf', [(i, to(i)) for i in everyone])  27.1 us
    optimization_barrier x2, local copies, waits for them, and re-layouts, after(): return lax.optimization_barrier((x, done))[0]  12.2 us
    unnamed x34, local copies, waits for them, and re-layouts  9.23 us
    pallas_call x1, Pallas kernels, near_part(): _call(functools.partial(_near_kernel, part, NEAR_PARTS), _shape((vectors....  9.2 us
    pallas_call x1, Pallas kernels, per_device(): _call(_final_kernel, _shape(vectors.shape, F32), 12 + NEAR_PARTS, smem=(0...  5.49 us
    ppermute x17, waiting for transfers between devices, permute(): return lax.ppermute(x, 'leaf', [(i, to(i)) for i in everyone])  4.49 us
    ppermute x3, waiting for transfers between devices, per_device(): lax.ppermute(points, 'vec', [((i + s) % n_vec, i) for i in range(n_vec)])  3.87 us
    ppermute x3, starting transfers between devices, per_device(): lax.ppermute(points, 'vec', [((i + s) % n_vec, i) for i in range(n_vec)])  3.77 us
  transfers between devices with their start and end apart: 21, of which 5 were waited for; matrix products, arithmetic and copies ran while one was open for 14% of the time, Pallas kernels for 14%

profile of v3, /device:TPU:1, one launch (start us, length us, event | category | flops | bytes accessed | tf_op | source)
XLA Modules:
  0.0 88.1 jit_solution(15577223346330897597)
XLA Ops:
  0.0 4.0 %copy.12.move_ref = bf16[128,64,64]{2,1,0:T(8,128)(2,1)S(1)} copy(bf16[128,64,64]{0,2,1:T(8,128)(2,1)} %param.14) | data formatting | bytes 2097152 | tf_op args[3]
  4.1 2.0 %prepare.1 = (bf16[33,16,128]{2,1,0:T(8,128)(2,1)S(1)}, f32[32,16,128]{2,1,0:T(8,128)S(1)}, f32[32,16,128]{2,1,0:T(8,128)S(1)}) custom-call(bf16[16,8192]{1,0:T(8,128)(2,1)S(1)} %copy-done.5, bf16[64,64,128]{2,1,0:T(8,128)(2,1)S(1)} %copy-done.2, bf16[128,64,64]{2,1,0:T(8,128)(2,1)S(1)} %copy.12.move_ref), custom_call_target="tpu_custom_call" | custom-call | flops 67108864 | bytes 1048576 | tf_op jit(solution)/shard_map/prepare/pallas_call | solution.py:502
  6.1 0.7 copy-done.10
  6.8 3.2 %collective-permute-start.4 = (bf16[33,16,128]{2,1,0:T(8,128)(2,1)S(1)}, bf16[33,16,128]{2,1,0:T(8,128)(2,1)S(1)}, u32[]{:S(2)}, u32[]{:S(2)}) collective-permute-start(bf16[33,16,128]{2,1,0:T(8,128)(2,1)S(1)} %get-tuple-element.44), channel_id=1, source_target_pairs={{0,4},{4,0},{8,12},{12,8},{16,20},{20,16},{24,28},{28,24},{32,36},... | collective-permute-start | bytes 405512 | tf_op jit(solution)/shard_map/ppermute | solution.py:491
  10.0 1.0 %collective-permute-done.4 = bf16[33,16,128]{2,1,0:T(8,128)(2,1)S(1)} collective-permute-done((bf16[33,16,128]{2,1,0:T(8,128)(2,1)S(1)}, bf16[33,16,128]{2,1,0:T(8,128)(2,1)S(1)}, u32[]{:S(2)}, u32[]{:S(2)}) %collective-permute-start.4) | collective-permute-done | bytes 135200 | tf_op jit(solution)/shard_map/ppermute | solution.py:491
  11.0 0.0 copy-start.14
  11.0 0.0 copy-start.15
  11.1 3.9 %collective-permute-start.5 = (bf16[66,16,128]{2,1,0:T(8,128)(2,1)S(1)}, bf16[66,16,128]{2,1,0:T(8,128)(2,1)}, u32[]{:S(2)}, u32[]{:S(2)}) collective-permute-start(bf16[66,16,128]{2,1,0:T(8,128)(2,1)S(1)} %constant_dynamic-update-slice_fusion.pair.pair_in), channel_id=1, source_target_pairs={{0,32},{4,228},{8,40},{12,236},{16,48},{20,244},{24,56},{28,252},{... | collective-permute-start | bytes 811016 | tf_op jit(solution)/shard_map/ppermute | solution.py:491
  15.0 7.4 %copy.13.block_ref = bf16[256,64,64]{2,1,0:T(8,128)(2,1)} copy(bf16[256,64,64]{0,2,1:T(8,128)(2,1)} %param.20) | data formatting | bytes 4194304 | tf_op jit(solution)/shard_map/optimization_barrier | solution.py:494
  22.4 0.0 collective-permute-done.5.r1
  22.4 0.7 collective-permute-start.6
  23.2 0.4 request.1
  23.6 0.1 collective-permute-start
  23.7 1.2 %collective-permute-done = s32[8,128]{1,0:T(8,128)S(1)} collective-permute-done((s32[8,128]{1,0:T(8,128)S(1)}, s32[8,128]{1,0:T(8,128)S(1)}, u32[]{:S(2)}, u32[]{:S(2)}) %collective-permute-start) | collective-permute-done | bytes 4128 | tf_op jit(solution)/shard_map/ppermute | solution.py:491
  24.8 1.2 %collective-permute-start.1 = (s32[2,8,128]{2,1,0:T(8,128)S(1)}, s32[2,8,128]{2,1,0:T(8,128)S(1)}, u32[]{:S(2)}, u32[]{:S(2)}) collective-permute-start(s32[2,8,128]{2,1,0:T(8,128)S(1)} %pad_add_fusion.t0), channel_id=1, source_target_pairs={{0,8},{4,12},{8,0},{12,4},{16,24},{20,28},{24,16},{28,20},{32,40},... | collective-permute-start | bytes 24584 | tf_op jit(solution)/shard_map/ppermute | solution.py:491
  26.0 2.5 %collective-permute-start.2 = (s32[2,8,128]{2,1,0:T(8,128)S(1)}, s32[2,8,128]{2,1,0:T(8,128)S(1)}, u32[]{:S(2)}, u32[]{:S(2)}) collective-permute-start(s32[2,8,128]{2,1,0:T(8,128)S(1)} %pad_add_fusion.t0), channel_id=1, source_target_pairs={{0,16},{4,20},{8,24},{12,28},{16,0},{20,4},{24,8},{28,12},{32,48},... | collective-permute-start | bytes 24584 | tf_op jit(solution)/shard_map/ppermute | solution.py:491
  28.5 0.2 collective-permute-start.3
  28.7 4.8 %copy.14.pair_ref = bf16[128,64,64]{2,1,0:T(8,128)(2,1)} copy(bf16[128,64,64]{0,2,1:T(8,128)(2,1)} %param.15) | data formatting | bytes 2097152 | tf_op jit(solution)/shard_map/optimization_barrier | solution.py:494
  33.5 0.0 collective-permute-done.1.t1
  33.5 0.0 collective-permute-done.2.t2
  33.5 0.0 collective-permute-done.6.r2
  33.5 0.8 collective-permute-start.7
  34.3 2.7 %collective-permute-start.8 = (f32[3,2048]{1,0:T(4,128)S(1)}, f32[3,2048]{1,0:T(4,128)S(1)}, u32[]{:S(2)}, u32[]{:S(2)}) collective-permute-start(f32[3,2048]{1,0:T(4,128)S(1)} %copy-done.12), channel_id=1, source_target_pairs={{1,0},{2,1},{3,2},{0,3},{5,4},{6,5},{7,6},{4,7},{9,8},{10,9},{11,1... | collective-permute-start | bytes 73736 | tf_op jit(solution)/shard_map/ppermute | solution.py:538
  37.0 0.3 collective-permute-start.9
  37.4 0.7 collective-permute-start.10
  38.1 0.0 collective-permute-done.8.p1
  38.1 3.3 %collective-permute-done.9.p2 = f32[3,2048]{1,0:T(4,128)S(1)} collective-permute-done((f32[3,2048]{1,0:T(4,128)S(1)}, f32[3,2048]{1,0:T(4,128)S(1)}, u32[]{:S(2)}, u32[]{:S(2)}) %collective-permute-start.9) | collective-permute-done | bytes 24608 | tf_op jit(solution)/shard_map/ppermute | solution.py:538
  41.3 0.6 collective-permute-done.10.p3
  42.0 0.5 collective-permute-start.13
  42.5 0.9 %copy-done.6 = bf16[16,8192]{1,0:T(8,128)(2,1)S(1)} copy-done((bf16[16,8192]{1,0:T(8,128)(2,1)S(1)}, bf16[16,8192]{1,0:T(8,128)(2,1)}, u32[]{:S(2)}) %copy-start.6) | copy-done | bytes 262168
  43.5 3.8 %collective-permute-start.11 = (bf16[16,16,128]{2,1,0:T(8,128)(2,1)S(1)}, bf16[16,16,128]{2,1,0:T(8,128)(2,1)S(1)}, u32[]{:S(2)}, u32[]{:S(2)}) collective-permute-start(bf16[16,16,128]{2,1,0:T(8,128)(2,1)S(1)} %get-tuple-element.59), channel_id=1, source_target_pairs={{0,4},{4,0},{8,12},{12,8},{16,20},{20,16},{24,28},{28,24},{32,36},... | collective-permute-start | bytes 196616 | tf_op jit(solution)/shard_map/ppermute | solution.py:491
  47.3 1.9 %collective-permute-start.12 = (bf16[16,16,128]{2,1,0:T(8,128)(2,1)S(1)}, bf16[16,16,128]{2,1,0:T(8,128)(2,1)S(1)}, u32[]{:S(2)}, u32[]{:S(2)}) collective-permute-start(bf16[16,16,128]{2,1,0:T(8,128)(2,1)S(1)} %get-tuple-element.60), channel_id=1, source_target_pairs={{4,8},{8,4},{12,16},{16,12},{20,24},{24,20},{28,32},{32,28},{36,40... | collective-permute-start | bytes 196616 | tf_op jit(solution)/shard_map/ppermute | solution.py:546
  49.2 1.6 %copy-done.1 = bf16[128,64,64]{2,1,0:T(8,128)(2,1)S(1)} copy-done((bf16[128,64,64]{2,1,0:T(8,128)(2,1)S(1)}, bf16[128,64,64]{2,1,0:T(8,128)(2,1)}, u32[]{:S(2)}) %copy-start.1) | copy-done | bytes 1048600
  50.8 0.9 %copy-done.9 = f32[32,16,128]{2,1,0:T(8,128)S(1)} copy-done((f32[32,16,128]{2,1,0:T(8,128)S(1)}, f32[32,16,128]{2,1,0:T(8,128)}, u32[]{:S(2)}) %copy-start.9) | copy-done | bytes 262168
  51.8 0.9 %copy-done.11 = f32[32,16,128]{2,1,0:T(8,128)S(1)} copy-done((f32[32,16,128]{2,1,0:T(8,128)S(1)}, f32[32,16,128]{2,1,0:T(8,128)}, u32[]{:S(2)}) %copy-start.11) | copy-done | bytes 262168
  52.7 2.8 %inner.1 = (f32[32,16,128]{2,1,0:T(8,128)S(1)}, bf16[64,64]{1,0:T(8,128)(2,1)S(1)}) custom-call(f32[32,16,128]{2,1,0:T(8,128)S(1)} %copy-done.9, f32[32,16,128]{2,1,0:T(8,128)S(1)} %copy-done.11, bf16[128,64,64]{2,1,0:T(8,128)(2,1)S(1)} %copy.12.move_ref, bf16[128,64,64]{2,1,0:T(8,128)(2,1)S(1)} %copy-done.1), custom_call_target="tpu_custom_call" | custom-call | flops 268435456 | bytes 1048576 | tf_op jit(solution)/shard_map/inner/pallas_call | solution.py:552
  55.6 2.1 %gather.1 = (bf16[35,16,128]{2,1,0:T(8,128)(2,1)S(1)}, bf16[35,16,128]{2,1,0:T(8,128)(2,1)S(1)}, bf16[35,16,128]{2,1,0:T(8,128)(2,1)S(1)}, bf16[35,16,128]{2,1,0...) custom-call(s32[2,8,128]{2,1,0:T(8,128)S(1)} %pad_add_fusion.t0, ...), custom_call_target="tpu_custom_call" | custom-call | flops 4194304 | bytes 1048576 | tf_op jit(solution)/shard_map/gather/pallas_call | solution.py:561
  57.7 0.1 collective-permute-start.14
  57.8 1.9 %collective-permute-start.15 = (bf16[35,16,128]{2,1,0:T(8,128)(2,1)S(1)}, bf16[35,16,128]{2,1,0:T(8,128)(2,1)S(1)}, u32[]{:S(2)}, u32[]{:S(2)}) collective-permute-start(bf16[35,16,128]{2,1,0:T(8,128)(2,1)S(1)} %get-tuple-element.68), channel_id=1, source_target_pairs={{0,8},{4,12},{8,0},{12,4},{16,24},{20,28},{24,16},{28,20},{32,40},... | collective-permute-start | bytes 430088 | tf_op jit(solution)/shard_map/ppermute | solution.py:491
  59.6 0.3 collective-permute-start.16
  59.9 3.6 %collective-permute-start.17 = (bf16[35,16,128]{2,1,0:T(8,128)(2,1)S(1)}, bf16[35,16,128]{2,1,0:T(8,128)(2,1)S(1)}, u32[]{:S(2)}, u32[]{:S(2)}) collective-permute-start(bf16[35,16,128]{2,1,0:T(8,128)(2,1)S(1)} %get-tuple-element.70), channel_id=1, source_target_pairs={{0,16},{4,20},{8,24},{12,28},{16,0},{20,4},{24,8},{28,12},{32,48},... | collective-permute-start | bytes 430088 | tf_op jit(solution)/shard_map/ppermute | solution.py:491
  63.5 2.4 %collective-permute-start.19 = (bf16[35,16,128]{2,1,0:T(8,128)(2,1)S(1)}, bf16[35,16,128]{2,1,0:T(8,128)(2,1)S(1)}, u32[]{:S(2)}, u32[]{:S(2)}) collective-permute-start(bf16[35,16,128]{2,1,0:T(8,128)(2,1)S(1)} %get-tuple-element.72), channel_id=1, source_target_pairs={{0,24},{4,28},{8,16},{12,20},{16,8},{20,12},{24,0},{28,4},{32,56},... | collective-permute-start | bytes 430088 | tf_op jit(solution)/shard_map/ppermute | solution.py:491
  65.9 1.9 %collective-permute-start.20 = (bf16[35,16,128]{2,1,0:T(8,128)(2,1)S(1)}, bf16[35,16,128]{2,1,0:T(8,128)(2,1)S(1)}, u32[]{:S(2)}, u32[]{:S(2)}) collective-permute-start(bf16[35,16,128]{2,1,0:T(8,128)(2,1)S(1)} %get-tuple-element.73), channel_id=1, source_target_pairs={{0,28},{4,24},{8,20},{12,16},{16,12},{20,8},{24,4},{28,0},{32,60},... | collective-permute-start | bytes 430088 | tf_op jit(solution)/shard_map/ppermute | solution.py:491
  67.8 9.2 %near0.1.rest_0_ = f32[16,8192]{1,0:T(8,128)S(1)} custom-call(s32[8,64]{1,0:T(8,128)S(1)} %bitcast.6, f32[3,2048]{1,0:T(4,128)S(1)} %copy-done.12, f32[3,2048]{1,0:T(4,128)S(1)} %collective-permute-done.8.p1, f32[3,2048]{1,0:T(4,128)S(1)} %collective-permute-done.9.p2, f32[3,2048]{1,0:T(4,128)S(1)} %collective-permute-done.10.p3, ...), custom_call_target="tpu_custom_call" | custom-call | flops 2147483648 | bytes 1048576 | tf_op jit(solution)/shard_map/near0/pallas_call | solution.py:577
  77.0 0.0 collective-permute-done.16.g3.r3
  77.1 2.3 %collective-permute-done.20.g7.r7 = bf16[35,16,128]{2,1,0:T(8,128)(2,1)S(1)} collective-permute-done((bf16[35,16,128]{2,1,0:T(8,128)(2,1)S(1)}, bf16[35,16,128]{2,1,0:T(8,128)(2,1)S(1)}, u32[]{:S(2)}, u32[]{:S(2)}) %collective-permute-start.20) | collective-permute-done | bytes 143392 | tf_op jit(solution)/shard_map/ppermute | solution.py:491
  79.4 3.2 %tree.1.local_ref = f32[32,16,128]{2,1,0:T(8,128)S(1)} custom-call(bf16[66,16,128]{2,1,0:T(8,128)(2,1)S(1)} %constant_dynamic-update-slice_fusion.pair.pair_in, bf16[35,16,128]{2,1,0:T(8,128)(2,1)S(1)} %get-tuple-element.66.g0.r0, bf16[35,16,128]{2,1,0:T(8,128)(2,1)S(1)} %collective-permute-done.14.g1.r1, ...), custom_call_target="tpu_custom_call" | custom-call | flops 67108864 | bytes 1048576 | tf_op jit(solution)/shard_map/tree/pallas_call | solution.py:595
  82.6 5.5 %final.1 = f32[16,8192]{1,0:T(8,128)} custom-call(s32[8,256]{1,0:T(8,128)S(1)} %get-tuple-element.47.plan_ref, bf16[35,16,128]{2,1,0:T(8,128)(2,1)S(1)} %get-tuple-element.66.g0.r0, bf16[35,16,128]{2,1,0:T(8,128)(2,1)S(1)} %collective-permute-done.14.g1.r1, bf16[35,16,128]{2,1,0:T(8,128)(2,1)S(1)} %collective-permute-done.15.g2.r2, ...), custom_call_target="tpu_custom_call" | custom-call | flops 134217728 | bytes 1048576 | tf_op jit(solution)/shard_map/final/pallas_call | solution.py:603
  (41 shorter events, 0.2 us)
Async XLA Ops:
  0.0 4.1 %copy-start.5 = (bf16[16,8192]{1,0:T(8,128)(2,1)S(1)}, bf16[16,8192]{1,0:T(8,128)(2,1)}, u32[]{:S(2)}) copy-start(bf16[16,8192]{1,0:T(8,128)(2,1)} %vec_ref.4) | copy-start | bytes 786436
  0.0 4.1 %copy-start.2 = (bf16[64,64,128]{2,1,0:T(8,128)(2,1)S(1)}, bf16[64,64,128]{2,1,0:T(8,128)(2,1)}, u32[]{:S(2)}) copy-start(bf16[64,64,128]{2,1,0:T(8,128)(2,1)} %basis_ref.3) | copy-start | bytes 3145732
  6.1 0.7 copy-start.10
  6.8 4.3 %copy-start.8 = (f32[32,16,128]{2,1,0:T(8,128)}, f32[32,16,128]{2,1,0:T(8,128)S(1)}, u32[]{:S(2)}) copy-start(f32[32,16,128]{2,1,0:T(8,128)S(1)} %get-tuple-element.55.coeff_ref) | copy-start | bytes 786436
  6.8 4.2 %collective-permute-start.4 = (bf16[33,16,128]{2,1,0:T(8,128)(2,1)S(1)}, bf16[33,16,128]{2,1,0:T(8,128)(2,1)S(1)}, u32[]{:S(2)}, u32[]{:S(2)}) collective-permute-start(bf16[33,16,128]{2,1,0:T(8,128)(2,1)S(1)} %get-tuple-element.44), channel_id=1, source_target_pairs={{0,4},{4,0},{8,12},{12,8},{16,20},{20,16},{24,28},{28,24},{32,36},... | collective-permute-start | bytes 405512 | tf_op jit(solution)/shard_map/ppermute | solution.py:491
  11.0 12.1 %copy-start.14 = (s32[256,2]{0,1:T(2,128)S(1)}, s32[256,2]{0,1:T(2,128)}, u32[]{:S(2)}) copy-start(s32[256,2]{0,1:T(2,128)} %param.19) | copy-start | bytes 6148
  11.0 12.1 %copy-start.15 = (s32[256,1]{0,1:T(1,128)S(1)}, s32[256,1]{0,1:T(1,128)}, u32[]{:S(2)}) copy-start(s32[256,1]{0,1:T(1,128)} %param.18) | copy-start | bytes 3076
  11.1 11.4 %collective-permute-start.5 = (bf16[66,16,128]{2,1,0:T(8,128)(2,1)S(1)}, bf16[66,16,128]{2,1,0:T(8,128)(2,1)}, u32[]{:S(2)}, u32[]{:S(2)}) collective-permute-start(bf16[66,16,128]{2,1,0:T(8,128)(2,1)S(1)} %constant_dynamic-update-slice_fusion.pair.pair_in), channel_id=1, source_target_pairs={{0,32},{4,228},{8,40},{12,236},{16,48},{20,244},{24,56},{28,252},{... | collective-permute-start | bytes 811016 | tf_op jit(solution)/shard_map/ppermute | solution.py:491
  22.4 11.9 %copy-start.12 = (f32[3,2048]{1,0:T(4,128)S(1)}, f32[3,2048]{1,0:T(4,128)}, u32[]{:S(2)}) copy-start(f32[3,2048]{1,0:T(4,128)} %p0.1) | copy-start | bytes 73732
  22.4 11.1 %collective-permute-start.6 = (bf16[66,16,128]{2,1,0:T(8,128)(2,1)}, bf16[66,16,128]{2,1,0:T(8,128)(2,1)}, u32[]{:S(2)}, u32[]{:S(2)}) collective-permute-start(bf16[66,16,128]{2,1,0:T(8,128)(2,1)} %collective-permute-done.5.r1), channel_id=1, source_target_pairs={{0,32},{4,228},{8,40},{12,236},{16,48},{20,244},{24,56},{28,252},{... | collective-permute-start | bytes 811016 | tf_op jit(solution)/shard_map/ppermute | solution.py:491
  23.6 1.3 %collective-permute-start = (s32[8,128]{1,0:T(8,128)S(1)}, s32[8,128]{1,0:T(8,128)S(1)}, u32[]{:S(2)}, u32[]{:S(2)}) collective-permute-start(s32[8,128]{1,0:T(8,128)S(1)} %get-tuple-element.48), channel_id=1, source_target_pairs={{0,4},{4,0},{8,12},{12,8},{16,20},{20,16},{24,28},{28,24},{32,36},... | collective-permute-start | bytes 12296 | tf_op jit(solution)/shard_map/ppermute | solution.py:491
  24.8 8.6 %collective-permute-start.1 = (s32[2,8,128]{2,1,0:T(8,128)S(1)}, s32[2,8,128]{2,1,0:T(8,128)S(1)}, u32[]{:S(2)}, u32[]{:S(2)}) collective-permute-start(s32[2,8,128]{2,1,0:T(8,128)S(1)} %pad_add_fusion.t0), channel_id=1, source_target_pairs={{0,8},{4,12},{8,0},{12,4},{16,24},{20,28},{24,16},{28,20},{32,40},... | collective-permute-start | bytes 24584 | tf_op jit(solution)/shard_map/ppermute | solution.py:491
  26.0 7.4 %collective-permute-start.2 = (s32[2,8,128]{2,1,0:T(8,128)S(1)}, s32[2,8,128]{2,1,0:T(8,128)S(1)}, u32[]{:S(2)}, u32[]{:S(2)}) collective-permute-start(s32[2,8,128]{2,1,0:T(8,128)S(1)} %pad_add_fusion.t0), channel_id=1, source_target_pairs={{0,16},{4,20},{8,24},{12,28},{16,0},{20,4},{24,8},{28,12},{32,48},... | collective-permute-start | bytes 24584 | tf_op jit(solution)/shard_map/ppermute | solution.py:491
  28.5 5.0 %collective-permute-start.3 = (s32[2,8,128]{2,1,0:T(8,128)S(1)}, s32[2,8,128]{2,1,0:T(8,128)S(1)}, u32[]{:S(2)}, u32[]{:S(2)}) collective-permute-start(s32[2,8,128]{2,1,0:T(8,128)S(1)} %pad_add_fusion.t0), channel_id=1, source_target_pairs={{0,24},{4,28},{8,16},{12,20},{16,8},{20,12},{24,0},{28,4},{32,56},... | collective-permute-start | bytes 24584 | tf_op jit(solution)/shard_map/ppermute | solution.py:491
  33.5 8.5 %collective-permute-start.7 = (bf16[66,16,128]{2,1,0:T(8,128)(2,1)}, bf16[66,16,128]{2,1,0:T(8,128)(2,1)S(1)}, u32[]{:S(2)}, u32[]{:S(2)}) collective-permute-start(bf16[66,16,128]{2,1,0:T(8,128)(2,1)} %collective-permute-done.6.r2), channel_id=1, source_target_pairs={{0,32},{4,228},{8,40},{12,236},{16,48},{20,244},{24,56},{28,252},{... | collective-permute-start | bytes 811016 | tf_op jit(solution)/shard_map/ppermute | solution.py:491
  34.3 3.8 %collective-permute-start.8 = (f32[3,2048]{1,0:T(4,128)S(1)}, f32[3,2048]{1,0:T(4,128)S(1)}, u32[]{:S(2)}, u32[]{:S(2)}) collective-permute-start(f32[3,2048]{1,0:T(4,128)S(1)} %copy-done.12), channel_id=1, source_target_pairs={{1,0},{2,1},{3,2},{0,3},{5,4},{6,5},{7,6},{4,7},{9,8},{10,9},{11,1... | collective-permute-start | bytes 73736 | tf_op jit(solution)/shard_map/ppermute | solution.py:538
  37.0 4.3 %collective-permute-start.9 = (f32[3,2048]{1,0:T(4,128)S(1)}, f32[3,2048]{1,0:T(4,128)S(1)}, u32[]{:S(2)}, u32[]{:S(2)}) collective-permute-start(f32[3,2048]{1,0:T(4,128)S(1)} %copy-done.12), channel_id=1, source_target_pairs={{2,0},{3,1},{0,2},{1,3},{6,4},{7,5},{4,6},{5,7},{10,8},{11,9},{8,1... | collective-permute-start | bytes 73736 | tf_op jit(solution)/shard_map/ppermute | solution.py:538
  37.4 4.6 %collective-permute-start.10 = (f32[3,2048]{1,0:T(4,128)S(1)}, f32[3,2048]{1,0:T(4,128)S(1)}, u32[]{:S(2)}, u32[]{:S(2)}) collective-permute-start(f32[3,2048]{1,0:T(4,128)S(1)} %copy-done.12), channel_id=1, source_target_pairs={{3,0},{0,1},{1,2},{2,3},{7,4},{4,5},{5,6},{6,7},{11,8},{8,9},{9,10... | collective-permute-start | bytes 73736 | tf_op jit(solution)/shard_map/ppermute | solution.py:538
  42.0 13.6 %collective-permute-start.13 = (bf16[33,16,128]{2,1,0:T(8,128)(2,1)S(1)}, bf16[33,16,128]{2,1,0:T(8,128)(2,1)S(1)}, u32[]{:S(2)}, u32[]{:S(2)}) collective-permute-start(bf16[33,16,128]{2,1,0:T(8,128)(2,1)S(1)} %slice.3), channel_id=1, source_target_pairs={{0,32},{4,228},{8,40},{12,236},{16,48},{20,244},{24,56},{28,252},{... | collective-permute-start | bytes 405512 | tf_op jit(solution)/shard_map/ppermute | solution.py:491
  42.5 0.9 %copy-start.6 = (bf16[16,8192]{1,0:T(8,128)(2,1)S(1)}, bf16[16,8192]{1,0:T(8,128)(2,1)}, u32[]{:S(2)}) copy-start(bf16[16,8192]{1,0:T(8,128)(2,1)} %vec_ref.4) | copy-start | bytes 786436
  43.5 12.1 %collective-permute-start.11 = (bf16[16,16,128]{2,1,0:T(8,128)(2,1)S(1)}, bf16[16,16,128]{2,1,0:T(8,128)(2,1)S(1)}, u32[]{:S(2)}, u32[]{:S(2)}) collective-permute-start(bf16[16,16,128]{2,1,0:T(8,128)(2,1)S(1)} %get-tuple-element.59), channel_id=1, source_target_pairs={{0,4},{4,0},{8,12},{12,8},{16,20},{20,16},{24,28},{28,24},{32,36},... | collective-permute-start | bytes 196616 | tf_op jit(solution)/shard_map/ppermute | solution.py:491
  47.3 8.3 %collective-permute-start.12 = (bf16[16,16,128]{2,1,0:T(8,128)(2,1)S(1)}, bf16[16,16,128]{2,1,0:T(8,128)(2,1)S(1)}, u32[]{:S(2)}, u32[]{:S(2)}) collective-permute-start(bf16[16,16,128]{2,1,0:T(8,128)(2,1)S(1)} %get-tuple-element.60), channel_id=1, source_target_pairs={{4,8},{8,4},{12,16},{16,12},{20,24},{24,20},{28,32},{32,28},{36,40... | collective-permute-start | bytes 196616 | tf_op jit(solution)/shard_map/ppermute | solution.py:546
  49.2 1.6 %copy-start.1 = (bf16[128,64,64]{2,1,0:T(8,128)(2,1)S(1)}, bf16[128,64,64]{2,1,0:T(8,128)(2,1)}, u32[]{:S(2)}) copy-start(bf16[128,64,64]{2,1,0:T(8,128)(2,1)} %copy.14.pair_ref) | copy-start | bytes 3145732
  50.8 0.9 %copy-start.9 = (f32[32,16,128]{2,1,0:T(8,128)S(1)}, f32[32,16,128]{2,1,0:T(8,128)}, u32[]{:S(2)}) copy-start(f32[32,16,128]{2,1,0:T(8,128)} %copy-done.8) | copy-start | bytes 786436
  51.8 0.9 %copy-start.11 = (f32[32,16,128]{2,1,0:T(8,128)S(1)}, f32[32,16,128]{2,1,0:T(8,128)}, u32[]{:S(2)}) copy-start(f32[32,16,128]{2,1,0:T(8,128)} %copy-done.10) | copy-start | bytes 786436
  52.7 15.1 %copy-start.7 = (bf16[16,8192]{1,0:T(8,128)(2,1)S(1)}, bf16[16,8192]{1,0:T(8,128)(2,1)}, u32[]{:S(2)}) copy-start(bf16[16,8192]{1,0:T(8,128)(2,1)} %vec_ref.4) | copy-start | bytes 786436
  52.7 15.1 %copy-start.13 = (s32[64,8]{0,1:T(8,128)S(1)}, s32[64,8]{0,1:T(8,128)}, u32[]{:S(2)}) copy-start(s32[64,8]{0,1:T(8,128)} %param.21) | copy-start | bytes 6148
  57.7 5.8 %collective-permute-start.14 = (bf16[35,16,128]{2,1,0:T(8,128)(2,1)S(1)}, bf16[35,16,128]{2,1,0:T(8,128)(2,1)S(1)}, u32[]{:S(2)}, u32[]{:S(2)}) collective-permute-start(bf16[35,16,128]{2,1,0:T(8,128)(2,1)S(1)} %get-tuple-element.67), channel_id=1, source_target_pairs={{0,4},{4,0},{8,12},{12,8},{16,20},{20,16},{24,28},{28,24},{32,36},... | collective-permute-start | bytes 430088 | tf_op jit(solution)/shard_map/ppermute | solution.py:491
  57.8 8.1 %collective-permute-start.15 = (bf16[35,16,128]{2,1,0:T(8,128)(2,1)S(1)}, bf16[35,16,128]{2,1,0:T(8,128)(2,1)S(1)}, u32[]{:S(2)}, u32[]{:S(2)}) collective-permute-start(bf16[35,16,128]{2,1,0:T(8,128)(2,1)S(1)} %get-tuple-element.68), channel_id=1, source_target_pairs={{0,8},{4,12},{8,0},{12,4},{16,24},{20,28},{24,16},{28,20},{32,40},... | collective-permute-start | bytes 430088 | tf_op jit(solution)/shard_map/ppermute | solution.py:491
  59.6 17.4 %collective-permute-start.16 = (bf16[35,16,128]{2,1,0:T(8,128)(2,1)S(1)}, bf16[35,16,128]{2,1,0:T(8,128)(2,1)S(1)}, u32[]{:S(2)}, u32[]{:S(2)}) collective-permute-start(bf16[35,16,128]{2,1,0:T(8,128)(2,1)S(1)} %get-tuple-element.69), channel_id=1, source_target_pairs={{0,12},{4,8},{8,4},{12,0},{16,28},{20,24},{24,20},{28,16},{32,44},... | collective-permute-start | bytes 430088 | tf_op jit(solution)/shard_map/ppermute | solution.py:491
  59.9 17.1 %collective-permute-start.17 = (bf16[35,16,128]{2,1,0:T(8,128)(2,1)S(1)}, bf16[35,16,128]{2,1,0:T(8,128)(2,1)S(1)}, u32[]{:S(2)}, u32[]{:S(2)}) collective-permute-start(bf16[35,16,128]{2,1,0:T(8,128)(2,1)S(1)} %get-tuple-element.70), channel_id=1, source_target_pairs={{0,16},{4,20},{8,24},{12,28},{16,0},{20,4},{24,8},{28,12},{32,48},... | collective-permute-start | bytes 430088 | tf_op jit(solution)/shard_map/ppermute | solution.py:491
  63.5 13.6 %collective-permute-start.18 = (bf16[35,16,128]{2,1,0:T(8,128)(2,1)S(1)}, bf16[35,16,128]{2,1,0:T(8,128)(2,1)S(1)}, u32[]{:S(2)}, u32[]{:S(2)}) collective-permute-start(bf16[35,16,128]{2,1,0:T(8,128)(2,1)S(1)} %get-tuple-element.71), channel_id=1, source_target_pairs={{0,20},{4,16},{8,28},{12,24},{16,4},{20,0},{24,12},{28,8},{32,52},... | collective-permute-start | bytes 430088 | tf_op jit(solution)/shard_map/ppermute | solution.py:491
  63.5 13.6 %collective-permute-start.19 = (bf16[35,16,128]{2,1,0:T(8,128)(2,1)S(1)}, bf16[35,16,128]{2,1,0:T(8,128)(2,1)S(1)}, u32[]{:S(2)}, u32[]{:S(2)}) collective-permute-start(bf16[35,16,128]{2,1,0:T(8,128)(2,1)S(1)} %get-tuple-element.72), channel_id=1, source_target_pairs={{0,24},{4,28},{8,16},{12,20},{16,8},{20,12},{24,0},{28,4},{32,56},... | collective-permute-start | bytes 430088 | tf_op jit(solution)/shard_map/ppermute | solution.py:491
  65.9 13.5 %copy-start.3 = (bf16[64,64,64]{2,1,0:T(8,128)(2,1)S(1)}, bf16[64,64,64]{2,1,0:T(8,128)(2,1)}, u32[]{:S(2)}) copy-start(bf16[64,64,64]{2,1,0:T(8,128)(2,1)} %upper_t_ref.1) | copy-start | bytes 1572868
  65.9 13.5 %copy-start.4 = (bf16[64,64,64]{2,1,0:T(8,128)(2,1)S(1)}, bf16[64,64,64]{2,1,0:T(8,128)(2,1)}, u32[]{:S(2)}) copy-start(bf16[64,64,64]{2,1,0:T(8,128)(2,1)} %upper_c_ref.1) | copy-start | bytes 1572868
  65.9 13.5 %collective-permute-start.20 = (bf16[35,16,128]{2,1,0:T(8,128)(2,1)S(1)}, bf16[35,16,128]{2,1,0:T(8,128)(2,1)S(1)}, u32[]{:S(2)}, u32[]{:S(2)}) collective-permute-start(bf16[35,16,128]{2,1,0:T(8,128)(2,1)S(1)} %get-tuple-element.73), channel_id=1, source_target_pairs={{0,28},{4,24},{8,20},{12,16},{16,12},{20,8},{24,4},{28,0},{32,60},... | collective-permute-start | bytes 430088 | tf_op jit(solution)/shard_map/ppermute | solution.py:491
  79.4 3.2 %copy-start = (bf16[256,64,64]{2,1,0:T(8,128)(2,1)S(1)}, bf16[256,64,64]{2,1,0:T(8,128)(2,1)}, u32[]{:S(2)}) copy-start(bf16[256,64,64]{2,1,0:T(8,128)(2,1)} %copy.13.block_ref) | copy-start | bytes 6291460

commit v4 on v3

--- a/solution.py
+++ b/solution.py
@@ -158,7 +158,7 @@
 
 
 def _prepare_kernel(
-    vec_ref, basis_ref, move_ref, own_ref, coeff_ref, levels_ref
+    vec_ref, basis_ref, move_ref, own_ref, nodes_ref
 ):
     leaves = basis_ref.shape[0]
     lane = lax.broadcasted_iota(jnp.int32, (16, 128), 1)
@@ -170,7 +170,7 @@
         w = basis_ref[2 * i : 2 * i + 2].reshape(128, 128)
         r = _dot_t(jnp.concatenate([x0, x1], axis=0), w)
         c = jnp.where(lane < 64, r[:16], r[16:])
-        coeff_ref[i] = c
+        nodes_ref[LEAF_TILES + i] = c
         own_ref[i] = c.astype(BF16)
         current.append(c)
 
@@ -187,8 +187,8 @@
         node //= 2
         current = [_pair(parents[2 * i], parents[2 * i + 1]) for i in range(size)]
         for i in range(size):
-            levels_ref[size + i] = current[i]
-    levels_ref[0] = jnp.zeros((16, 128), F32)
+            nodes_ref[size + i] = current[i]
+    nodes_ref[0] = jnp.zeros((16, 128), F32)
     passed = _pair(_mul(root, move_ref[1]), root).astype(BF16)
     own_ref[LEAF_TILES] = passed
 
@@ -222,7 +222,7 @@
     place(edge_ref, 0, jnp.where(core == 0, low, high), jnp.where(core == 0, 0, leaves - REACH))
 
 
-def _inner_kernel(coeff_ref, levels_ref, move_ref, pair_ref, out_ref, couple_ref):
+def _inner_kernel(nodes_ref, move_ref, pair_ref, out_ref, couple_ref):
     lane = lax.broadcasted_iota(jnp.int32, (16, 128), 1)
     couple_ref[...] = pair_ref[1]
     parents = None
@@ -231,8 +231,7 @@
         children = []
         for i in range(size):
             node = 2 * size + 2 * i
-            tile = coeff_ref[i] if size == LEAF_TILES else levels_ref[size + i]
-            other = _swap_halves(tile)
+            other = _swap_halves(nodes_ref[size + i])
             both = _mul(
                 jnp.concatenate(
                     [jnp.where(lane < 64, other, 0.0), jnp.where(lane < 64, 0.0, other)], axis=0
@@ -384,7 +383,7 @@
     return source, target
 
 
-TOGETHER = 8
+TOGETHER = 16
 
 
 def _near_kernel(
@@ -434,7 +433,7 @@
     lax.fori_loop(0, count // TOGETHER, group, 0)
 
 
-BATCH = 8
+BATCH = 16
 
 
 def _final_kernel(plan_ref, r0, r1, r2, r3, r4, r5, r6, r7, block_ref, local_ref, basis_ref, *rest):
@@ -499,9 +498,9 @@
     width = vectors.shape[1]
     leaves = leaf_basis.shape[0]
 
-    own, coeff, levels = _call(
+    own, nodes = _call(
         _prepare_kernel,
-        [tiles(OWN_TILES), tiles(LEAF_TILES, F32), tiles(LEAF_TILES, F32)],
+        [tiles(OWN_TILES), tiles(2 * LEAF_TILES, F32)],
         3,
         flops=1 << 26,
         name="prepare",
@@ -552,10 +551,10 @@
     inner, couple = _call(
         _inner_kernel,
         [tiles(LEAF_TILES, F32), _shape((64, 64), BF16)],
-        4,
+        3,
         flops=1 << 28,
         name="inner",
-    )(*after((coeff, levels), ring3), local_transfer, local_coupling)
+    )(after(nodes, ring3), local_transfer, local_coupling)
 
 
     rows = _call(

time: 88.7 us -> 87 us (0.981)
  Pallas kernels: 25.3 us -> 23.9 us
    pallas_call x1, Pallas kernels: 5.49 us -> 4.6 us  [per_device(): _call(_final_kernel, _shape(vectors.shape, F32), 12 + NEAR_PARTS, smem=(0...]
    unnamed x34 -> x30, local copies, waits for them, and re-layouts: 9.23 us -> 8.47 us
where the time goes in v4:
time: 87 us; the launch traced here: 86.4 us
  starting transfers between devices  32.8 us (38%)
  Pallas kernels  23.9 us (27%)
  local copies, waits for them, and re-layouts  20.7 us (24%)
  waiting for transfers between devices  8.9 us (10%)
    ppermute x17, starting transfers between devices, permute(): return lax.ppermute(x, 'leaf', [(i, to(i)) for i in everyone])  27.1 us
    optimization_barrier x2, local copies, waits for them, and re-layouts, after(): return lax.optimization_barrier((x, done))[0]  12.2 us
    pallas_call x1, Pallas kernels, near_part(): _call(functools.partial(_near_kernel, part, NEAR_PARTS), _shape((vectors....  8.67 us
    unnamed x30, local copies, waits for them, and re-layouts  8.47 us
    ppermute x17, waiting for transfers between devices, permute(): return lax.ppermute(x, 'leaf', [(i, to(i)) for i in everyone])  5.02 us
    pallas_call x1, Pallas kernels, per_device(): _call(_final_kernel, _shape(vectors.shape, F32), 12 + NEAR_PARTS, smem=(0...  4.6 us
    ppermute x3, waiting for transfers between devices, per_device(): lax.ppermute(points, 'vec', [((i + s) % n_vec, i) for i in range(n_vec)])  3.87 us
    ppermute x3, starting transfers between devices, per_device(): lax.ppermute(points, 'vec', [((i + s) % n_vec, i) for i in range(n_vec)])  3.77 us
  transfers between devices with their start and end apart: 21, of which 5 were waited for; matrix products, arithmetic and copies ran while one was open for 14% of the time, Pallas kernels for 14%

profile of v4, /device:TPU:1, one launch (start us, length us, event | category | flops | bytes accessed | tf_op | source)
XLA Modules:
  0.0 86.4 jit_solution(11807671325457878062)
XLA Ops:
  0.0 4.0 %copy.12.move_ref = bf16[128,64,64]{2,1,0:T(8,128)(2,1)S(1)} copy(bf16[128,64,64]{0,2,1:T(8,128)(2,1)} %param.14) | data formatting | bytes 2097152 | tf_op args[3]
  4.1 2.0 %prepare.1 = (bf16[33,16,128]{2,1,0:T(8,128)(2,1)S(1)}, f32[64,16,128]{2,1,0:T(8,128)S(1)}) custom-call(bf16[16,8192]{1,0:T(8,128)(2,1)S(1)} %copy-done.5, bf16[64,64,128]{2,1,0:T(8,128)(2,1)S(1)} %copy-done.2, bf16[128,64,64]{2,1,0:T(8,128)(2,1)S(1)} %copy.12.move_ref), custom_call_target="tpu_custom_call" | custom-call | flops 67108864 | bytes 1048576 | tf_op jit(solution)/shard_map/prepare/pallas_call | solution.py:501
  6.1 0.8 copy-done.8
  6.9 3.2 %collective-permute-start.4 = (bf16[33,16,128]{2,1,0:T(8,128)(2,1)S(1)}, bf16[33,16,128]{2,1,0:T(8,128)(2,1)S(1)}, u32[]{:S(2)}, u32[]{:S(2)}) collective-permute-start(bf16[33,16,128]{2,1,0:T(8,128)(2,1)S(1)} %get-tuple-element.42), channel_id=1, source_target_pairs={{0,4},{4,0},{8,12},{12,8},{16,20},{20,16},{24,28},{28,24},{32,36},... | collective-permute-start | bytes 405512 | tf_op jit(solution)/shard_map/ppermute | solution.py:490
  10.1 1.0 %collective-permute-done.4 = bf16[33,16,128]{2,1,0:T(8,128)(2,1)S(1)} collective-permute-done((bf16[33,16,128]{2,1,0:T(8,128)(2,1)S(1)}, bf16[33,16,128]{2,1,0:T(8,128)(2,1)S(1)}, u32[]{:S(2)}, u32[]{:S(2)}) %collective-permute-start.4) | collective-permute-done | bytes 135200 | tf_op jit(solution)/shard_map/ppermute | solution.py:490
  11.1 0.0 copy-start.12
  11.1 0.0 copy-start.13
  11.2 3.9 %collective-permute-start.5 = (bf16[66,16,128]{2,1,0:T(8,128)(2,1)S(1)}, bf16[66,16,128]{2,1,0:T(8,128)(2,1)}, u32[]{:S(2)}, u32[]{:S(2)}) collective-permute-start(bf16[66,16,128]{2,1,0:T(8,128)(2,1)S(1)} %constant_dynamic-update-slice_fusion.pair.pair_in), channel_id=1, source_target_pairs={{0,32},{4,228},{8,40},{12,236},{16,48},{20,244},{24,56},{28,252},{... | collective-permute-start | bytes 811016 | tf_op jit(solution)/shard_map/ppermute | solution.py:490
  15.1 7.4 %copy.13.block_ref = bf16[256,64,64]{2,1,0:T(8,128)(2,1)} copy(bf16[256,64,64]{0,2,1:T(8,128)(2,1)} %param.20) | data formatting | bytes 4194304 | tf_op jit(solution)/shard_map/optimization_barrier | solution.py:493
  22.5 0.7 collective-permute-start.6
  23.2 0.4 request.1
  23.7 0.1 collective-permute-start
  23.8 1.2 %collective-permute-done = s32[8,128]{1,0:T(8,128)S(1)} collective-permute-done((s32[8,128]{1,0:T(8,128)S(1)}, s32[8,128]{1,0:T(8,128)S(1)}, u32[]{:S(2)}, u32[]{:S(2)}) %collective-permute-start) | collective-permute-done | bytes 4128 | tf_op jit(solution)/shard_map/ppermute | solution.py:490
  24.9 1.2 %collective-permute-start.1 = (s32[2,8,128]{2,1,0:T(8,128)S(1)}, s32[2,8,128]{2,1,0:T(8,128)S(1)}, u32[]{:S(2)}, u32[]{:S(2)}) collective-permute-start(s32[2,8,128]{2,1,0:T(8,128)S(1)} %pad_add_fusion.t0), channel_id=1, source_target_pairs={{0,8},{4,12},{8,0},{12,4},{16,24},{20,28},{24,16},{28,20},{32,40},... | collective-permute-start | bytes 24584 | tf_op jit(solution)/shard_map/ppermute | solution.py:490
  26.1 2.5 %collective-permute-start.2 = (s32[2,8,128]{2,1,0:T(8,128)S(1)}, s32[2,8,128]{2,1,0:T(8,128)S(1)}, u32[]{:S(2)}, u32[]{:S(2)}) collective-permute-start(s32[2,8,128]{2,1,0:T(8,128)S(1)} %pad_add_fusion.t0), channel_id=1, source_target_pairs={{0,16},{4,20},{8,24},{12,28},{16,0},{20,4},{24,8},{28,12},{32,48},... | collective-permute-start | bytes 24584 | tf_op jit(solution)/shard_map/ppermute | solution.py:490
  28.6 0.2 collective-permute-start.3
  28.8 4.8 %copy.14.pair_ref = bf16[128,64,64]{2,1,0:T(8,128)(2,1)} copy(bf16[128,64,64]{0,2,1:T(8,128)(2,1)} %param.15) | data formatting | bytes 2097152 | tf_op jit(solution)/shard_map/optimization_barrier | solution.py:493
  33.6 0.0 collective-permute-done.1.t1
  33.6 0.0 collective-permute-done.2.t2
  33.6 0.0 collective-permute-done.3.t3
  33.6 0.8 collective-permute-start.7
  34.4 2.7 %collective-permute-start.8 = (f32[3,2048]{1,0:T(4,128)S(1)}, f32[3,2048]{1,0:T(4,128)S(1)}, u32[]{:S(2)}, u32[]{:S(2)}) collective-permute-start(f32[3,2048]{1,0:T(4,128)S(1)} %copy-done.10), channel_id=1, source_target_pairs={{1,0},{2,1},{3,2},{0,3},{5,4},{6,5},{7,6},{4,7},{9,8},{10,9},{11,1... | collective-permute-start | bytes 73736 | tf_op jit(solution)/shard_map/ppermute | solution.py:537
  37.1 0.3 collective-permute-start.9
  37.5 0.7 collective-permute-start.10
  38.2 3.3 %collective-permute-done.9.p2 = f32[3,2048]{1,0:T(4,128)S(1)} collective-permute-done((f32[3,2048]{1,0:T(4,128)S(1)}, f32[3,2048]{1,0:T(4,128)S(1)}, u32[]{:S(2)}, u32[]{:S(2)}) %collective-permute-start.9) | collective-permute-done | bytes 24608 | tf_op jit(solution)/shard_map/ppermute | solution.py:537
  41.4 0.6 collective-permute-done.10.p3
  42.0 0.5 collective-permute-start.13
  42.6 0.9 %copy-done.6 = bf16[16,8192]{1,0:T(8,128)(2,1)S(1)} copy-done((bf16[16,8192]{1,0:T(8,128)(2,1)S(1)}, bf16[16,8192]{1,0:T(8,128)(2,1)}, u32[]{:S(2)}) %copy-start.6) | copy-done | bytes 262168
  43.6 3.8 %collective-permute-start.11 = (bf16[16,16,128]{2,1,0:T(8,128)(2,1)S(1)}, bf16[16,16,128]{2,1,0:T(8,128)(2,1)S(1)}, u32[]{:S(2)}, u32[]{:S(2)}) collective-permute-start(bf16[16,16,128]{2,1,0:T(8,128)(2,1)S(1)} %get-tuple-element.55), channel_id=1, source_target_pairs={{0,4},{4,0},{8,12},{12,8},{16,20},{20,16},{24,28},{28,24},{32,36},... | collective-permute-start | bytes 196616 | tf_op jit(solution)/shard_map/ppermute | solution.py:490
  47.4 1.9 %collective-permute-start.12 = (bf16[16,16,128]{2,1,0:T(8,128)(2,1)S(1)}, bf16[16,16,128]{2,1,0:T(8,128)(2,1)S(1)}, u32[]{:S(2)}, u32[]{:S(2)}) collective-permute-start(bf16[16,16,128]{2,1,0:T(8,128)(2,1)S(1)} %get-tuple-element.56), channel_id=1, source_target_pairs={{4,8},{8,4},{12,16},{16,12},{20,24},{24,20},{28,32},{32,28},{36,40... | collective-permute-start | bytes 196616 | tf_op jit(solution)/shard_map/ppermute | solution.py:545
  49.3 1.6 %copy-done.1 = bf16[128,64,64]{2,1,0:T(8,128)(2,1)S(1)} copy-done((bf16[128,64,64]{2,1,0:T(8,128)(2,1)S(1)}, bf16[128,64,64]{2,1,0:T(8,128)(2,1)}, u32[]{:S(2)}) %copy-start.1) | copy-done | bytes 1048600
  50.9 1.0 %copy-done.9 = f32[64,16,128]{2,1,0:T(8,128)S(1)} copy-done((f32[64,16,128]{2,1,0:T(8,128)S(1)}, f32[64,16,128]{2,1,0:T(8,128)}, u32[]{:S(2)}) %copy-start.9) | copy-done | bytes 524312
  52.0 2.8 %inner.1 = (f32[32,16,128]{2,1,0:T(8,128)S(1)}, bf16[64,64]{1,0:T(8,128)(2,1)S(1)}) custom-call(f32[64,16,128]{2,1,0:T(8,128)S(1)} %copy-done.9, bf16[128,64,64]{2,1,0:T(8,128)(2,1)S(1)} %copy.12.move_ref, bf16[128,64,64]{2,1,0:T(8,128)(2,1)S(1)} %copy-done.1), custom_call_target="tpu_custom_call" | custom-call | flops 268435456 | bytes 1048576 | tf_op jit(solution)/shard_map/inner/pallas_call | solution.py:551
  54.8 0.0 collective-permute-done.11.mate_ref
  54.8 0.0 collective-permute-done.12.edge_ref
  54.8 2.1 %gather.1 = (bf16[35,16,128]{2,1,0:T(8,128)(2,1)S(1)}, bf16[35,16,128]{2,1,0:T(8,128)(2,1)S(1)}, bf16[35,16,128]{2,1,0:T(8,128)(2,1)S(1)}, bf16[35,16,128]{2,1,0...) custom-call(s32[2,8,128]{2,1,0:T(8,128)S(1)} %pad_add_fusion.t0, ...), custom_call_target="tpu_custom_call" | custom-call | flops 4194304 | bytes 1048576 | tf_op jit(solution)/shard_map/gather/pallas_call | solution.py:560
  56.9 0.1 collective-permute-start.14
  57.0 1.9 %collective-permute-start.15 = (bf16[35,16,128]{2,1,0:T(8,128)(2,1)S(1)}, bf16[35,16,128]{2,1,0:T(8,128)(2,1)S(1)}, u32[]{:S(2)}, u32[]{:S(2)}) collective-permute-start(bf16[35,16,128]{2,1,0:T(8,128)(2,1)S(1)} %get-tuple-element.64), channel_id=1, source_target_pairs={{0,8},{4,12},{8,0},{12,4},{16,24},{20,28},{24,16},{28,20},{32,40},... | collective-permute-start | bytes 430088 | tf_op jit(solution)/shard_map/ppermute | solution.py:490
  58.9 0.3 collective-permute-start.16
  59.1 3.6 %collective-permute-start.17 = (bf16[35,16,128]{2,1,0:T(8,128)(2,1)S(1)}, bf16[35,16,128]{2,1,0:T(8,128)(2,1)S(1)}, u32[]{:S(2)}, u32[]{:S(2)}) collective-permute-start(bf16[35,16,128]{2,1,0:T(8,128)(2,1)S(1)} %get-tuple-element.66), channel_id=1, source_target_pairs={{0,16},{4,20},{8,24},{12,28},{16,0},{20,4},{24,8},{28,12},{32,48},... | collective-permute-start | bytes 430088 | tf_op jit(solution)/shard_map/ppermute | solution.py:490
  62.7 0.0 collective-permute-start.18
  62.7 2.4 %collective-permute-start.19 = (bf16[35,16,128]{2,1,0:T(8,128)(2,1)S(1)}, bf16[35,16,128]{2,1,0:T(8,128)(2,1)S(1)}, u32[]{:S(2)}, u32[]{:S(2)}) collective-permute-start(bf16[35,16,128]{2,1,0:T(8,128)(2,1)S(1)} %get-tuple-element.68), channel_id=1, source_target_pairs={{0,24},{4,28},{8,16},{12,20},{16,8},{20,12},{24,0},{28,4},{32,56},... | collective-permute-start | bytes 430088 | tf_op jit(solution)/shard_map/ppermute | solution.py:490
  65.1 1.9 %collective-permute-start.20 = (bf16[35,16,128]{2,1,0:T(8,128)(2,1)S(1)}, bf16[35,16,128]{2,1,0:T(8,128)(2,1)S(1)}, u32[]{:S(2)}, u32[]{:S(2)}) collective-permute-start(bf16[35,16,128]{2,1,0:T(8,128)(2,1)S(1)} %get-tuple-element.69), channel_id=1, source_target_pairs={{0,28},{4,24},{8,20},{12,16},{16,12},{20,8},{24,4},{28,0},{32,60},... | collective-permute-start | bytes 430088 | tf_op jit(solution)/shard_map/ppermute | solution.py:490
  67.0 8.7 %near0.1.rest_0_ = f32[16,8192]{1,0:T(8,128)S(1)} custom-call(s32[8,64]{1,0:T(8,128)S(1)} %bitcast.6, f32[3,2048]{1,0:T(4,128)S(1)} %copy-done.10, f32[3,2048]{1,0:T(4,128)S(1)} %collective-permute-done.8.p1, f32[3,2048]{1,0:T(4,128)S(1)} %collective-permute-done.9.p2, f32[3,2048]{1,0:T(4,128)S(1)} %collective-permute-done.10.p3, ...), custom_call_target="tpu_custom_call" | custom-call | flops 2147483648 | bytes 1048576 | tf_op jit(solution)/shard_map/near0/pallas_call | solution.py:576
  75.7 0.0 collective-permute-done.16.g3.r3
  75.8 2.9 %collective-permute-done.20.g7.r7 = bf16[35,16,128]{2,1,0:T(8,128)(2,1)S(1)} collective-permute-done((bf16[35,16,128]{2,1,0:T(8,128)(2,1)S(1)}, bf16[35,16,128]{2,1,0:T(8,128)(2,1)S(1)}, u32[]{:S(2)}, u32[]{:S(2)}) %collective-permute-start.20) | collective-permute-done | bytes 143392 | tf_op jit(solution)/shard_map/ppermute | solution.py:490
  78.6 3.2 %tree.1.local_ref = f32[32,16,128]{2,1,0:T(8,128)S(1)} custom-call(bf16[66,16,128]{2,1,0:T(8,128)(2,1)S(1)} %constant_dynamic-update-slice_fusion.pair.pair_in, bf16[35,16,128]{2,1,0:T(8,128)(2,1)S(1)} %get-tuple-element.62.g0.r0, bf16[35,16,128]{2,1,0:T(8,128)(2,1)S(1)} %collective-permute-done.14.g1.r1, ...), custom_call_target="tpu_custom_call" | custom-call | flops 67108864 | bytes 1048576 | tf_op jit(solution)/shard_map/tree/pallas_call | solution.py:594
  81.8 4.6 %final.1 = f32[16,8192]{1,0:T(8,128)} custom-call(s32[8,256]{1,0:T(8,128)S(1)} %get-tuple-element.45.plan_ref, bf16[35,16,128]{2,1,0:T(8,128)(2,1)S(1)} %get-tuple-element.62.g0.r0, bf16[35,16,128]{2,1,0:T(8,128)(2,1)S(1)} %collective-permute-done.14.g1.r1, bf16[35,16,128]{2,1,0:T(8,128)(2,1)S(1)} %collective-permute-done.15.g2.r2, ...), custom_call_target="tpu_custom_call" | custom-call | flops 134217728 | bytes 1048576 | tf_op jit(solution)/shard_map/final/pallas_call | solution.py:602
  (37 shorter events, 0.2 us)
Async XLA Ops:
  0.0 4.1 %copy-start.5 = (bf16[16,8192]{1,0:T(8,128)(2,1)S(1)}, bf16[16,8192]{1,0:T(8,128)(2,1)}, u32[]{:S(2)}) copy-start(bf16[16,8192]{1,0:T(8,128)(2,1)} %vec_ref.4) | copy-start | bytes 786436
  0.0 4.1 %copy-start.2 = (bf16[64,64,128]{2,1,0:T(8,128)(2,1)S(1)}, bf16[64,64,128]{2,1,0:T(8,128)(2,1)}, u32[]{:S(2)}) copy-start(bf16[64,64,128]{2,1,0:T(8,128)(2,1)} %basis_ref.3) | copy-start | bytes 3145732
  6.1 0.8 copy-start.8
  6.9 4.2 %collective-permute-start.4 = (bf16[33,16,128]{2,1,0:T(8,128)(2,1)S(1)}, bf16[33,16,128]{2,1,0:T(8,128)(2,1)S(1)}, u32[]{:S(2)}, u32[]{:S(2)}) collective-permute-start(bf16[33,16,128]{2,1,0:T(8,128)(2,1)S(1)} %get-tuple-element.42), channel_id=1, source_target_pairs={{0,4},{4,0},{8,12},{12,8},{16,20},{20,16},{24,28},{28,24},{32,36},... | collective-permute-start | bytes 405512 | tf_op jit(solution)/shard_map/ppermute | solution.py:490
  11.1 12.1 %copy-start.12 = (s32[256,2]{0,1:T(2,128)S(1)}, s32[256,2]{0,1:T(2,128)}, u32[]{:S(2)}) copy-start(s32[256,2]{0,1:T(2,128)} %param.19) | copy-start | bytes 6148
  11.1 12.1 %copy-start.13 = (s32[256,1]{0,1:T(1,128)S(1)}, s32[256,1]{0,1:T(1,128)}, u32[]{:S(2)}) copy-start(s32[256,1]{0,1:T(1,128)} %param.18) | copy-start | bytes 3076
  11.2 11.3 %collective-permute-start.5 = (bf16[66,16,128]{2,1,0:T(8,128)(2,1)S(1)}, bf16[66,16,128]{2,1,0:T(8,128)(2,1)}, u32[]{:S(2)}, u32[]{:S(2)}) collective-permute-start(bf16[66,16,128]{2,1,0:T(8,128)(2,1)S(1)} %constant_dynamic-update-slice_fusion.pair.pair_in), channel_id=1, source_target_pairs={{0,32},{4,228},{8,40},{12,236},{16,48},{20,244},{24,56},{28,252},{... | collective-permute-start | bytes 811016 | tf_op jit(solution)/shard_map/ppermute | solution.py:490
  22.5 11.9 %copy-start.10 = (f32[3,2048]{1,0:T(4,128)S(1)}, f32[3,2048]{1,0:T(4,128)}, u32[]{:S(2)}) copy-start(f32[3,2048]{1,0:T(4,128)} %p0.1) | copy-start | bytes 73732
  22.5 11.1 %collective-permute-start.6 = (bf16[66,16,128]{2,1,0:T(8,128)(2,1)}, bf16[66,16,128]{2,1,0:T(8,128)(2,1)}, u32[]{:S(2)}, u32[]{:S(2)}) collective-permute-start(bf16[66,16,128]{2,1,0:T(8,128)(2,1)} %collective-permute-done.5.r1), channel_id=1, source_target_pairs={{0,32},{4,228},{8,40},{12,236},{16,48},{20,244},{24,56},{28,252},{... | collective-permute-start | bytes 811016 | tf_op jit(solution)/shard_map/ppermute | solution.py:490
  23.7 1.3 %collective-permute-start = (s32[8,128]{1,0:T(8,128)S(1)}, s32[8,128]{1,0:T(8,128)S(1)}, u32[]{:S(2)}, u32[]{:S(2)}) collective-permute-start(s32[8,128]{1,0:T(8,128)S(1)} %get-tuple-element.46), channel_id=1, source_target_pairs={{0,4},{4,0},{8,12},{12,8},{16,20},{20,16},{24,28},{28,24},{32,36},... | collective-permute-start | bytes 12296 | tf_op jit(solution)/shard_map/ppermute | solution.py:490
  24.9 8.6 %collective-permute-start.1 = (s32[2,8,128]{2,1,0:T(8,128)S(1)}, s32[2,8,128]{2,1,0:T(8,128)S(1)}, u32[]{:S(2)}, u32[]{:S(2)}) collective-permute-start(s32[2,8,128]{2,1,0:T(8,128)S(1)} %pad_add_fusion.t0), channel_id=1, source_target_pairs={{0,8},{4,12},{8,0},{12,4},{16,24},{20,28},{24,16},{28,20},{32,40},... | collective-permute-start | bytes 24584 | tf_op jit(solution)/shard_map/ppermute | solution.py:490
  26.1 7.4 %collective-permute-start.2 = (s32[2,8,128]{2,1,0:T(8,128)S(1)}, s32[2,8,128]{2,1,0:T(8,128)S(1)}, u32[]{:S(2)}, u32[]{:S(2)}) collective-permute-start(s32[2,8,128]{2,1,0:T(8,128)S(1)} %pad_add_fusion.t0), channel_id=1, source_target_pairs={{0,16},{4,20},{8,24},{12,28},{16,0},{20,4},{24,8},{28,12},{32,48},... | collective-permute-start | bytes 24584 | tf_op jit(solution)/shard_map/ppermute | solution.py:490
  28.6 5.0 %collective-permute-start.3 = (s32[2,8,128]{2,1,0:T(8,128)S(1)}, s32[2,8,128]{2,1,0:T(8,128)S(1)}, u32[]{:S(2)}, u32[]{:S(2)}) collective-permute-start(s32[2,8,128]{2,1,0:T(8,128)S(1)} %pad_add_fusion.t0), channel_id=1, source_target_pairs={{0,24},{4,28},{8,16},{12,20},{16,8},{20,12},{24,0},{28,4},{32,56},... | collective-permute-start | bytes 24584 | tf_op jit(solution)/shard_map/ppermute | solution.py:490
  33.6 8.5 %collective-permute-start.7 = (bf16[66,16,128]{2,1,0:T(8,128)(2,1)}, bf16[66,16,128]{2,1,0:T(8,128)(2,1)S(1)}, u32[]{:S(2)}, u32[]{:S(2)}) collective-permute-start(bf16[66,16,128]{2,1,0:T(8,128)(2,1)} %collective-permute-done.6.r2), channel_id=1, source_target_pairs={{0,32},{4,228},{8,40},{12,236},{16,48},{20,244},{24,56},{28,252},{... | collective-permute-start | bytes 811016 | tf_op jit(solution)/shard_map/ppermute | solution.py:490
  34.4 3.8 %collective-permute-start.8 = (f32[3,2048]{1,0:T(4,128)S(1)}, f32[3,2048]{1,0:T(4,128)S(1)}, u32[]{:S(2)}, u32[]{:S(2)}) collective-permute-start(f32[3,2048]{1,0:T(4,128)S(1)} %copy-done.10), channel_id=1, source_target_pairs={{1,0},{2,1},{3,2},{0,3},{5,4},{6,5},{7,6},{4,7},{9,8},{10,9},{11,1... | collective-permute-start | bytes 73736 | tf_op jit(solution)/shard_map/ppermute | solution.py:537
  37.1 4.3 %collective-permute-start.9 = (f32[3,2048]{1,0:T(4,128)S(1)}, f32[3,2048]{1,0:T(4,128)S(1)}, u32[]{:S(2)}, u32[]{:S(2)}) collective-permute-start(f32[3,2048]{1,0:T(4,128)S(1)} %copy-done.10), channel_id=1, source_target_pairs={{2,0},{3,1},{0,2},{1,3},{6,4},{7,5},{4,6},{5,7},{10,8},{11,9},{8,1... | collective-permute-start | bytes 73736 | tf_op jit(solution)/shard_map/ppermute | solution.py:537
  37.5 4.6 %collective-permute-start.10 = (f32[3,2048]{1,0:T(4,128)S(1)}, f32[3,2048]{1,0:T(4,128)S(1)}, u32[]{:S(2)}, u32[]{:S(2)}) collective-permute-start(f32[3,2048]{1,0:T(4,128)S(1)} %copy-done.10), channel_id=1, source_target_pairs={{3,0},{0,1},{1,2},{2,3},{7,4},{4,5},{5,6},{6,7},{11,8},{8,9},{9,10... | collective-permute-start | bytes 73736 | tf_op jit(solution)/shard_map/ppermute | solution.py:537
  42.0 12.8 %collective-permute-start.13 = (bf16[33,16,128]{2,1,0:T(8,128)(2,1)S(1)}, bf16[33,16,128]{2,1,0:T(8,128)(2,1)S(1)}, u32[]{:S(2)}, u32[]{:S(2)}) collective-permute-start(bf16[33,16,128]{2,1,0:T(8,128)(2,1)S(1)} %slice.3), channel_id=1, source_target_pairs={{0,32},{4,228},{8,40},{12,236},{16,48},{20,244},{24,56},{28,252},{... | collective-permute-start | bytes 405512 | tf_op jit(solution)/shard_map/ppermute | solution.py:490
  42.6 0.9 %copy-start.6 = (bf16[16,8192]{1,0:T(8,128)(2,1)S(1)}, bf16[16,8192]{1,0:T(8,128)(2,1)}, u32[]{:S(2)}) copy-start(bf16[16,8192]{1,0:T(8,128)(2,1)} %vec_ref.4) | copy-start | bytes 786436
  43.6 11.2 %collective-permute-start.11 = (bf16[16,16,128]{2,1,0:T(8,128)(2,1)S(1)}, bf16[16,16,128]{2,1,0:T(8,128)(2,1)S(1)}, u32[]{:S(2)}, u32[]{:S(2)}) collective-permute-start(bf16[16,16,128]{2,1,0:T(8,128)(2,1)S(1)} %get-tuple-element.55), channel_id=1, source_target_pairs={{0,4},{4,0},{8,12},{12,8},{16,20},{20,16},{24,28},{28,24},{32,36},... | collective-permute-start | bytes 196616 | tf_op jit(solution)/shard_map/ppermute | solution.py:490
  47.4 7.4 %collective-permute-start.12 = (bf16[16,16,128]{2,1,0:T(8,128)(2,1)S(1)}, bf16[16,16,128]{2,1,0:T(8,128)(2,1)S(1)}, u32[]{:S(2)}, u32[]{:S(2)}) collective-permute-start(bf16[16,16,128]{2,1,0:T(8,128)(2,1)S(1)} %get-tuple-element.56), channel_id=1, source_target_pairs={{4,8},{8,4},{12,16},{16,12},{20,24},{24,20},{28,32},{32,28},{36,40... | collective-permute-start | bytes 196616 | tf_op jit(solution)/shard_map/ppermute | solution.py:545
  49.3 1.6 %copy-start.1 = (bf16[128,64,64]{2,1,0:T(8,128)(2,1)S(1)}, bf16[128,64,64]{2,1,0:T(8,128)(2,1)}, u32[]{:S(2)}) copy-start(bf16[128,64,64]{2,1,0:T(8,128)(2,1)} %copy.14.pair_ref) | copy-start | bytes 3145732
  50.9 1.0 %copy-start.9 = (f32[64,16,128]{2,1,0:T(8,128)S(1)}, f32[64,16,128]{2,1,0:T(8,128)}, u32[]{:S(2)}) copy-start(f32[64,16,128]{2,1,0:T(8,128)} %copy-done.8) | copy-start | bytes 1572868
  52.0 15.1 %copy-start.7 = (bf16[16,8192]{1,0:T(8,128)(2,1)S(1)}, bf16[16,8192]{1,0:T(8,128)(2,1)}, u32[]{:S(2)}) copy-start(bf16[16,8192]{1,0:T(8,128)(2,1)} %vec_ref.4) | copy-start | bytes 786436
  52.0 15.1 %copy-start.11 = (s32[64,8]{0,1:T(8,128)S(1)}, s32[64,8]{0,1:T(8,128)}, u32[]{:S(2)}) copy-start(s32[64,8]{0,1:T(8,128)} %param.21) | copy-start | bytes 6148
  56.9 5.8 %collective-permute-start.14 = (bf16[35,16,128]{2,1,0:T(8,128)(2,1)S(1)}, bf16[35,16,128]{2,1,0:T(8,128)(2,1)S(1)}, u32[]{:S(2)}, u32[]{:S(2)}) collective-permute-start(bf16[35,16,128]{2,1,0:T(8,128)(2,1)S(1)} %get-tuple-element.63), channel_id=1, source_target_pairs={{0,4},{4,0},{8,12},{12,8},{16,20},{20,16},{24,28},{28,24},{32,36},... | collective-permute-start | bytes 430088 | tf_op jit(solution)/shard_map/ppermute | solution.py:490
  57.0 8.1 %collective-permute-start.15 = (bf16[35,16,128]{2,1,0:T(8,128)(2,1)S(1)}, bf16[35,16,128]{2,1,0:T(8,128)(2,1)S(1)}, u32[]{:S(2)}, u32[]{:S(2)}) collective-permute-start(bf16[35,16,128]{2,1,0:T(8,128)(2,1)S(1)} %get-tuple-element.64), channel_id=1, source_target_pairs={{0,8},{4,12},{8,0},{12,4},{16,24},{20,28},{24,16},{28,20},{32,40},... | collective-permute-start | bytes 430088 | tf_op jit(solution)/shard_map/ppermute | solution.py:490
  58.9 16.9 %collective-permute-start.16 = (bf16[35,16,128]{2,1,0:T(8,128)(2,1)S(1)}, bf16[35,16,128]{2,1,0:T(8,128)(2,1)S(1)}, u32[]{:S(2)}, u32[]{:S(2)}) collective-permute-start(bf16[35,16,128]{2,1,0:T(8,128)(2,1)S(1)} %get-tuple-element.65), channel_id=1, source_target_pairs={{0,12},{4,8},{8,4},{12,0},{16,28},{20,24},{24,20},{28,16},{32,44},... | collective-permute-start | bytes 430088 | tf_op jit(solution)/shard_map/ppermute | solution.py:490
  59.1 16.6 %collective-permute-start.17 = (bf16[35,16,128]{2,1,0:T(8,128)(2,1)S(1)}, bf16[35,16,128]{2,1,0:T(8,128)(2,1)S(1)}, u32[]{:S(2)}, u32[]{:S(2)}) collective-permute-start(bf16[35,16,128]{2,1,0:T(8,128)(2,1)S(1)} %get-tuple-element.66), channel_id=1, source_target_pairs={{0,16},{4,20},{8,24},{12,28},{16,0},{20,4},{24,8},{28,12},{32,48},... | collective-permute-start | bytes 430088 | tf_op jit(solution)/shard_map/ppermute | solution.py:490
  62.7 13.1 %collective-permute-start.18 = (bf16[35,16,128]{2,1,0:T(8,128)(2,1)S(1)}, bf16[35,16,128]{2,1,0:T(8,128)(2,1)S(1)}, u32[]{:S(2)}, u32[]{:S(2)}) collective-permute-start(bf16[35,16,128]{2,1,0:T(8,128)(2,1)S(1)} %get-tuple-element.67), channel_id=1, source_target_pairs={{0,20},{4,16},{8,28},{12,24},{16,4},{20,0},{24,12},{28,8},{32,52},... | collective-permute-start | bytes 430088 | tf_op jit(solution)/shard_map/ppermute | solution.py:490
  62.7 13.1 %collective-permute-start.19 = (bf16[35,16,128]{2,1,0:T(8,128)(2,1)S(1)}, bf16[35,16,128]{2,1,0:T(8,128)(2,1)S(1)}, u32[]{:S(2)}, u32[]{:S(2)}) collective-permute-start(bf16[35,16,128]{2,1,0:T(8,128)(2,1)S(1)} %get-tuple-element.68), channel_id=1, source_target_pairs={{0,24},{4,28},{8,16},{12,20},{16,8},{20,12},{24,0},{28,4},{32,56},... | collective-permute-start | bytes 430088 | tf_op jit(solution)/shard_map/ppermute | solution.py:490
  65.1 13.5 %copy-start.3 = (bf16[64,64,64]{2,1,0:T(8,128)(2,1)S(1)}, bf16[64,64,64]{2,1,0:T(8,128)(2,1)}, u32[]{:S(2)}) copy-start(bf16[64,64,64]{2,1,0:T(8,128)(2,1)} %upper_t_ref.1) | copy-start | bytes 1572868
  65.1 13.5 %copy-start.4 = (bf16[64,64,64]{2,1,0:T(8,128)(2,1)S(1)}, bf16[64,64,64]{2,1,0:T(8,128)(2,1)}, u32[]{:S(2)}) copy-start(bf16[64,64,64]{2,1,0:T(8,128)(2,1)} %upper_c_ref.1) | copy-start | bytes 1572868
  65.1 13.5 %collective-permute-start.20 = (bf16[35,16,128]{2,1,0:T(8,128)(2,1)S(1)}, bf16[35,16,128]{2,1,0:T(8,128)(2,1)S(1)}, u32[]{:S(2)}, u32[]{:S(2)}) collective-permute-start(bf16[35,16,128]{2,1,0:T(8,128)(2,1)S(1)} %get-tuple-element.69), channel_id=1, source_target_pairs={{0,28},{4,24},{8,20},{12,16},{16,12},{20,8},{24,4},{28,0},{32,60},... | collective-permute-start | bytes 430088 | tf_op jit(solution)/shard_map/ppermute | solution.py:490
  78.6 3.2 %copy-start = (bf16[256,64,64]{2,1,0:T(8,128)(2,1)S(1)}, bf16[256,64,64]{2,1,0:T(8,128)(2,1)}, u32[]{:S(2)}) copy-start(bf16[256,64,64]{2,1,0:T(8,128)(2,1)} %copy.13.block_ref) | copy-start | bytes 6291460

commit v5 on v4

--- a/solution.py
+++ b/solution.py
@@ -536,7 +536,7 @@
     turns = [points] + [
         lax.ppermute(points, "vec", [((i + s) % n_vec, i) for i in range(n_vec)]) for s in range(1, n_vec)
     ]
-    ring4 = permute(after(ring3, turns)[:OWN_TILES], onward)
+    ring4 = permute(ring3[:OWN_TILES], onward)
     give, edge = _call(
         _edges_kernel, [tiles(2 * REACH), tiles(2 * REACH)], 5, flops=1 << 22, name="edges"
     )(*turns, vectors)
@@ -554,7 +554,7 @@
         3,
         flops=1 << 28,
         name="inner",
-    )(after(nodes, ring3), local_transfer, local_coupling)
+    )(after(nodes, ring2), local_transfer, local_coupling)
 
 
     rows = _call(

time: 87 us -> 91.7 us (1.054)
  waiting for transfers between devices: 8.9 us -> 12.4 us
  starting transfers between devices: 32.8 us -> 34.1 us
    ppermute x17, waiting for transfers between devices: 5.02 us -> 10.2 us  [permute(): return lax.ppermute(x, 'leaf', [(i, to(i)) for i in everyone])]
    ppermute x3, waiting for transfers between devices: 3.87 us -> 2.14 us  [per_device(): lax.ppermute(points, 'vec', [((i + s) % n_vec, i) for i in range(n_vec)])]
    ppermute x3, starting transfers between devices: 3.77 us -> 4.99 us  [per_device(): lax.ppermute(points, 'vec', [((i + s) % n_vec, i) for i in range(n_vec)])]
    ppermute x1, starting transfers between devices: 1.91 us -> 3.02 us  [per_device(): lax.ppermute(edge, 'leaf', [(i, i - 1 + 2 * (i % 2)) for i in range(n_lea...]
    ppermute x17, starting transfers between devices: 27.1 us -> 26.1 us  [permute(): return lax.ppermute(x, 'leaf', [(i, to(i)) for i in everyone])]
  transfers between devices with their start and end apart: 21 -> 21, of which waited for: 5 -> 6; matrix products, arithmetic and copies ran while one was open for 14% -> 13% of each run, Pallas kernels for 14% -> 13%
where the time goes in v5:
time: 91.7 us; the launch traced here: 91.2 us
  starting transfers between devices  34.1 us (37%)
  Pallas kernels  23.9 us (26%)
  local copies, waits for them, and re-layouts  20.7 us (23%)
  waiting for transfers between devices  12.4 us (14%)
    ppermute x17, starting transfers between devices, permute(): return lax.ppermute(x, 'leaf', [(i, to(i)) for i in everyone])  26.1 us
    optimization_barrier x2, local copies, waits for them, and re-layouts, after(): return lax.optimization_barrier((x, done))[0]  12.2 us
    ppermute x17, waiting for transfers between devices, permute(): return lax.ppermute(x, 'leaf', [(i, to(i)) for i in everyone])  10.2 us
    pallas_call x1, Pallas kernels, near_part(): _call(functools.partial(_near_kernel, part, NEAR_PARTS), _shape((vectors....  8.67 us
    unnamed x30, local copies, waits for them, and re-layouts  8.48 us
    ppermute x3, starting transfers between devices, per_device(): lax.ppermute(points, 'vec', [((i + s) % n_vec, i) for i in range(n_vec)])  4.99 us
    pallas_call x1, Pallas kernels, per_device(): _call(_final_kernel, _shape(vectors.shape, F32), 12 + NEAR_PARTS, smem=(0...  4.61 us
    pallas_call x1, Pallas kernels, per_device(): _call(_tree_kernel, tiles(LEAF_TILES, F32), 14, scratch=[pltpu.VMEM((GROU...  3.23 us
  transfers between devices with their start and end apart: 21, of which 6 were waited for; matrix products, arithmetic and copies ran while one was open for 13% of the time, Pallas kernels for 13%

profile of v5, /device:TPU:1, one launch (start us, length us, event | category | flops | bytes accessed | tf_op | source)
XLA Modules:
  0.0 91.2 jit_solution(9100936188681635629)
XLA Ops:
  0.0 4.0 %copy.12.move_ref = bf16[128,64,64]{2,1,0:T(8,128)(2,1)S(1)} copy(bf16[128,64,64]{0,2,1:T(8,128)(2,1)} %param.14) | data formatting | bytes 2097152 | tf_op args[3]
  4.1 2.0 %prepare.1 = (bf16[33,16,128]{2,1,0:T(8,128)(2,1)S(1)}, f32[64,16,128]{2,1,0:T(8,128)S(1)}) custom-call(bf16[16,8192]{1,0:T(8,128)(2,1)S(1)} %copy-done.5, bf16[64,64,128]{2,1,0:T(8,128)(2,1)S(1)} %copy-done.2, bf16[128,64,64]{2,1,0:T(8,128)(2,1)S(1)} %copy.12.move_ref), custom_call_target="tpu_custom_call" | custom-call | flops 67108864 | bytes 1048576 | tf_op jit(solution)/shard_map/prepare/pallas_call | solution.py:501
  6.1 0.8 copy-done.8
  6.9 3.2 %collective-permute-start.4 = (bf16[33,16,128]{2,1,0:T(8,128)(2,1)S(1)}, bf16[33,16,128]{2,1,0:T(8,128)(2,1)S(1)}, u32[]{:S(2)}, u32[]{:S(2)}) collective-permute-start(bf16[33,16,128]{2,1,0:T(8,128)(2,1)S(1)} %get-tuple-element.41), channel_id=1, source_target_pairs={{0,4},{4,0},{8,12},{12,8},{16,20},{20,16},{24,28},{28,24},{32,36},... | collective-permute-start | bytes 405512 | tf_op jit(solution)/shard_map/ppermute | solution.py:490
  10.1 1.0 %collective-permute-done.4 = bf16[33,16,128]{2,1,0:T(8,128)(2,1)S(1)} collective-permute-done((bf16[33,16,128]{2,1,0:T(8,128)(2,1)S(1)}, bf16[33,16,128]{2,1,0:T(8,128)(2,1)S(1)}, u32[]{:S(2)}, u32[]{:S(2)}) %collective-permute-start.4) | collective-permute-done | bytes 135200 | tf_op jit(solution)/shard_map/ppermute | solution.py:490
  11.1 0.0 copy-start.12
  11.1 0.0 copy-start.13
  11.2 3.9 %collective-permute-start.5 = (bf16[66,16,128]{2,1,0:T(8,128)(2,1)S(1)}, bf16[66,16,128]{2,1,0:T(8,128)(2,1)}, u32[]{:S(2)}, u32[]{:S(2)}) collective-permute-start(bf16[66,16,128]{2,1,0:T(8,128)(2,1)S(1)} %constant_dynamic-update-slice_fusion.pair.pair_in), channel_id=1, source_target_pairs={{0,32},{4,228},{8,40},{12,236},{16,48},{20,244},{24,56},{28,252},{... | collective-permute-start | bytes 811016 | tf_op jit(solution)/shard_map/ppermute | solution.py:490
  15.1 7.4 %copy.13.block_ref = bf16[256,64,64]{2,1,0:T(8,128)(2,1)} copy(bf16[256,64,64]{0,2,1:T(8,128)(2,1)} %param.20) | data formatting | bytes 4194304 | tf_op jit(solution)/shard_map/optimization_barrier | solution.py:493
  22.5 0.0 collective-permute-done.5.r1
  22.5 0.7 collective-permute-start.6
  23.2 0.4 request.1
  23.7 0.1 collective-permute-start
  23.8 1.2 %collective-permute-done = s32[8,128]{1,0:T(8,128)S(1)} collective-permute-done((s32[8,128]{1,0:T(8,128)S(1)}, s32[8,128]{1,0:T(8,128)S(1)}, u32[]{:S(2)}, u32[]{:S(2)}) %collective-permute-start) | collective-permute-done | bytes 4128 | tf_op jit(solution)/shard_map/ppermute | solution.py:490
  24.9 2.5 %collective-permute-start.3 = (s32[2,8,128]{2,1,0:T(8,128)S(1)}, s32[2,8,128]{2,1,0:T(8,128)S(1)}, u32[]{:S(2)}, u32[]{:S(2)}) collective-permute-start(s32[2,8,128]{2,1,0:T(8,128)S(1)} %pad_add_fusion.t0), channel_id=1, source_target_pairs={{0,24},{4,28},{8,16},{12,20},{16,8},{20,12},{24,0},{28,4},{32,56},... | collective-permute-start | bytes 24584 | tf_op jit(solution)/shard_map/ppermute | solution.py:490
  27.4 0.5 collective-permute-start.2
  27.9 0.3 collective-permute-start.1
  28.2 4.8 %copy.14.pair_ref = bf16[128,64,64]{2,1,0:T(8,128)(2,1)} copy(bf16[128,64,64]{0,2,1:T(8,128)(2,1)} %param.15) | data formatting | bytes 2097152 | tf_op jit(solution)/shard_map/optimization_barrier | solution.py:493
  33.0 0.0 collective-permute-done.6.r2
  33.0 0.8 collective-permute-start.12
  33.8 5.1 %collective-permute-done.12.r3 = bf16[66,16,128]{2,1,0:T(8,128)(2,1)S(1)} collective-permute-done((bf16[66,16,128]{2,1,0:T(8,128)(2,1)}, bf16[66,16,128]{2,1,0:T(8,128)(2,1)S(1)}, u32[]{:S(2)}, u32[]{:S(2)}) %collective-permute-start.12) | collective-permute-done | bytes 270368 | tf_op jit(solution)/shard_map/ppermute | solution.py:490
  38.9 1.7 %collective-permute-start.13 = (bf16[33,16,128]{2,1,0:T(8,128)(2,1)S(1)}, bf16[33,16,128]{2,1,0:T(8,128)(2,1)S(1)}, u32[]{:S(2)}, u32[]{:S(2)}) collective-permute-start(bf16[33,16,128]{2,1,0:T(8,128)(2,1)S(1)} %slice.4), channel_id=1, source_target_pairs={{0,32},{4,228},{8,40},{12,236},{16,48},{20,244},{24,56},{28,252},{... | collective-permute-start | bytes 405512 | tf_op jit(solution)/shard_map/ppermute | solution.py:490
  40.6 1.3 %collective-permute-start.9 = (f32[3,2048]{1,0:T(4,128)S(1)}, f32[3,2048]{1,0:T(4,128)S(1)}, u32[]{:S(2)}, u32[]{:S(2)}) collective-permute-start(f32[3,2048]{1,0:T(4,128)S(1)} %copy-done.10), channel_id=1, source_target_pairs={{3,0},{0,1},{1,2},{2,3},{7,4},{4,5},{5,6},{6,7},{11,8},{8,9},{9,10... | collective-permute-start | bytes 73736 | tf_op jit(solution)/shard_map/ppermute | solution.py:537
  41.9 2.6 %collective-permute-start.8 = (f32[3,2048]{1,0:T(4,128)S(1)}, f32[3,2048]{1,0:T(4,128)S(1)}, u32[]{:S(2)}, u32[]{:S(2)}) collective-permute-start(f32[3,2048]{1,0:T(4,128)S(1)} %copy-done.10), channel_id=1, source_target_pairs={{2,0},{3,1},{0,2},{1,3},{6,4},{7,5},{4,6},{5,7},{10,8},{11,9},{8,1... | collective-permute-start | bytes 73736 | tf_op jit(solution)/shard_map/ppermute | solution.py:537
  44.5 1.1 %collective-permute-start.7 = (f32[3,2048]{1,0:T(4,128)S(1)}, f32[3,2048]{1,0:T(4,128)S(1)}, u32[]{:S(2)}, u32[]{:S(2)}) collective-permute-start(f32[3,2048]{1,0:T(4,128)S(1)} %copy-done.10), channel_id=1, source_target_pairs={{1,0},{2,1},{3,2},{0,3},{5,4},{6,5},{7,6},{4,7},{9,8},{10,9},{11,1... | collective-permute-start | bytes 73736 | tf_op jit(solution)/shard_map/ppermute | solution.py:537
  45.6 0.6 collective-permute-done.8.p2
  46.2 1.6 %collective-permute-done.7.p1 = f32[3,2048]{1,0:T(4,128)S(1)} collective-permute-done((f32[3,2048]{1,0:T(4,128)S(1)}, f32[3,2048]{1,0:T(4,128)S(1)}, u32[]{:S(2)}, u32[]{:S(2)}) %collective-permute-start.7) | collective-permute-done | bytes 24608 | tf_op jit(solution)/shard_map/ppermute | solution.py:537
  47.7 0.9 %copy-done.6 = bf16[16,8192]{1,0:T(8,128)(2,1)S(1)} copy-done((bf16[16,8192]{1,0:T(8,128)(2,1)S(1)}, bf16[16,8192]{1,0:T(8,128)(2,1)}, u32[]{:S(2)}) %copy-start.6) | copy-done | bytes 262168
  48.7 2.9 %collective-permute-start.10 = (bf16[16,16,128]{2,1,0:T(8,128)(2,1)S(1)}, bf16[16,16,128]{2,1,0:T(8,128)(2,1)S(1)}, u32[]{:S(2)}, u32[]{:S(2)}) collective-permute-start(bf16[16,16,128]{2,1,0:T(8,128)(2,1)S(1)} %get-tuple-element.53), channel_id=1, source_target_pairs={{0,4},{4,0},{8,12},{12,8},{16,20},{20,16},{24,28},{28,24},{32,36},... | collective-permute-start | bytes 196616 | tf_op jit(solution)/shard_map/ppermute | solution.py:490
  51.6 3.0 %collective-permute-start.11 = (bf16[16,16,128]{2,1,0:T(8,128)(2,1)S(1)}, bf16[16,16,128]{2,1,0:T(8,128)(2,1)S(1)}, u32[]{:S(2)}, u32[]{:S(2)}) collective-permute-start(bf16[16,16,128]{2,1,0:T(8,128)(2,1)S(1)} %get-tuple-element.54), channel_id=1, source_target_pairs={{4,8},{8,4},{12,16},{16,12},{20,24},{24,20},{28,32},{32,28},{36,40... | collective-permute-start | bytes 196616 | tf_op jit(solution)/shard_map/ppermute | solution.py:545
  54.6 1.6 %copy-done.1 = bf16[128,64,64]{2,1,0:T(8,128)(2,1)S(1)} copy-done((bf16[128,64,64]{2,1,0:T(8,128)(2,1)S(1)}, bf16[128,64,64]{2,1,0:T(8,128)(2,1)}, u32[]{:S(2)}) %copy-start.1) | copy-done | bytes 1048600
  56.2 1.0 %copy-done.9 = f32[64,16,128]{2,1,0:T(8,128)S(1)} copy-done((f32[64,16,128]{2,1,0:T(8,128)S(1)}, f32[64,16,128]{2,1,0:T(8,128)}, u32[]{:S(2)}) %copy-start.9) | copy-done | bytes 524312
  57.3 2.8 %inner.1 = (f32[32,16,128]{2,1,0:T(8,128)S(1)}, bf16[64,64]{1,0:T(8,128)(2,1)S(1)}) custom-call(f32[64,16,128]{2,1,0:T(8,128)S(1)} %copy-done.9, bf16[128,64,64]{2,1,0:T(8,128)(2,1)S(1)} %copy.12.move_ref, bf16[128,64,64]{2,1,0:T(8,128)(2,1)S(1)} %copy-done.1), custom_call_target="tpu_custom_call" | custom-call | flops 268435456 | bytes 1048576 | tf_op jit(solution)/shard_map/inner/pallas_call | solution.py:551
  60.1 0.0 collective-permute-done.10.mate_ref
  60.1 0.0 collective-permute-done.11.edge_ref
  60.1 2.1 %gather.1 = (bf16[35,16,128]{2,1,0:T(8,128)(2,1)S(1)}, bf16[35,16,128]{2,1,0:T(8,128)(2,1)S(1)}, bf16[35,16,128]{2,1,0:T(8,128)(2,1)S(1)}, bf16[35,16,128]{2,1,0...) custom-call(s32[2,8,128]{2,1,0:T(8,128)S(1)} %pad_add_fusion.t0, ...), custom_call_target="tpu_custom_call" | custom-call | flops 4194304 | bytes 1048576 | tf_op jit(solution)/shard_map/gather/pallas_call | solution.py:560
  62.2 0.1 collective-permute-start.14
  62.3 1.3 %collective-permute-start.15 = (bf16[35,16,128]{2,1,0:T(8,128)(2,1)S(1)}, bf16[35,16,128]{2,1,0:T(8,128)(2,1)S(1)}, u32[]{:S(2)}, u32[]{:S(2)}) collective-permute-start(bf16[35,16,128]{2,1,0:T(8,128)(2,1)S(1)} %get-tuple-element.62), channel_id=1, source_target_pairs={{0,8},{4,12},{8,0},{12,4},{16,24},{20,28},{24,16},{28,20},{32,40},... | collective-permute-start | bytes 430088 | tf_op jit(solution)/shard_map/ppermute | solution.py:490
  63.6 0.8 collective-permute-start.16
  64.4 2.5 %collective-permute-start.17 = (bf16[35,16,128]{2,1,0:T(8,128)(2,1)S(1)}, bf16[35,16,128]{2,1,0:T(8,128)(2,1)S(1)}, u32[]{:S(2)}, u32[]{:S(2)}) collective-permute-start(bf16[35,16,128]{2,1,0:T(8,128)(2,1)S(1)} %get-tuple-element.64), channel_id=1, source_target_pairs={{0,16},{4,20},{8,24},{12,28},{16,0},{20,4},{24,8},{28,12},{32,48},... | collective-permute-start | bytes 430088 | tf_op jit(solution)/shard_map/ppermute | solution.py:490
  66.9 0.6 collective-permute-start.18
  67.5 2.3 %collective-permute-start.19 = (bf16[35,16,128]{2,1,0:T(8,128)(2,1)S(1)}, bf16[35,16,128]{2,1,0:T(8,128)(2,1)S(1)}, u32[]{:S(2)}, u32[]{:S(2)}) collective-permute-start(bf16[35,16,128]{2,1,0:T(8,128)(2,1)S(1)} %get-tuple-element.66), channel_id=1, source_target_pairs={{0,24},{4,28},{8,16},{12,20},{16,8},{20,12},{24,0},{28,4},{32,56},... | collective-permute-start | bytes 430088 | tf_op jit(solution)/shard_map/ppermute | solution.py:490
  69.8 1.9 %collective-permute-start.20 = (bf16[35,16,128]{2,1,0:T(8,128)(2,1)S(1)}, bf16[35,16,128]{2,1,0:T(8,128)(2,1)S(1)}, u32[]{:S(2)}, u32[]{:S(2)}) collective-permute-start(bf16[35,16,128]{2,1,0:T(8,128)(2,1)S(1)} %get-tuple-element.67), channel_id=1, source_target_pairs={{0,28},{4,24},{8,20},{12,16},{16,12},{20,8},{24,4},{28,0},{32,60},... | collective-permute-start | bytes 430088 | tf_op jit(solution)/shard_map/ppermute | solution.py:490
  71.7 8.7 %near0.1.rest_0_ = f32[16,8192]{1,0:T(8,128)S(1)} custom-call(s32[8,64]{1,0:T(8,128)S(1)} %bitcast.6, f32[3,2048]{1,0:T(4,128)S(1)} %copy-done.10, f32[3,2048]{1,0:T(4,128)S(1)} %collective-permute-done.7.p1, f32[3,2048]{1,0:T(4,128)S(1)} %collective-permute-done.8.p2, f32[3,2048]{1,0:T(4,128)S(1)} %collective-permute-done.9.p3, ...), custom_call_target="tpu_custom_call" | custom-call | flops 2147483648 | bytes 1048576 | tf_op jit(solution)/shard_map/near0/pallas_call | solution.py:576
  80.4 0.0 collective-permute-done.16.g3.r3
  80.4 3.0 %collective-permute-done.20.g7.r7 = bf16[35,16,128]{2,1,0:T(8,128)(2,1)S(1)} collective-permute-done((bf16[35,16,128]{2,1,0:T(8,128)(2,1)S(1)}, bf16[35,16,128]{2,1,0:T(8,128)(2,1)S(1)}, u32[]{:S(2)}, u32[]{:S(2)}) %collective-permute-start.20) | collective-permute-done | bytes 143392 | tf_op jit(solution)/shard_map/ppermute | solution.py:490
  83.4 3.2 %tree.1.local_ref = f32[32,16,128]{2,1,0:T(8,128)S(1)} custom-call(bf16[66,16,128]{2,1,0:T(8,128)(2,1)S(1)} %constant_dynamic-update-slice_fusion.pair.pair_in, bf16[35,16,128]{2,1,0:T(8,128)(2,1)S(1)} %get-tuple-element.60.g0.r0, bf16[35,16,128]{2,1,0:T(8,128)(2,1)S(1)} %collective-permute-done.14.g1.r1, ...), custom_call_target="tpu_custom_call" | custom-call | flops 67108864 | bytes 1048576 | tf_op jit(solution)/shard_map/tree/pallas_call | solution.py:594
  86.6 4.6 %final.1 = f32[16,8192]{1,0:T(8,128)} custom-call(s32[8,256]{1,0:T(8,128)S(1)} %get-tuple-element.44.plan_ref, bf16[35,16,128]{2,1,0:T(8,128)(2,1)S(1)} %get-tuple-element.60.g0.r0, bf16[35,16,128]{2,1,0:T(8,128)(2,1)S(1)} %collective-permute-done.14.g1.r1, bf16[35,16,128]{2,1,0:T(8,128)(2,1)S(1)} %collective-permute-done.15.g2.r2, ...), custom_call_target="tpu_custom_call" | custom-call | flops 134217728 | bytes 1048576 | tf_op jit(solution)/shard_map/final/pallas_call | solution.py:602
  (37 shorter events, 0.2 us)
Async XLA Ops:
  0.0 4.1 %copy-start.5 = (bf16[16,8192]{1,0:T(8,128)(2,1)S(1)}, bf16[16,8192]{1,0:T(8,128)(2,1)}, u32[]{:S(2)}) copy-start(bf16[16,8192]{1,0:T(8,128)(2,1)} %vec_ref.4) | copy-start | bytes 786436
  0.0 4.1 %copy-start.2 = (bf16[64,64,128]{2,1,0:T(8,128)(2,1)S(1)}, bf16[64,64,128]{2,1,0:T(8,128)(2,1)}, u32[]{:S(2)}) copy-start(bf16[64,64,128]{2,1,0:T(8,128)(2,1)} %basis_ref.3) | copy-start | bytes 3145732
  6.1 0.8 copy-start.8
  6.9 4.2 %collective-permute-start.4 = (bf16[33,16,128]{2,1,0:T(8,128)(2,1)S(1)}, bf16[33,16,128]{2,1,0:T(8,128)(2,1)S(1)}, u32[]{:S(2)}, u32[]{:S(2)}) collective-permute-start(bf16[33,16,128]{2,1,0:T(8,128)(2,1)S(1)} %get-tuple-element.41), channel_id=1, source_target_pairs={{0,4},{4,0},{8,12},{12,8},{16,20},{20,16},{24,28},{28,24},{32,36},... | collective-permute-start | bytes 405512 | tf_op jit(solution)/shard_map/ppermute | solution.py:490
  11.1 12.1 %copy-start.12 = (s32[256,2]{0,1:T(2,128)S(1)}, s32[256,2]{0,1:T(2,128)}, u32[]{:S(2)}) copy-start(s32[256,2]{0,1:T(2,128)} %param.19) | copy-start | bytes 6148
  11.1 12.1 %copy-start.13 = (s32[256,1]{0,1:T(1,128)S(1)}, s32[256,1]{0,1:T(1,128)}, u32[]{:S(2)}) copy-start(s32[256,1]{0,1:T(1,128)} %param.18) | copy-start | bytes 3076
  11.2 11.3 %collective-permute-start.5 = (bf16[66,16,128]{2,1,0:T(8,128)(2,1)S(1)}, bf16[66,16,128]{2,1,0:T(8,128)(2,1)}, u32[]{:S(2)}, u32[]{:S(2)}) collective-permute-start(bf16[66,16,128]{2,1,0:T(8,128)(2,1)S(1)} %constant_dynamic-update-slice_fusion.pair.pair_in), channel_id=1, source_target_pairs={{0,32},{4,228},{8,40},{12,236},{16,48},{20,244},{24,56},{28,252},{... | collective-permute-start | bytes 811016 | tf_op jit(solution)/shard_map/ppermute | solution.py:490
  22.5 18.1 %copy-start.10 = (f32[3,2048]{1,0:T(4,128)S(1)}, f32[3,2048]{1,0:T(4,128)}, u32[]{:S(2)}) copy-start(f32[3,2048]{1,0:T(4,128)} %p0.1) | copy-start | bytes 73732
  22.5 10.5 %collective-permute-start.6 = (bf16[66,16,128]{2,1,0:T(8,128)(2,1)}, bf16[66,16,128]{2,1,0:T(8,128)(2,1)}, u32[]{:S(2)}, u32[]{:S(2)}) collective-permute-start(bf16[66,16,128]{2,1,0:T(8,128)(2,1)} %collective-permute-done.5.r1), channel_id=1, source_target_pairs={{0,32},{4,228},{8,40},{12,236},{16,48},{20,244},{24,56},{28,252},{... | collective-permute-start | bytes 811016 | tf_op jit(solution)/shard_map/ppermute | solution.py:490
  23.7 1.3 %collective-permute-start = (s32[8,128]{1,0:T(8,128)S(1)}, s32[8,128]{1,0:T(8,128)S(1)}, u32[]{:S(2)}, u32[]{:S(2)}) collective-permute-start(s32[8,128]{1,0:T(8,128)S(1)} %get-tuple-element.45), channel_id=1, source_target_pairs={{0,4},{4,0},{8,12},{12,8},{16,20},{20,16},{24,28},{28,24},{32,36},... | collective-permute-start | bytes 12296 | tf_op jit(solution)/shard_map/ppermute | solution.py:490
  24.9 8.0 %collective-permute-start.3 = (s32[2,8,128]{2,1,0:T(8,128)S(1)}, s32[2,8,128]{2,1,0:T(8,128)S(1)}, u32[]{:S(2)}, u32[]{:S(2)}) collective-permute-start(s32[2,8,128]{2,1,0:T(8,128)S(1)} %pad_add_fusion.t0), channel_id=1, source_target_pairs={{0,24},{4,28},{8,16},{12,20},{16,8},{20,12},{24,0},{28,4},{32,56},... | collective-permute-start | bytes 24584 | tf_op jit(solution)/shard_map/ppermute | solution.py:490
  27.4 5.6 %collective-permute-start.2 = (s32[2,8,128]{2,1,0:T(8,128)S(1)}, s32[2,8,128]{2,1,0:T(8,128)S(1)}, u32[]{:S(2)}, u32[]{:S(2)}) collective-permute-start(s32[2,8,128]{2,1,0:T(8,128)S(1)} %pad_add_fusion.t0), channel_id=1, source_target_pairs={{0,16},{4,20},{8,24},{12,28},{16,0},{20,4},{24,8},{28,12},{32,48},... | collective-permute-start | bytes 24584 | tf_op jit(solution)/shard_map/ppermute | solution.py:490
  27.9 5.0 %collective-permute-start.1 = (s32[2,8,128]{2,1,0:T(8,128)S(1)}, s32[2,8,128]{2,1,0:T(8,128)S(1)}, u32[]{:S(2)}, u32[]{:S(2)}) collective-permute-start(s32[2,8,128]{2,1,0:T(8,128)S(1)} %pad_add_fusion.t0), channel_id=1, source_target_pairs={{0,8},{4,12},{8,0},{12,4},{16,24},{20,28},{24,16},{28,20},{32,40},... | collective-permute-start | bytes 24584 | tf_op jit(solution)/shard_map/ppermute | solution.py:490
  33.0 5.9 %collective-permute-start.12 = (bf16[66,16,128]{2,1,0:T(8,128)(2,1)}, bf16[66,16,128]{2,1,0:T(8,128)(2,1)S(1)}, u32[]{:S(2)}, u32[]{:S(2)}) collective-permute-start(bf16[66,16,128]{2,1,0:T(8,128)(2,1)} %collective-permute-done.6.r2), channel_id=1, source_target_pairs={{0,32},{4,228},{8,40},{12,236},{16,48},{20,244},{24,56},{28,252},{... | collective-permute-start | bytes 811016 | tf_op jit(solution)/shard_map/ppermute | solution.py:490
  38.9 21.3 %collective-permute-start.13 = (bf16[33,16,128]{2,1,0:T(8,128)(2,1)S(1)}, bf16[33,16,128]{2,1,0:T(8,128)(2,1)S(1)}, u32[]{:S(2)}, u32[]{:S(2)}) collective-permute-start(bf16[33,16,128]{2,1,0:T(8,128)(2,1)S(1)} %slice.4), channel_id=1, source_target_pairs={{0,32},{4,228},{8,40},{12,236},{16,48},{20,244},{24,56},{28,252},{... | collective-permute-start | bytes 405512 | tf_op jit(solution)/shard_map/ppermute | solution.py:490
  40.6 5.0 %collective-permute-start.9 = (f32[3,2048]{1,0:T(4,128)S(1)}, f32[3,2048]{1,0:T(4,128)S(1)}, u32[]{:S(2)}, u32[]{:S(2)}) collective-permute-start(f32[3,2048]{1,0:T(4,128)S(1)} %copy-done.10), channel_id=1, source_target_pairs={{3,0},{0,1},{1,2},{2,3},{7,4},{4,5},{5,6},{6,7},{11,8},{8,9},{9,10... | collective-permute-start | bytes 73736 | tf_op jit(solution)/shard_map/ppermute | solution.py:537
  41.9 4.3 %collective-permute-start.8 = (f32[3,2048]{1,0:T(4,128)S(1)}, f32[3,2048]{1,0:T(4,128)S(1)}, u32[]{:S(2)}, u32[]{:S(2)}) collective-permute-start(f32[3,2048]{1,0:T(4,128)S(1)} %copy-done.10), channel_id=1, source_target_pairs={{2,0},{3,1},{0,2},{1,3},{6,4},{7,5},{4,6},{5,7},{10,8},{11,9},{8,1... | collective-permute-start | bytes 73736 | tf_op jit(solution)/shard_map/ppermute | solution.py:537
  44.5 3.2 %collective-permute-start.7 = (f32[3,2048]{1,0:T(4,128)S(1)}, f32[3,2048]{1,0:T(4,128)S(1)}, u32[]{:S(2)}, u32[]{:S(2)}) collective-permute-start(f32[3,2048]{1,0:T(4,128)S(1)} %copy-done.10), channel_id=1, source_target_pairs={{1,0},{2,1},{3,2},{0,3},{5,4},{6,5},{7,6},{4,7},{9,8},{10,9},{11,1... | collective-permute-start | bytes 73736 | tf_op jit(solution)/shard_map/ppermute | solution.py:537
  47.7 1.0 %copy-start.6 = (bf16[16,8192]{1,0:T(8,128)(2,1)S(1)}, bf16[16,8192]{1,0:T(8,128)(2,1)}, u32[]{:S(2)}) copy-start(bf16[16,8192]{1,0:T(8,128)(2,1)} %vec_ref.4) | copy-start | bytes 786436
  48.7 11.4 %collective-permute-start.10 = (bf16[16,16,128]{2,1,0:T(8,128)(2,1)S(1)}, bf16[16,16,128]{2,1,0:T(8,128)(2,1)S(1)}, u32[]{:S(2)}, u32[]{:S(2)}) collective-permute-start(bf16[16,16,128]{2,1,0:T(8,128)(2,1)S(1)} %get-tuple-element.53), channel_id=1, source_target_pairs={{0,4},{4,0},{8,12},{12,8},{16,20},{20,16},{24,28},{28,24},{32,36},... | collective-permute-start | bytes 196616 | tf_op jit(solution)/shard_map/ppermute | solution.py:490
  51.6 8.5 %collective-permute-start.11 = (bf16[16,16,128]{2,1,0:T(8,128)(2,1)S(1)}, bf16[16,16,128]{2,1,0:T(8,128)(2,1)S(1)}, u32[]{:S(2)}, u32[]{:S(2)}) collective-permute-start(bf16[16,16,128]{2,1,0:T(8,128)(2,1)S(1)} %get-tuple-element.54), channel_id=1, source_target_pairs={{4,8},{8,4},{12,16},{16,12},{20,24},{24,20},{28,32},{32,28},{36,40... | collective-permute-start | bytes 196616 | tf_op jit(solution)/shard_map/ppermute | solution.py:545
  54.6 1.6 %copy-start.1 = (bf16[128,64,64]{2,1,0:T(8,128)(2,1)S(1)}, bf16[128,64,64]{2,1,0:T(8,128)(2,1)}, u32[]{:S(2)}) copy-start(bf16[128,64,64]{2,1,0:T(8,128)(2,1)} %copy.14.pair_ref) | copy-start | bytes 3145732
  56.2 1.0 %copy-start.9 = (f32[64,16,128]{2,1,0:T(8,128)S(1)}, f32[64,16,128]{2,1,0:T(8,128)}, u32[]{:S(2)}) copy-start(f32[64,16,128]{2,1,0:T(8,128)} %copy-done.8) | copy-start | bytes 1572868
  57.3 14.4 %copy-start.7 = (bf16[16,8192]{1,0:T(8,128)(2,1)S(1)}, bf16[16,8192]{1,0:T(8,128)(2,1)}, u32[]{:S(2)}) copy-start(bf16[16,8192]{1,0:T(8,128)(2,1)} %vec_ref.4) | copy-start | bytes 786436
  57.3 14.4 %copy-start.11 = (s32[64,8]{0,1:T(8,128)S(1)}, s32[64,8]{0,1:T(8,128)}, u32[]{:S(2)}) copy-start(s32[64,8]{0,1:T(8,128)} %param.21) | copy-start | bytes 6148
  62.2 5.2 %collective-permute-start.14 = (bf16[35,16,128]{2,1,0:T(8,128)(2,1)S(1)}, bf16[35,16,128]{2,1,0:T(8,128)(2,1)S(1)}, u32[]{:S(2)}, u32[]{:S(2)}) collective-permute-start(bf16[35,16,128]{2,1,0:T(8,128)(2,1)S(1)} %get-tuple-element.61), channel_id=1, source_target_pairs={{0,4},{4,0},{8,12},{12,8},{16,20},{20,16},{24,28},{28,24},{32,36},... | collective-permute-start | bytes 430088 | tf_op jit(solution)/shard_map/ppermute | solution.py:490
  62.3 7.5 %collective-permute-start.15 = (bf16[35,16,128]{2,1,0:T(8,128)(2,1)S(1)}, bf16[35,16,128]{2,1,0:T(8,128)(2,1)S(1)}, u32[]{:S(2)}, u32[]{:S(2)}) collective-permute-start(bf16[35,16,128]{2,1,0:T(8,128)(2,1)S(1)} %get-tuple-element.62), channel_id=1, source_target_pairs={{0,8},{4,12},{8,0},{12,4},{16,24},{20,28},{24,16},{28,20},{32,40},... | collective-permute-start | bytes 430088 | tf_op jit(solution)/shard_map/ppermute | solution.py:490
  63.6 16.8 %collective-permute-start.16 = (bf16[35,16,128]{2,1,0:T(8,128)(2,1)S(1)}, bf16[35,16,128]{2,1,0:T(8,128)(2,1)S(1)}, u32[]{:S(2)}, u32[]{:S(2)}) collective-permute-start(bf16[35,16,128]{2,1,0:T(8,128)(2,1)S(1)} %get-tuple-element.63), channel_id=1, source_target_pairs={{0,12},{4,8},{8,4},{12,0},{16,28},{20,24},{24,20},{28,16},{32,44},... | collective-permute-start | bytes 430088 | tf_op jit(solution)/shard_map/ppermute | solution.py:490
  64.4 15.9 %collective-permute-start.17 = (bf16[35,16,128]{2,1,0:T(8,128)(2,1)S(1)}, bf16[35,16,128]{2,1,0:T(8,128)(2,1)S(1)}, u32[]{:S(2)}, u32[]{:S(2)}) collective-permute-start(bf16[35,16,128]{2,1,0:T(8,128)(2,1)S(1)} %get-tuple-element.64), channel_id=1, source_target_pairs={{0,16},{4,20},{8,24},{12,28},{16,0},{20,4},{24,8},{28,12},{32,48},... | collective-permute-start | bytes 430088 | tf_op jit(solution)/shard_map/ppermute | solution.py:490
  66.9 13.5 %collective-permute-start.18 = (bf16[35,16,128]{2,1,0:T(8,128)(2,1)S(1)}, bf16[35,16,128]{2,1,0:T(8,128)(2,1)S(1)}, u32[]{:S(2)}, u32[]{:S(2)}) collective-permute-start(bf16[35,16,128]{2,1,0:T(8,128)(2,1)S(1)} %get-tuple-element.65), channel_id=1, source_target_pairs={{0,20},{4,16},{8,28},{12,24},{16,4},{20,0},{24,12},{28,8},{32,52},... | collective-permute-start | bytes 430088 | tf_op jit(solution)/shard_map/ppermute | solution.py:490
  67.5 12.9 %collective-permute-start.19 = (bf16[35,16,128]{2,1,0:T(8,128)(2,1)S(1)}, bf16[35,16,128]{2,1,0:T(8,128)(2,1)S(1)}, u32[]{:S(2)}, u32[]{:S(2)}) collective-permute-start(bf16[35,16,128]{2,1,0:T(8,128)(2,1)S(1)} %get-tuple-element.66), channel_id=1, source_target_pairs={{0,24},{4,28},{8,16},{12,20},{16,8},{20,12},{24,0},{28,4},{32,56},... | collective-permute-start | bytes 430088 | tf_op jit(solution)/shard_map/ppermute | solution.py:490
  69.8 13.6 %copy-start.3 = (bf16[64,64,64]{2,1,0:T(8,128)(2,1)S(1)}, bf16[64,64,64]{2,1,0:T(8,128)(2,1)}, u32[]{:S(2)}) copy-start(bf16[64,64,64]{2,1,0:T(8,128)(2,1)} %upper_t_ref.1) | copy-start | bytes 1572868
  69.8 13.6 %copy-start.4 = (bf16[64,64,64]{2,1,0:T(8,128)(2,1)S(1)}, bf16[64,64,64]{2,1,0:T(8,128)(2,1)}, u32[]{:S(2)}) copy-start(bf16[64,64,64]{2,1,0:T(8,128)(2,1)} %upper_c_ref.1) | copy-start | bytes 1572868
  69.8 13.6 %collective-permute-start.20 = (bf16[35,16,128]{2,1,0:T(8,128)(2,1)S(1)}, bf16[35,16,128]{2,1,0:T(8,128)(2,1)S(1)}, u32[]{:S(2)}, u32[]{:S(2)}) collective-permute-start(bf16[35,16,128]{2,1,0:T(8,128)(2,1)S(1)} %get-tuple-element.67), channel_id=1, source_target_pairs={{0,28},{4,24},{8,20},{12,16},{16,12},{20,8},{24,4},{28,0},{32,60},... | collective-permute-start | bytes 430088 | tf_op jit(solution)/shard_map/ppermute | solution.py:490
  83.4 3.2 %copy-start = (bf16[256,64,64]{2,1,0:T(8,128)(2,1)S(1)}, bf16[256,64,64]{2,1,0:T(8,128)(2,1)}, u32[]{:S(2)}) copy-start(bf16[256,64,64]{2,1,0:T(8,128)(2,1)} %copy.13.block_ref) | copy-start | bytes 6291460
